TPU v7x, 32 devices: a whole 2x2x4 slice. The times are simulated.
32 devices in a mesh: slide: 4 (over y, core), blk: 8 (over z, x).
Axes of the slice: x: 2, y: 2, z: 4, core: 2. Of those that a mesh axis runs over, the one named last changes fastest.
Arguments:
- counts: int32 [4, 1024, 1024], P('slide', 'blk'), may hold values from 0 to 39, as said below
- library: int32 [4, 1024], P('slide', 'blk'), may hold values from 2000 to 19999
- gene_ids: int32 [1024], replicated, may hold values from 0 to 16383, as said below
- positions: int32 [4, 2, 1024], P('slide', None, 'blk'), may hold values from 0 to 2047
- slide_of_cell: int32 [4, 1024], P('slide', 'blk'), may hold values from 0 to 3, as said below
- latent_noise: float32 [4, 1024, 512], P('slide', 'blk'), may hold values from -6 to 6
- decoded_grad: bfloat16 [4, 1024, 1024], P('slide', 'blk'), may hold values from -6 to 6
- gene_table: bfloat16 [16384, 1024], P('blk'), may hold values from -0.0625 to 0.0625
- first_gain: float32 [1024], replicated, may hold values from 0.5 to 1.5
- first_shift: float32 [1024], replicated, may hold values from -1.5 to 1.5
- query_weight: bfloat16 [1024, 1024], replicated, may hold values from -0.25 to 0.25
- key_weight: bfloat16 [1024, 1024], replicated, may hold values from -0.25 to 0.25
- value_weight: bfloat16 [1024, 1024], replicated, may hold values from -0.1875 to 0.1875
- output_weight: bfloat16 [1024, 1024], replicated, may hold values from -0.375 to 0.375
- second_gain: float32 [1024], replicated, may hold values from 0.5 to 1.5
- second_shift: float32 [1024], replicated, may hold values from -1.5 to 1.5
- hidden_weight: bfloat16 [1024, 4096], replicated, may hold values from -0.1875 to 0.1875
- hidden_bias: float32 [4096], replicated, may hold values from -3 to 3
- down_weight: bfloat16 [4096, 1024], replicated, may hold values from -0.09375 to 0.09375
- down_bias: float32 [1024], replicated, may hold values from -3 to 3
- mean_weight: bfloat16 [1024, 512], replicated, may hold values from -0.09375 to 0.09375
- logvar_weight: bfloat16 [1024, 512], replicated, may hold values from -0.046875 to 0.046875
- component_means: float32 [16, 512], replicated, may hold values from -5 to 5
- decoder_weight: bfloat16 [512, 1024], replicated, may hold values from -0.25 to 0.25
- divergence_weight: float32 [1], replicated, may hold values from 0.005 to 0.02
- free_floor: float32 [512], replicated, may hold values from 0.1 to 4
Outputs:
- decoded: float32 [4, 1024, 1024], P('slide', 'blk')
- divergence: float32 [1], replicated
- gene_table_grad: float32 [16384, 1024], P('blk')
- first_gain_grad: float32 [1024], P('blk')
- first_shift_grad: float32 [1024], P('blk')
- query_weight_grad: float32 [1024, 1024], P('blk')
- key_weight_grad: float32 [1024, 1024], P('blk')
- value_weight_grad: float32 [1024, 1024], P('blk')
- output_weight_grad: float32 [1024, 1024], P('blk')
- second_gain_grad: float32 [1024], P('blk')
- second_shift_grad: float32 [1024], P('blk')
- hidden_weight_grad: float32 [1024, 4096], P('blk')
- hidden_bias_grad: float32 [4096], P('blk')
- down_weight_grad: float32 [4096, 1024], P('blk')
- down_bias_grad: float32 [1024], P('blk')
- mean_weight_grad: float32 [1024, 512], P('blk')
- logvar_weight_grad: float32 [1024, 512], P('blk')
- component_means_grad: float32 [16, 512], P(None, 'blk')
- decoder_weight_grad: float32 [512, 1024], P('blk')
Inputs may be any that keep to these rules, and one draw needn't show every extreme that they name: `counts`: most entries are zero, about four in five. `gene_ids`: distinct rows of the gene table. `slide_of_cell`: each of the 4 slides of a group holds about 1024/4 cells, at any positions of the group.
All inputs are finite; a program needn't handle non-finite values.
Results may differ from a plain program's by a relative error of at most 0.019.
Values may be sent and summed in bfloat16 or wider, within the bound.
A program may use at most 256 MiB of HBM per device.

v0:
```python
import math

import jax
import jax.numpy as jnp
from jax import lax
from jax.sharding import PartitionSpec as P

HEAD_DIM = 64


def normalized(counts, library):
    scaled = counts.astype(jnp.float32) * (10000.0 / library.astype(jnp.float32))[..., None]
    return jnp.log1p(scaled)


def position_code(coords, model_width):
    quarter = model_width // 4
    freqs = jnp.exp(-math.log(10000.0) * jnp.arange(quarter, dtype=jnp.float32) / quarter)
    along_x = coords[0].astype(jnp.float32)[:, None] * freqs[None, :]
    along_y = coords[1].astype(jnp.float32)[:, None] * freqs[None, :]
    return jnp.concatenate(
        [jnp.sin(along_x), jnp.cos(along_x), jnp.sin(along_y), jnp.cos(along_y)], axis=1
    )


def layer_norm(inputs, scaling, offsets):
    centre = inputs - jnp.mean(inputs, axis=-1, keepdims=True)
    spread = jnp.mean(centre * centre, axis=-1, keepdims=True)
    return centre * lax.rsqrt(spread + 1e-05) * scaling + offsets


def gelu_tanh(inputs):
    return (
        0.5
        * inputs
        * (1.0 + jnp.tanh(0.7978845608028654 * (inputs + 0.044715 * inputs * inputs * inputs)))
    )


def divergence_cells(mean_part, logvar_part, centres):
    latent_width = mean_part.shape[-1]
    crossed = jnp.dot(mean_part, centres.T, precision=lax.Precision.HIGHEST)
    centre_square = jnp.sum(centres * centres, axis=-1)
    logits = (crossed - 0.5 * centre_square[None, :]) / math.sqrt(latent_width)
    shifted = jnp.exp(logits - jnp.max(logits, axis=-1, keepdims=True))
    resp = shifted / jnp.sum(shifted, axis=-1, keepdims=True)
    mixed = jnp.dot(resp, centres, precision=lax.Precision.HIGHEST)
    mixed_square = jnp.dot(resp, centres * centres, precision=lax.Precision.HIGHEST)
    return 0.5 * (
        jnp.exp(logvar_part)
        - 1.0
        - logvar_part
        + mean_part * mean_part
        - 2.0 * mean_part * mixed
        + mixed_square
    )


def to_heads(array, head_count):
    return array.reshape(array.shape[0], head_count, -1).transpose(1, 0, 2)


def from_heads(array):
    return array.transpose(1, 0, 2).reshape(array.shape[1], -1)


def matmul(left, right):
    return jnp.dot(left, right, preferred_element_type=jnp.float32)


def on_device(
    counts,
    library,
    gene_ids,
    positions,
    slide_of_cell,
    latent_noise,
    decoded_grad,
    gene_table,
    first_gain,
    first_shift,
    query_weight,
    key_weight,
    value_weight,
    output_weight,
    second_gain,
    second_shift,
    hidden_weight,
    hidden_bias,
    down_weight,
    down_bias,
    mean_weight,
    logvar_weight,
    component_means,
    decoder_weight,
    divergence_weight,
    free_floor,
):
    cell_count = counts.shape[1]
    model_width = gene_table.shape[1]
    head_count = model_width // HEAD_DIM
    score_scale = HEAD_DIM ** (-0.5)
    express = normalized(counts[0], library[0]).astype(jnp.bfloat16)
    table_rows = gene_table.shape[0]
    first_row = lax.axis_index("blk") * table_rows
    selector = (
        gene_ids[:, None] == first_row + jnp.arange(table_rows, dtype=jnp.int32)[None, :]
    ).astype(jnp.bfloat16)
    panel_part = matmul(selector, gene_table)
    panel_weight = lax.psum(panel_part, "blk").astype(jnp.bfloat16)
    hidden_start = matmul(express, panel_weight) + position_code(positions[0], model_width)
    normed_one = layer_norm(hidden_start, first_gain, first_shift).astype(jnp.bfloat16)
    query_low = matmul(normed_one, query_weight).astype(jnp.bfloat16)
    key_low = matmul(normed_one, key_weight).astype(jnp.bfloat16)
    value_low = matmul(normed_one, value_weight).astype(jnp.bfloat16)
    slide_labels = slide_of_cell[0].astype(jnp.bfloat16)
    keys_all, values_all, labels_all = (
        lax.all_gather(key_low, "blk", axis=0, tiled=True),
        lax.all_gather(value_low, "blk", axis=0, tiled=True),
        lax.all_gather(slide_labels, "blk", axis=0, tiled=True),
    )
    same_slide = slide_labels[:, None] == labels_all[None, :]
    query_heads = to_heads(query_low, head_count)
    key_heads = to_heads(keys_all, head_count)
    value_heads = to_heads(values_all, head_count)

    def head_forward(head_items):
        query_head, key_head, value_head = head_items
        scores = (
            jnp.einsum("qd,kd->qk", query_head, key_head, preferred_element_type=jnp.float32)
            * score_scale
        )
        scores = jnp.where(same_slide, scores, -1e30)
        row_max = jnp.max(scores, axis=1, keepdims=True)
        shifted = jnp.exp(scores - row_max)
        row_sum = jnp.sum(shifted, axis=1, keepdims=True)
        shares = shifted / row_sum
        attended_head = jnp.einsum(
            "qk,kd->qd", shares.astype(jnp.bfloat16), value_head, preferred_element_type=jnp.float32
        )
        return (attended_head, row_max[:, 0], row_sum[:, 0])

    attended_heads, row_maxes, row_sums = lax.map(
        head_forward, (query_heads, key_heads, value_heads)
    )
    attended = from_heads(attended_heads).astype(jnp.bfloat16)
    hidden_middle = hidden_start + matmul(attended, output_weight)
    normed_two = layer_norm(hidden_middle, second_gain, second_shift).astype(jnp.bfloat16)
    inner_sum = matmul(normed_two, hidden_weight) + hidden_bias
    act_low = gelu_tanh(inner_sum).astype(jnp.bfloat16)
    hidden_final = hidden_middle + matmul(act_low, down_weight) + down_bias
    base_low = hidden_final.astype(jnp.bfloat16)
    mean_lat = matmul(base_low, mean_weight)
    log_var = matmul(base_low, logvar_weight)
    noise_local = latent_noise[0]

    def bottleneck(mean_part, logvar_part, centres):
        return (
            mean_part + jnp.exp(0.5 * logvar_part) * noise_local,
            divergence_cells(mean_part, logvar_part, centres),
        )

    (latent, kl_cell), pull_latent = jax.vjp(bottleneck, mean_lat, log_var, component_means)
    latent_low = latent.astype(jnp.bfloat16)
    decoded = matmul(latent_low, decoder_weight)
    everyone = cell_count * lax.axis_size("blk") * lax.axis_size("slide")
    kl_sum = lax.psum(jnp.sum(kl_cell, axis=0), ("slide", "blk"))
    kl_mean = kl_sum / everyone
    divergence = divergence_weight * jnp.mean(jnp.maximum(kl_mean, free_floor))
    binding = (kl_mean > free_floor).astype(jnp.float32)
    grad_source = decoded_grad[0]
    grad_latent = matmul(grad_source, decoder_weight.T)
    decoder_grad = matmul(latent_low.T, grad_source)
    grad_kl = jnp.broadcast_to(divergence_weight * binding, kl_cell.shape)
    grad_mean, grad_logvar, centres_grad = pull_latent((grad_latent, grad_kl))
    grad_mean_low = grad_mean.astype(jnp.bfloat16)
    grad_logvar_low = grad_logvar.astype(jnp.bfloat16)
    mean_grad = matmul(base_low.T, grad_mean_low)
    logvar_grad = matmul(base_low.T, grad_logvar_low)
    grad_final = matmul(grad_mean_low, mean_weight.T) + matmul(grad_logvar_low, logvar_weight.T)
    grad_branch = grad_final.astype(jnp.bfloat16)
    down_grad = matmul(act_low.T, grad_branch)
    down_bias_grad = jnp.sum(grad_branch.astype(jnp.float32), axis=0)
    grad_act = matmul(grad_branch, down_weight.T)
    gelu_pull = jax.vjp(gelu_tanh, inner_sum)[1]
    grad_inner = gelu_pull(grad_act)[0].astype(jnp.bfloat16)
    hidden_grad = matmul(normed_two.T, grad_inner)
    hidden_bias_grad = jnp.sum(grad_inner.astype(jnp.float32), axis=0)
    norm_two_pull = jax.vjp(layer_norm, hidden_middle, second_gain, second_shift)[1]
    grad_norm_two, second_gain_grad, second_shift_grad = norm_two_pull(
        matmul(grad_inner, hidden_weight.T)
    )
    grad_middle = grad_final + grad_norm_two
    grad_out = grad_middle.astype(jnp.bfloat16)
    output_grad = matmul(attended.T, grad_out)
    grad_attended = matmul(grad_out, output_weight.T).astype(jnp.bfloat16)
    keys_again, values_again = (
        lax.all_gather(key_low, "blk", axis=0, tiled=True),
        lax.all_gather(value_low, "blk", axis=0, tiled=True),
    )
    key_heads_back = to_heads(keys_again, head_count)
    value_heads_back = to_heads(values_again, head_count)
    grad_heads_local = to_heads(grad_attended, head_count)

    def head_queries(head_items):
        query_head, key_head, value_head, grad_head, row_max, row_sum = head_items
        scores = (
            jnp.einsum("qd,kd->qk", query_head, key_head, preferred_element_type=jnp.float32)
            * score_scale
        )
        scores = jnp.where(same_slide, scores, -1e30)
        shares = jnp.exp(scores - row_max[:, None]) / row_sum[:, None]
        grad_shares = jnp.einsum(
            "qd,kd->qk", grad_head, value_head, preferred_element_type=jnp.float32
        )
        inner_dot = jnp.sum(shares * grad_shares, axis=1, keepdims=True)
        grad_scores = (shares * (grad_shares - inner_dot)).astype(jnp.bfloat16)
        grad_query_head = (
            jnp.einsum("qk,kd->qd", grad_scores, key_head, preferred_element_type=jnp.float32)
            * score_scale
        )
        return (grad_query_head, inner_dot[:, 0])

    grad_query_heads, inner_dots = lax.map(
        head_queries,
        (query_heads, key_heads_back, value_heads_back, grad_heads_local, row_maxes, row_sums),
    )
    queries_group, grads_group = (
        lax.all_gather(query_low, "blk", axis=0, tiled=True),
        lax.all_gather(grad_attended, "blk", axis=0, tiled=True),
    )
    maxes_group, totals_group, dots_group = (
        lax.all_gather(row_maxes, "blk", axis=1, tiled=True),
        lax.all_gather(row_sums, "blk", axis=1, tiled=True),
        lax.all_gather(inner_dots, "blk", axis=1, tiled=True),
    )
    mask_back = labels_all[:, None] == slide_labels[None, :]

    def head_keys(head_items):
        query_head, key_head, value_head, grad_head, row_max, row_sum, inner_dot = head_items
        scores = (
            jnp.einsum("qd,kd->qk", query_head, key_head, preferred_element_type=jnp.float32)
            * score_scale
        )
        scores = jnp.where(mask_back, scores, -1e30)
        shares = jnp.exp(scores - row_max[:, None]) / row_sum[:, None]
        grad_shares = jnp.einsum(
            "qd,kd->qk", grad_head, value_head, preferred_element_type=jnp.float32
        )
        grad_scores = (shares * (grad_shares - inner_dot[:, None])).astype(jnp.bfloat16)
        grad_key_head = (
            jnp.einsum("qk,qd->kd", grad_scores, query_head, preferred_element_type=jnp.float32)
            * score_scale
        )
        grad_value_head = jnp.einsum(
            "qk,qd->kd", shares.astype(jnp.bfloat16), grad_head, preferred_element_type=jnp.float32
        )
        return (grad_key_head, grad_value_head)

    grad_key_heads, grad_value_heads = lax.map(
        head_keys,
        (
            to_heads(queries_group, head_count),
            to_heads(key_low, head_count),
            to_heads(value_low, head_count),
            to_heads(grads_group, head_count),
            maxes_group,
            totals_group,
            dots_group,
        ),
    )
    grad_query_low = from_heads(grad_query_heads).astype(jnp.bfloat16)
    grad_key = from_heads(grad_key_heads)
    grad_value = from_heads(grad_value_heads)
    grad_key_low = grad_key.astype(jnp.bfloat16)
    grad_value_low = grad_value.astype(jnp.bfloat16)
    query_grad = matmul(normed_one.T, grad_query_low)
    key_grad = matmul(normed_one.T, grad_key_low)
    value_grad = matmul(normed_one.T, grad_value_low)
    grad_norm_input = (
        matmul(grad_query_low, query_weight.T)
        + matmul(grad_key_low, key_weight.T)
        + matmul(grad_value_low, value_weight.T)
    )
    norm_one_pull = jax.vjp(layer_norm, hidden_start, first_gain, first_shift)[1]
    grad_norm_one, first_gain_grad, first_shift_grad = norm_one_pull(grad_norm_input)
    grad_start = grad_middle + grad_norm_one
    grad_encoded = grad_start.astype(jnp.bfloat16)
    panel_grad = matmul(express.T, grad_encoded)
    panel_total = lax.psum(panel_grad, ("slide", "blk"))
    table_grad = jnp.dot(
        selector.astype(jnp.float32).T, panel_total, precision=lax.Precision.HIGHEST
    )
    shares_grads = (
        lax.psum_scatter(first_gain_grad, "blk", scatter_dimension=0, tiled=True),
        lax.psum_scatter(first_shift_grad, "blk", scatter_dimension=0, tiled=True),
        lax.psum_scatter(query_grad, "blk", scatter_dimension=0, tiled=True),
        lax.psum_scatter(key_grad, "blk", scatter_dimension=0, tiled=True),
        lax.psum_scatter(value_grad, "blk", scatter_dimension=0, tiled=True),
        lax.psum_scatter(output_grad, "blk", scatter_dimension=0, tiled=True),
        lax.psum_scatter(second_gain_grad, "blk", scatter_dimension=0, tiled=True),
        lax.psum_scatter(second_shift_grad, "blk", scatter_dimension=0, tiled=True),
        lax.psum_scatter(hidden_grad, "blk", scatter_dimension=0, tiled=True),
        lax.psum_scatter(hidden_bias_grad, "blk", scatter_dimension=0, tiled=True),
        lax.psum_scatter(down_grad, "blk", scatter_dimension=0, tiled=True),
        lax.psum_scatter(down_bias_grad, "blk", scatter_dimension=0, tiled=True),
        lax.psum_scatter(mean_grad, "blk", scatter_dimension=0, tiled=True),
        lax.psum_scatter(logvar_grad, "blk", scatter_dimension=0, tiled=True),
        lax.psum_scatter(centres_grad, "blk", scatter_dimension=1, tiled=True),
        lax.psum_scatter(decoder_grad, "blk", scatter_dimension=0, tiled=True),
    )
    summed = (
        lax.psum(shares_grads[0].astype(jnp.bfloat16), "slide").astype(jnp.float32),
        lax.psum(shares_grads[1].astype(jnp.bfloat16), "slide").astype(jnp.float32),
        lax.psum(shares_grads[2].astype(jnp.bfloat16), "slide").astype(jnp.float32),
        lax.psum(shares_grads[3].astype(jnp.bfloat16), "slide").astype(jnp.float32),
        lax.psum(shares_grads[4].astype(jnp.bfloat16), "slide").astype(jnp.float32),
        lax.psum(shares_grads[5].astype(jnp.bfloat16), "slide").astype(jnp.float32),
        lax.psum(shares_grads[6].astype(jnp.bfloat16), "slide").astype(jnp.float32),
        lax.psum(shares_grads[7].astype(jnp.bfloat16), "slide").astype(jnp.float32),
        lax.psum(shares_grads[8].astype(jnp.bfloat16), "slide").astype(jnp.float32),
        lax.psum(shares_grads[9].astype(jnp.bfloat16), "slide").astype(jnp.float32),
        lax.psum(shares_grads[10].astype(jnp.bfloat16), "slide").astype(jnp.float32),
        lax.psum(shares_grads[11].astype(jnp.bfloat16), "slide").astype(jnp.float32),
        lax.psum(shares_grads[12].astype(jnp.bfloat16), "slide").astype(jnp.float32),
        lax.psum(shares_grads[13].astype(jnp.bfloat16), "slide").astype(jnp.float32),
        lax.psum(shares_grads[14].astype(jnp.bfloat16), "slide").astype(jnp.float32),
        lax.psum(shares_grads[15].astype(jnp.bfloat16), "slide").astype(jnp.float32),
    )
    return (decoded[None], divergence, table_grad) + tuple(summed)


def solution(mesh):
    placed = (
        P("slide", "blk", None),
        P("slide", "blk"),
        P(),
        P("slide", None, "blk"),
        P("slide", "blk"),
        P("slide", "blk", None),
        P("slide", "blk", None),
        P("blk", None),
        P(),
        P(),
        P(),
        P(),
        P(),
        P(),
        P(),
        P(),
        P(),
        P(),
        P(),
        P(),
        P(),
        P(),
        P(),
        P(),
        P(),
        P(),
    )
    return jax.shard_map(
        on_device,
        mesh=mesh,
        in_specs=placed,
        out_specs=(
            P("slide", "blk", None),
            P(),
            P("blk", None),
            P("blk"),
            P("blk"),
            P("blk", None),
            P("blk", None),
            P("blk", None),
            P("blk", None),
            P("blk"),
            P("blk"),
            P("blk", None),
            P("blk"),
            P("blk", None),
            P("blk"),
            P("blk", None),
            P("blk", None),
            P(None, "blk"),
            P("blk", None),
        ),
        check_vma=False,
    )
```

profile of v0, /device:TPU:1, one launch (start us, length us, event | category | flops | bytes accessed | tf_op | source)
XLA Modules:
  0.0 1927.4 jit_solution(5960952832974443741)
XLA Ops:
  17.8 168.1 %all-reduce.16 = bf16[1024,1024]{1,0:T(8,128)(2,1)} all-reduce(f32[1024,1024]{1,0:T(8,128)} %fusion.77), channel_id=1, replica_groups=mesh['slide'=4,'blk'=8] {'blk'}, use_global_device_ids=true, to_apply=%region_0.0 | all-reduce | flops 1048576 | bytes 6291456 | tf_op jit(solution)/shard_map/psum | solution.py:110
  197.1 13.6 all-gather
  211.0 27.4 %all-gather.6.cloned.1.call-done = bf16[1024,1024]{1,0:T(8,128)(2,1)} async-done(((bf16[128,1024]{1,0:T(8,128)(2,1)}), bf16[1024,1024]{1,0:T(8,128)(2,1)}) %all-gather.6.cloned.1.call-update) | async-done | bytes 2097168 | tf_op jit(solution)/shard_map/all_gather | solution.py:118
  247.0 41.8 %all-gather.8.cloned.1.call-done = bf16[1024,1024]{1,0:T(8,128)(2,1)} async-done(((bf16[128,1024]{1,0:T(8,128)(2,1)}), bf16[1024,1024]{1,0:T(8,128)(2,1)}) %all-gather.8.cloned.1.call-update) | async-done | bytes 2097168 | tf_op jit(solution)/shard_map/all_gather | solution.py:119
  297.6 46.0 %while.41 = (s32[]{:T(128)}, bf16[16,128,64]{1,2,0:T(8,128)(2,1)S(1)}, f32[16,128]{1,0:T(8,128)S(1)}, f32[16,128]{1,0:T(8,128)S(1)}, bf16[16,128,64]{2,1,0:T(8,1...) while((s32[]{:T(128)}, ...), condition=%wide.region_6.7_spmd.clone, body=%wide.region_3.6_spmd.clone.sunk | while | flops 34733824 | bytes 2172029 | solution.py:143
  356.0 39.8 %psum.134 = f32[512]{0:T(512)S(1)} all-reduce(f32[512]{0:T(512)S(1)} %fusion.99), channel_id=1, replica_groups=mesh['slide'=4,'blk'=8] {'slide','blk'}, use_global_device_ids=true, to_apply=%region_13.14 | all-reduce | flops 512 | bytes 4096 | tf_op jit(solution)/shard_map/psum | solution.py:167
  431.3 26.4 %all_gather.31 = f32[16,1024]{1,0:T(8,128)} all-gather(f32[16,128]{1,0:T(8,128)S(1)} %get-tuple-element.709), channel_id=1, replica_groups=mesh['slide'=4,'blk'=8] {'blk'}, dimensions={1}, use_global_device_ids=true | all-gather | bytes 73728 | tf_op jit(solution)/shard_map/all_gather | solution.py:234
  457.7 26.3 %all_gather.30 = f32[16,1024]{1,0:T(8,128)} all-gather(f32[16,128]{1,0:T(8,128)S(1)} %get-tuple-element.708), channel_id=1, replica_groups=mesh['slide'=4,'blk'=8] {'blk'}, dimensions={1}, use_global_device_ids=true | all-gather | bytes 73728 | tf_op jit(solution)/shard_map/all_gather | solution.py:233
  488.3 63.2 %while.42 = (s32[]{:T(128)}, bf16[16,128,64]{1,2,0:T(8,128)(2,1)S(1)}, f32[16,128]{1,0:T(8,128)S(1)}, bf16[16,128,64]{2,1,0:T(8,128)(2,1)}, bf16[16,1024,64]{2,1...) while((s32[]{:T(128)}, ...), condition=%wide.region_22.23_spmd.clone, body=%wide.region_20.22_spmd.clone.sunk | while | flops 51650432 | bytes 3500429 | solution.py:224
  553.2 24.5 %all_gather.33 = f32[16,1024]{1,0:T(8,128)S(1)} all-gather(f32[16,128]{1,0:T(8,128)} %copy-done.42), channel_id=1, replica_groups=mesh['slide'=4,'blk'=8] {'blk'}, dimensions={1}, use_global_device_ids=true | all-gather | bytes 73728 | tf_op jit(solution)/shard_map/all_gather | solution.py:235
  589.9 96.2 %while.43 = (s32[]{:T(128)}, bf16[16,128,64]{1,2,0:T(8,128)(2,1)}, bf16[16,128,64]{1,2,0:T(8,128)(2,1)}, bf16[16,1024,64]{1,2,0:T(8,128)(2,1)}, bf16[16,128,64]{...) while((s32[]{:T(128)}, bf16[16,128,64]{1,2,0:T(8,128)(2,1)}, ...), condition=%wide.region_24.25_spmd.clone, body=%wide.region_23.24_spmd.clone.sunk | while | flops 68296704 | bytes 2239117 | solution.py:260
  694.7 9.8 fusion.134
  732.4 36.9 %reduce-scatter.19.cloned.1.call-done = f32[128,1024]{1,0:T(8,128)} async-done(((f32[1024,1024]{1,0:T(8,128)}), f32[128,1024]{1,0:T(8,128)}) %reduce-scatter.19.cloned.1.call-update) | async-done | bytes 524304 | tf_op jit(solution)/shard_map/reduce_scatter | solution.py:300
  771.0 90.0 %reduce-scatter.13.cloned.1.call-done = f32[128,1024]{1,0:T(8,128)} async-done(((f32[1024,1024]{1,0:T(8,128)}), f32[128,1024]{1,0:T(8,128)}) %reduce-scatter.13.cloned.1.call-update) | async-done | bytes 524304 | tf_op jit(solution)/shard_map/reduce_scatter | solution.py:297
  862.8 89.4 %reduce-scatter.17.cloned.1.call-done = f32[128,1024]{1,0:T(8,128)} async-done(((f32[1024,1024]{1,0:T(8,128)}), f32[128,1024]{1,0:T(8,128)}) %reduce-scatter.17.cloned.1.call-update) | async-done | bytes 524304 | tf_op jit(solution)/shard_map/reduce_scatter | solution.py:299
  954.0 90.1 %reduce-scatter.15.cloned.1.call-done = f32[128,1024]{1,0:T(8,128)} async-done(((f32[1024,1024]{1,0:T(8,128)}), f32[128,1024]{1,0:T(8,128)}) %reduce-scatter.15.cloned.1.call-update) | async-done | bytes 524304 | tf_op jit(solution)/shard_map/reduce_scatter | solution.py:298
  1045.9 284.3 %reduce-scatter.23.cloned.1.call-done = f32[512,1024]{1,0:T(8,128)} async-done(((f32[4096,1024]{1,0:T(8,128)}), f32[512,1024]{1,0:T(8,128)}) %reduce-scatter.23.cloned.1.call-update) | async-done | bytes 2097168 | tf_op jit(solution)/shard_map/reduce_scatter | solution.py:305
  1332.9 283.3 %reduce-scatter.21.cloned.1.call-done = f32[128,4096]{1,0:T(8,128)} async-done(((f32[1024,4096]{1,0:T(8,128)}), f32[128,4096]{1,0:T(8,128)}) %reduce-scatter.21.cloned.1.call-update) | async-done | bytes 2097168 | tf_op jit(solution)/shard_map/reduce_scatter | solution.py:303
  1623.2 55.1 %reduce-scatter.31.cloned.1.call-done = f32[64,16]{1,0:T(8,128)} async-done(((f32[512,16]{1,0:T(8,128)}), f32[64,16]{1,0:T(8,128)}) %reduce-scatter.31.cloned.1.call-update) | async-done | bytes 4112
  1679.2 29.2 %all-reduce.6 = (bf16[1024]{0:T(1024)(128)(2,1)S(1)}, bf16[1024]{0:T(1024)(128)(2,1)S(1)}, bf16[1024]{0:T(1024)(128)(2,1)S(1)}, bf16[1024]{0:T(1024)(128)(2,1)S(...) all-reduce(f32[1024]{0:T(1024)S(1)} %get-tuple-element.323, ...), channel_id=3, replica_groups=mesh['slide'=4,'blk'=8] {'blk'}, use_global_device_ids=true, to_apply=%region_29.30.clone | all-reduce | flops 9216 | bytes 55296
  1708.9 14.8 all-reduce.7
  1727.4 98.4 %all-reduce.13.cloned.1.call-done = f32[1024,1024]{1,0:T(8,128)} async-done(((f32[1024,1024]{1,0:T(8,128)}), f32[1024,1024]{1,0:T(8,128)}) %all-reduce.13.cloned.1.call-update) | async-done | bytes 4194320 | tf_op jit(solution)/shard_map/psum | solution.py:290
  1825.8 17.8 fusion.75
  1843.6 63.5 %all-reduce.15.cloned.1.call-done = (bf16[128,1024]{1,0:T(8,128)(2,1)}, bf16[128,1024]{1,0:T(8,128)(2,1)}, bf16[128,1024]{1,0:T(8,128)(2,1)}, bf16[128,1024]{1,0...) async-done(((bf16[128,1024]{1,0:T(8,128)(2,1)}, ...) | async-done | bytes 3538960 | tf_op jit(solution)/shard_map/psum | solution.py:315
  (557 shorter events, 376.9 us)
Async XLA Ops:
  7.2 183.9 %copy-start = (bf16[1024,1024]{1,0:T(8,128)(2,1)S(1)}, bf16[1024,1024]{1,0:T(8,128)(2,1)}, u32[]{:S(2)}) copy-start(bf16[1024,1024]{1,0:T(8,128)(2,1)} %param.44) | copy-start | bytes 6291460
  7.2 231.1 %all-gather.6.cloned.1.call-start = ((), (), s32[]{:S(2)}) async-start(), calls=%async_computation.10 | async-start | bytes 2359296 | tf_op jit(solution)/shard_map/all_gather | solution.py:118
  8.1 178.8 %copy-start.63 = (f32[128]{0:T(128)}, f32[128]{0:T(128)S(1)}, u32[]{:S(2)}) copy-start(f32[128]{0:T(128)S(1)} %divide_bitcast_fusion) | copy-start | bytes 1540
  17.8 169.1 %copy-start.28 = (s32[1,128,1024]{2,1,0:T(8,128)S(1)}, s32[1,128,1024]{2,1,0:T(8,128)}, u32[]{:S(2)}) copy-start(s32[1,128,1024]{2,1,0:T(8,128)} %param.32) | copy-start | bytes 1572868
  189.3 155.1 %copy-start.1 = (f32[128,1024]{1,0:T(8,128)}, f32[128,1024]{1,0:T(8,128)S(1)}, u32[]{:S(2)}) copy-start(f32[128,1024]{1,0:T(8,128)S(1)} %get-tuple-element.448) | copy-start | bytes 1572868
  191.0 97.9 %all-gather.8.cloned.1.call-start = ((), (), s32[]{:S(2)}) async-start(), calls=%async_computation.11 | async-start | bytes 2359296 | tf_op jit(solution)/shard_map/all_gather | solution.py:119
  192.2 388.2 %all-gather.10.cloned.1.call-start = ((), (), s32[]{:S(2)}) async-start(), calls=%async_computation.12 | async-start | bytes 2359296 | tf_op jit(solution)/shard_map/all_gather | solution.py:229
  195.1 389.4 %all-gather.12.cloned.1.call-start = ((), (), s32[]{:S(2)}) async-start(), calls=%async_computation.13 | async-start | bytes 2359296 | tf_op jit(solution)/shard_map/all_gather | solution.py:230
  415.0 69.0 %copy-start.8 = (f32[128,1024]{1,0:T(8,128)}, f32[128,1024]{1,0:T(8,128)S(1)}, u32[]{:S(2)}) copy-start(f32[128,1024]{1,0:T(8,128)S(1)} %get-tuple-element.432) | copy-start | bytes 1572868
  417.2 310.3 %reduce-scatter.29.cloned.1.call-start = ((), (), s32[]{:S(2)}) async-start(), calls=%async_computation.23 | async-start | bytes 2359296 | tf_op jit(solution)/shard_map/reduce_scatter | solution.py:310
  420.1 309.0 %reduce-scatter.27.cloned.1.call-start = ((), (), s32[]{:S(2)}) async-start(), calls=%async_computation.22 | async-start | bytes 2359296 | tf_op jit(solution)/shard_map/reduce_scatter | solution.py:308
  422.9 307.9 %reduce-scatter.25.cloned.1.call-start = ((), (), s32[]{:S(2)}) async-start(), calls=%async_computation.21 | async-start | bytes 2359296 | tf_op jit(solution)/shard_map/reduce_scatter | solution.py:307
  425.8 343.4 %reduce-scatter.19.cloned.1.call-start = ((), (), s32[]{:S(2)}) async-start(), calls=%async_computation.18 | async-start | bytes 4718592 | tf_op jit(solution)/shard_map/reduce_scatter | solution.py:300
  487.7 373.3 %reduce-scatter.13.cloned.1.call-start = ((), (), s32[]{:S(2)}) async-start(), calls=%async_computation.15 | async-start | bytes 4718592 | tf_op jit(solution)/shard_map/reduce_scatter | solution.py:297
  488.2 89.4 %copy-start.4 = (bf16[128,1024]{1,0:T(8,128)(2,1)S(1)}, bf16[128,1024]{1,0:T(8,128)(2,1)}, u32[]{:S(2)}) copy-start(bf16[128,1024]{1,0:T(8,128)(2,1)} %copy-done.3) | copy-start | bytes 786436
  580.4 371.8 %reduce-scatter.17.cloned.1.call-start = ((), (), s32[]{:S(2)}) async-start(), calls=%async_computation.17 | async-start | bytes 4718592 | tf_op jit(solution)/shard_map/reduce_scatter | solution.py:299
  689.9 354.2 %reduce-scatter.15.cloned.1.call-start = ((), (), s32[]{:S(2)}) async-start(), calls=%async_computation.16 | async-start | bytes 4718592 | tf_op jit(solution)/shard_map/reduce_scatter | solution.py:298
  693.7 636.5 %reduce-scatter.23.cloned.1.call-start = ((), (), s32[]{:S(2)}) async-start(), calls=%async_computation.20 | async-start | bytes 18874368 | tf_op jit(solution)/shard_map/reduce_scatter | solution.py:305
  704.6 911.7 %reduce-scatter.21.cloned.1.call-start = ((), (), s32[]{:S(2)}) async-start(), calls=%async_computation.19 | async-start | bytes 18874368 | tf_op jit(solution)/shard_map/reduce_scatter | solution.py:303
  714.7 963.6 %reduce-scatter.31.cloned.1.call-start = ((), (), s32[]{:S(2)}) async-start(), calls=%async_computation.24 | async-start | bytes 294912
  720.2 1105.6 %all-reduce.13.cloned.1.call-start = ((), (), s32[]{:S(2)}) async-start(), calls=%async_computation.14 | async-start | bytes 8388608 | tf_op jit(solution)/shard_map/psum | solution.py:290
  727.4 1179.6 %all-reduce.15.cloned.1.call-start = ((), (), s32[]{:S(2)}) async-start(), calls=%async_computation.25 | async-start | bytes 7077888 | tf_op jit(solution)/shard_map/psum | solution.py:315
  1619.0 206.9 %copy-start.55 = (s32[2048]{0:T(1024)S(1)}, s32[2048]{0:T(1024)}, u32[]{:S(2)}) copy-start(s32[2048]{0:T(1024)} %copy-done.54) | copy-start | bytes 24580
  1619.0 206.8 %copy-start.70 = (s32[1024]{0:T(1024)S(1)}, s32[1024]{0:T(1024)}, u32[]{:S(2)}) copy-start(s32[1024]{0:T(1024)} %param.34) | copy-start | bytes 12292
  (70 other events, 613.0 us)
Sparse Core Ops, SparseCore 0:
  191.1 47.1 all-gather.5
  241.0 47.7 all-gather.7
  291.6 47.9 all-gather.9
  417.3 49.9 all-gather.11
  470.7 65.5 reduce-scatter.28
  539.6 66.8 reduce-scatter.26
  610.1 66.6 reduce-scatter.24
  680.4 88.7 reduce-scatter.18
  773.3 87.6 reduce-scatter.12
  864.5 87.6 reduce-scatter.16
  956.3 87.7 reduce-scatter.14
  1047.7 282.4 reduce-scatter.22
  1334.5 281.7 reduce-scatter.20
  1620.0 58.3 reduce-scatter.30
  1684.3 141.4 all-reduce.12
  1830.4 76.6 all-reduce.14
where the time goes:
time: 1940 us; the launch traced here: 1930 us
  waiting for transfers between devices  1160 us (60%)
  blocking collectives  343 us (18%)
  matrix products  301 us (16%)
  local copies, waits for them, and re-layouts  59.7 us (3%)
  other arithmetic  42.7 us (2%)
    reduce_scatter x1, waiting for transfers between devices, on_device(): lax.psum_scatter(down_grad, 'blk', scatter_dimension=0, tiled=True)  284 us
    reduce_scatter x1, waiting for transfers between devices, on_device(): lax.psum_scatter(hidden_grad, 'blk', scatter_dimension=0, tiled=True)  283 us
    psum x1, blocking collectives, on_device(): panel_weight = lax.psum(panel_part, 'blk').astype(jnp.bfloat16)  168 us
    psum x1, waiting for transfers between devices, on_device(): panel_total = lax.psum(panel_grad, ('slide', 'blk'))  98.4 us
    dot_general x30, matrix products, matmul(): return jnp.dot(left, right, preferred_element_type=jnp.float32)  93.7 us
    reduce_scatter x1, waiting for transfers between devices, on_device(): lax.psum_scatter(key_grad, 'blk', scatter_dimension=0, tiled=True)  90.1 us
    reduce_scatter x1, waiting for transfers between devices, on_device(): lax.psum_scatter(query_grad, 'blk', scatter_dimension=0, tiled=True)  90 us
    reduce_scatter x1, waiting for transfers between devices, on_device(): lax.psum_scatter(value_grad, 'blk', scatter_dimension=0, tiled=True)  89.4 us
  transfers between devices with their start and end apart: 16, of which 11 were waited for; matrix products, arithmetic and copies ran while one was open for 19% of the time, Pallas kernels for 0%

commit v1 on v0

--- a/solution.py
+++ b/solution.py
@@ -1,11 +1,17 @@
+import functools
 import math
 
 import jax
 import jax.numpy as jnp
 from jax import lax
+from jax.experimental import pallas as pl
+from jax.experimental.pallas import tpu as pltpu
 from jax.sharding import PartitionSpec as P
 
 HEAD_DIM = 64
+MESH = pl.DeviceIdType.MESH
+F32 = jnp.float32
+BF16 = jnp.bfloat16
 
 
 def normalized(counts, library):
@@ -68,7 +74,7 @@
     return jnp.dot(left, right, preferred_element_type=jnp.float32)
 
 
-def on_device(
+def on_device_general(
     counts,
     library,
     gene_ids,
@@ -330,6 +336,655 @@
     return (decoded[None], divergence, table_grad) + tuple(summed)
 
 
+def fits(mesh):
+    return mesh.shape["slide"] == 4 and mesh.shape["blk"] == 8
+
+
+def flipped(index, mask):
+    for bit in (1, 2, 4):
+        if mask & bit:
+            index = index + bit - 2 * bit * ((index // bit) % 2)
+    return index
+
+
+def greet(slide, blk, peers):
+    barrier = pltpu.get_barrier_semaphore()
+    for far_slide, far_blk in peers:
+        pl.semaphore_signal(
+            barrier,
+            inc=1,
+            device_id={"slide": flipped(slide, far_slide), "blk": flipped(blk, far_blk)},
+            device_id_type=MESH,
+        )
+    pl.semaphore_wait(barrier, len(peers))
+
+
+def gather_blocks(slide, blk, out_ref, send_sem, recv_sem):
+    copies = {}
+
+    def push(rel_slide, rel_blk, to_slide, to_blk):
+        slot = flipped(slide, rel_slide) * 8 + flipped(blk, rel_blk)
+        key = (rel_slide ^ to_slide) * 8 + (rel_blk ^ to_blk)
+        copies[key] = pltpu.make_async_remote_copy(
+            src_ref=out_ref.at[slot],
+            dst_ref=out_ref.at[slot],
+            send_sem=send_sem.at[key],
+            recv_sem=recv_sem.at[key],
+            device_id={"slide": flipped(slide, to_slide), "blk": flipped(blk, to_blk)},
+            device_id_type=MESH,
+        )
+        copies[key].start()
+
+    for far in (2, 4, 6):
+        push(0, 0, 0, far)
+    push(0, 0, 0, 1)
+    push(0, 0, 2, 0)
+    push(0, 0, 1, 0)
+    for rel in (2, 4, 6):
+        copies[rel].wait_recv()
+        push(0, rel, 0, 1)
+        push(0, rel, 2, 0)
+        push(0, rel, 1, 0)
+    for rel in (1, 3, 5, 7):
+        copies[rel].wait_recv()
+        push(0, rel, 2, 0)
+        push(0, rel, 1, 0)
+    for rel in (0, 2, 4, 6, 1, 3, 5, 7):
+        copies[16 + rel].wait_recv()
+        push(2, rel, 1, 0)
+    for rel in (0, 2, 4, 6, 1, 3, 5, 7):
+        copies[8 + rel].wait_recv()
+    for rel in (0, 2, 4, 6, 1, 3, 5, 7):
+        copies[24 + rel].wait_recv()
+    for key in sorted(copies):
+        copies[key].wait_send()
+
+
+GATHER_PEERS = [(0, 1), (0, 2), (0, 4), (0, 6), (2, 0), (1, 0)]
+BLK_PEERS = [(0, far) for far in range(1, 8)]
+SLIDE_PEERS = [(far, 0) for far in range(1, 4)]
+
+
+def panel_kernel(part_ref, out_ref, land, send_one, recv_one, send_sem, recv_sem):
+    slide, blk = lax.axis_index("slide"), lax.axis_index("blk")
+    greet(slide, blk, BLK_PEERS + [(2, 0), (1, 0)])
+    copies = []
+    for far in range(1, 8):
+        target = flipped(blk, far)
+        copies.append(
+            pltpu.make_async_remote_copy(
+                src_ref=part_ref.at[target],
+                dst_ref=land.at[far],
+                send_sem=send_one.at[far],
+                recv_sem=recv_one.at[far],
+                device_id={"slide": slide, "blk": target},
+                device_id_type=MESH,
+            )
+        )
+        copies[-1].start()
+    total = part_ref[blk].astype(F32)
+    for far in range(1, 8):
+        copies[far - 1].wait_recv()
+        total = total + land[far].astype(F32)
+    out_ref[slide * 8 + blk] = total.astype(BF16)
+    gather_blocks(slide, blk, out_ref, send_sem, recv_sem)
+    for copy in copies:
+        copy.wait_send()
+
+
+def panel_rows(part):
+    _, rows, width = part.shape
+    return pl.pallas_call(
+        panel_kernel,
+        out_shape=jax.ShapeDtypeStruct((32, rows, width), BF16),
+        in_specs=[pl.BlockSpec(memory_space=pltpu.VMEM)],
+        out_specs=pl.BlockSpec(memory_space=pltpu.VMEM),
+        scratch_shapes=[
+            pltpu.VMEM((8, rows, width), BF16),
+            pltpu.SemaphoreType.DMA((8,)),
+            pltpu.SemaphoreType.DMA((8,)),
+            pltpu.SemaphoreType.DMA((32,)),
+            pltpu.SemaphoreType.DMA((32,)),
+        ],
+        compiler_params=pltpu.CompilerParams(
+            collective_id=1, has_side_effects=True, vmem_limit_bytes=32 << 20
+        ),
+        name="panel_rows",
+    )(part)
+
+
+def gather_kernel(block_ref, out_ref, send_sem, recv_sem):
+    slide, blk = lax.axis_index("slide"), lax.axis_index("blk")
+    greet(slide, blk, GATHER_PEERS)
+    out_ref[slide * 8 + blk] = block_ref[...]
+    gather_blocks(slide, blk, out_ref, send_sem, recv_sem)
+
+
+def gather_everywhere(block):
+    return pl.pallas_call(
+        gather_kernel,
+        out_shape=jax.ShapeDtypeStruct((32,) + block.shape, block.dtype),
+        in_specs=[pl.BlockSpec(memory_space=pltpu.VMEM)],
+        out_specs=pl.BlockSpec(memory_space=pltpu.VMEM),
+        scratch_shapes=[
+            pltpu.SemaphoreType.DMA((32,)),
+            pltpu.SemaphoreType.DMA((32,)),
+        ],
+        compiler_params=pltpu.CompilerParams(
+            collective_id=2, has_side_effects=True, vmem_limit_bytes=32 << 20
+        ),
+        name="gather_everywhere",
+    )(block)
+
+
+def exchange(slide, blk, peers, source_of, land, place, send_sem, recv_sem):
+    copies = []
+    for number, (far_slide, far_blk) in enumerate(peers):
+        to_slide, to_blk = flipped(slide, far_slide), flipped(blk, far_blk)
+        copies.append(
+            pltpu.make_async_remote_copy(
+                src_ref=source_of(to_slide, to_blk),
+                dst_ref=land.at[place],
+                send_sem=send_sem.at[number],
+                recv_sem=recv_sem.at[number],
+                device_id={"slide": to_slide, "blk": to_blk},
+                device_id_type=MESH,
+            )
+        )
+        copies[-1].start()
+    return copies
+
+
+def sum_all_kernel(in_ref, out_ref, land_one, land_two, own, send_one, recv_one, send_two, recv_two):
+    slide, blk = lax.axis_index("slide"), lax.axis_index("blk")
+    greet(slide, blk, SLIDE_PEERS + BLK_PEERS)
+    copies = exchange(slide, blk, SLIDE_PEERS, lambda *_: in_ref, land_one, slide, send_one, recv_one)
+    land_one[slide] = in_ref[...]
+    for copy in copies:
+        copy.wait()
+    own[...] = (land_one[0] + land_one[1]) + (land_one[2] + land_one[3])
+    copies = exchange(slide, blk, BLK_PEERS, lambda *_: own, land_two, blk, send_two, recv_two)
+    land_two[blk] = own[...]
+    for copy in copies:
+        copy.wait()
+    total = land_two[0]
+    for place in range(1, 8):
+        total = total + land_two[place]
+    out_ref[...] = total
+
+
+def sum_all(block):
+    return pl.pallas_call(
+        sum_all_kernel,
+        out_shape=jax.ShapeDtypeStruct(block.shape, F32),
+        in_specs=[pl.BlockSpec(memory_space=pltpu.VMEM)],
+        out_specs=pl.BlockSpec(memory_space=pltpu.VMEM),
+        scratch_shapes=[
+            pltpu.VMEM((4,) + block.shape, F32),
+            pltpu.VMEM((8,) + block.shape, F32),
+            pltpu.VMEM(block.shape, F32),
+            pltpu.SemaphoreType.DMA((3,)),
+            pltpu.SemaphoreType.DMA((3,)),
+            pltpu.SemaphoreType.DMA((7,)),
+            pltpu.SemaphoreType.DMA((7,)),
+        ],
+        compiler_params=pltpu.CompilerParams(collective_id=3, has_side_effects=True),
+        name="sum_all",
+    )(block)
+
+
+def sum_parts_kernel(in_ref, out_ref, land_one, land_two, own, send_one, recv_one, send_two, recv_two):
+    slide, blk = lax.axis_index("slide"), lax.axis_index("blk")
+    greet(slide, blk, SLIDE_PEERS + BLK_PEERS)
+    copies = exchange(
+        slide, blk, BLK_PEERS, lambda _, to_blk: in_ref.at[to_blk], land_one, blk, send_two, recv_two
+    )
+    land_one[blk] = in_ref[blk]
+    for copy in copies:
+        copy.wait()
+    total = land_one[0]
+    for place in range(1, 8):
+        total = total + land_one[place]
+    own[...] = total
+    copies = exchange(slide, blk, SLIDE_PEERS, lambda *_: own, land_two, slide, send_one, recv_one)
+    land_two[slide] = total
+    for copy in copies:
+        copy.wait()
+    out_ref[...] = (land_two[0] + land_two[1]) + (land_two[2] + land_two[3])
+
+
+def sum_parts(parts):
+    shape = parts.shape[1:]
+    return pl.pallas_call(
+        sum_parts_kernel,
+        out_shape=jax.ShapeDtypeStruct(shape, F32),
+        in_specs=[pl.BlockSpec(memory_space=pltpu.VMEM)],
+        out_specs=pl.BlockSpec(memory_space=pltpu.VMEM),
+        scratch_shapes=[
+            pltpu.VMEM((8,) + shape, F32),
+            pltpu.VMEM((4,) + shape, F32),
+            pltpu.VMEM(shape, F32),
+            pltpu.SemaphoreType.DMA((3,)),
+            pltpu.SemaphoreType.DMA((3,)),
+            pltpu.SemaphoreType.DMA((7,)),
+            pltpu.SemaphoreType.DMA((7,)),
+        ],
+        compiler_params=pltpu.CompilerParams(collective_id=4, has_side_effects=True),
+        name="sum_parts",
+    )(parts)
+
+
+def dot_nt(left, right):
+    return lax.dot_general(left, right, (((1,), (1,)), ((), ())), preferred_element_type=F32)
+
+
+def dot_tn(left, right):
+    return lax.dot_general(left, right, (((0,), (0,)), ((), ())), preferred_element_type=F32)
+
+
+def head_scores(query, key, same_slide):
+    scores = jnp.where(same_slide, dot_nt(query, key) * (HEAD_DIM**-0.5), -1e30)
+    shifted = jnp.exp(scores - jnp.max(scores, axis=1, keepdims=True))
+    return shifted / jnp.sum(shifted, axis=1, keepdims=True)
+
+
+def attend_kernel(q_ref, k_ref, v_ref, row_ref, col_ref, out_ref):
+    same_slide = row_ref[...] == col_ref[...]
+    lanes = lax.broadcasted_iota(jnp.int32, q_ref.shape, 1)
+    query, key, value = q_ref[...], k_ref[...], v_ref[...]
+    out = None
+    for head in range(q_ref.shape[1] // HEAD_DIM):
+        mine = lanes // HEAD_DIM == head
+        shares = head_scores(jnp.where(mine, query, 0), key, same_slide)
+        part = jnp.dot(shares.astype(BF16), value, preferred_element_type=F32)
+        out = part if out is None else jnp.where(mine, part, out)
+    out_ref[...] = out.astype(BF16)
+
+
+def attend(query, key, value, row_labels, col_labels, rows=256):
+    count, width = query.shape
+    whole = pl.BlockSpec((count, width), lambda i: (0, 0))
+    part = pl.BlockSpec((rows, width), lambda i: (i, 0))
+    return pl.pallas_call(
+        attend_kernel,
+        grid=(count // rows,),
+        out_shape=jax.ShapeDtypeStruct((count, width), BF16),
+        in_specs=[
+            part,
+            whole,
+            whole,
+            pl.BlockSpec((rows, 1), lambda i: (i, 0)),
+            pl.BlockSpec((1, count), lambda i: (0, 0)),
+        ],
+        out_specs=part,
+        compiler_params=pltpu.CompilerParams(vmem_limit_bytes=48 << 20),
+        cost_estimate=pl.CostEstimate(
+            flops=8 * count * count * width, bytes_accessed=8 * count * width, transcendentals=0
+        ),
+        name="attend",
+    )(query, key, value, row_labels, col_labels)
+
+
+def attend_back_kernel(q_ref, g_ref, k_ref, v_ref, row_ref, col_ref, dq_ref, dk_ref, dv_ref, dk_sum, dv_sum):
+    step = pl.program_id(0)
+
+    @pl.when(step == 0)
+    def _():
+        dk_sum[...] = jnp.zeros_like(dk_sum)
+        dv_sum[...] = jnp.zeros_like(dv_sum)
+
+    scale = HEAD_DIM**-0.5
+    same_slide = row_ref[...] == col_ref[...]
+    lanes = lax.broadcasted_iota(jnp.int32, q_ref.shape, 1)
+    query, grad, key, value = q_ref[...], g_ref[...], k_ref[...], v_ref[...]
+    grad_query = None
+    for head in range(q_ref.shape[1] // HEAD_DIM):
+        mine = lanes // HEAD_DIM == head
+        own_query = jnp.where(mine, query, 0)
+        own_grad = jnp.where(mine, grad, 0)
+        shares = head_scores(own_query, key, same_slide)
+        grad_shares = dot_nt(own_grad, value)
+        inner = jnp.sum(shares * grad_shares, axis=1, keepdims=True)
+        grad_scores = (shares * (grad_shares - inner)).astype(BF16)
+        part = jnp.dot(grad_scores, key, preferred_element_type=F32)
+        grad_query = part if grad_query is None else jnp.where(mine, part, grad_query)
+        dk_sum[...] += dot_tn(grad_scores, own_query)
+        dv_sum[...] += dot_tn(shares.astype(BF16), own_grad)
+    dq_ref[...] = (grad_query * scale).astype(BF16)
+
+    @pl.when(step == pl.num_programs(0) - 1)
+    def _():
+        dk_ref[...] = (dk_sum[...] * scale).astype(BF16)
+        dv_ref[...] = dv_sum[...].astype(BF16)
+
+
+def attend_back(query, grad, key, value, row_labels, col_labels, rows=256):
+    count, width = query.shape
+    whole = pl.BlockSpec((count, width), lambda i: (0, 0))
+    part = pl.BlockSpec((rows, width), lambda i: (i, 0))
+    shape = jax.ShapeDtypeStruct((count, width), BF16)
+    return pl.pallas_call(
+        attend_back_kernel,
+        grid=(count // rows,),
+        out_shape=(shape, shape, shape),
+        in_specs=[
+            part,
+            part,
+            whole,
+            whole,
+            pl.BlockSpec((rows, 1), lambda i: (i, 0)),
+            pl.BlockSpec((1, count), lambda i: (0, 0)),
+        ],
+        out_specs=(part, whole, whole),
+        scratch_shapes=[pltpu.VMEM((count, width), F32), pltpu.VMEM((count, width), F32)],
+        compiler_params=pltpu.CompilerParams(vmem_limit_bytes=48 << 20),
+        cost_estimate=pl.CostEstimate(
+            flops=20 * count * count * width, bytes_accessed=14 * count * width, transcendentals=0
+        ),
+        name="attend_back",
+    )(query, grad, key, value, row_labels, col_labels)
+
+
+def over_slide(array, mask):
+    return lax.ppermute(array, "slide", [(place, place ^ mask) for place in range(4)])
+
+
+def over_blk(array, mask):
+    return lax.ppermute(array, "blk", [(place, place ^ mask) for place in range(8)])
+
+
+def gather_slide(array):
+    far = over_slide(array, 2)
+    return [array, over_slide(array, 1), far, over_slide(far, 1)]
+
+
+def swap_slide(pick, slide):
+    return [pick(slide)] + [over_slide(pick(jnp.bitwise_xor(slide, far)), far) for far in (1, 2, 3)]
+
+
+def in_order(parts, index):
+    low = jnp.bitwise_and(index, 1) == 1
+    high = jnp.bitwise_and(index, 2) == 2
+    one = [jnp.where(low, parts[j ^ 1], parts[j]) for j in range(4)]
+    return [jnp.where(high, one[j ^ 2], one[j]) for j in range(4)]
+
+
+def reduce_blk(left, right, blk):
+    cells, total_rows = left.shape
+    rows = total_rows // 8
+    shaped = left.reshape(cells, 4, 2, rows)
+    along_x = blk % 2
+    along_z = blk // 2
+
+    def half(which):
+        columns = lax.dynamic_index_in_dim(shaped, which, 2, keepdims=False).reshape(cells, 4 * rows)
+        return dot_tn(columns, right)
+
+    away = over_blk(half(1 - along_x).astype(BF16), 1)
+    kept = (half(along_x) + away.astype(F32)).astype(BF16).reshape(4, rows, right.shape[1])
+
+    def piece(which):
+        return lax.dynamic_index_in_dim(kept, which, 0, keepdims=False)
+
+    total = piece(along_z).astype(F32)
+    for far in (1, 2, 3):
+        total = total + over_blk(piece(jnp.bitwise_xor(along_z, far)), 2 * far).astype(F32)
+    return total.astype(BF16)
+
+
+def on_device_fast(
+    counts,
+    library,
+    gene_ids,
+    positions,
+    slide_of_cell,
+    latent_noise,
+    decoded_grad,
+    gene_table,
+    first_gain,
+    first_shift,
+    query_weight,
+    key_weight,
+    value_weight,
+    output_weight,
+    second_gain,
+    second_shift,
+    hidden_weight,
+    hidden_bias,
+    down_weight,
+    down_bias,
+    mean_weight,
+    logvar_weight,
+    component_means,
+    decoder_weight,
+    divergence_weight,
+    free_floor,
+):
+    cells = counts.shape[1]
+    width = gene_table.shape[1]
+    genes = gene_ids.shape[0]
+    latents = mean_weight.shape[1]
+    inner = hidden_weight.shape[1]
+    slide, blk = lax.axis_index("slide"), lax.axis_index("blk")
+    per = width // 8
+
+    def columns(array, start, size):
+        return lax.dynamic_slice_in_dim(array, start, size, 1)
+
+    table_rows = gene_table.shape[0]
+    first_row = blk * table_rows
+    row_ids = first_row + jnp.arange(table_rows, dtype=jnp.int32)
+    my_ids = lax.dynamic_slice_in_dim(gene_ids, slide * (genes // 4), genes // 4, 0)
+    selector = (my_ids[:, None] == row_ids[None, :]).astype(BF16)
+    part = matmul(selector, gene_table).astype(BF16).reshape(8, genes // 32, width)
+    panel_weight = panel_rows(part).reshape(genes, width)
+
+    express = normalized(counts[0], library[0]).astype(BF16)
+    hidden_start = matmul(express, panel_weight) + position_code(positions[0], width)
+    normed_one = layer_norm(hidden_start, first_gain, first_shift).astype(BF16)
+
+    def to_blocks(array):
+        return array.reshape(cells, 8, per).transpose(1, 0, 2)
+
+    def from_blocks(array):
+        return array.transpose(1, 0, 2).reshape(cells, 8 * per)
+
+    labels = jnp.broadcast_to(
+        jnp.pad(slide_of_cell[0].astype(BF16), (0, per - cells))[None, None, :], (8, 16, per)
+    )
+    qkv = jnp.concatenate(
+        [to_blocks(matmul(normed_one, w).astype(BF16)) for w in (query_weight, key_weight, value_weight)]
+        + [labels],
+        axis=1,
+    )
+    qkv = lax.all_to_all(qkv, "blk", 0, 0)
+    query, key, value = [
+        qkv[:, i * cells : (i + 1) * cells].reshape(8 * cells, per) for i in range(3)
+    ]
+    labels_all = qkv[:, 3 * cells, :cells].reshape(8 * cells).astype(F32)
+    row_labels, col_labels = labels_all[:, None], labels_all[None, :]
+    attended = attend(query, key, value, row_labels, col_labels)
+    attended = from_blocks(lax.all_to_all(attended.reshape(8, cells, per), "blk", 0, 0))
+
+    hidden_middle = hidden_start + matmul(attended, output_weight)
+    normed_two = layer_norm(hidden_middle, second_gain, second_shift).astype(BF16)
+    inner_sum = matmul(normed_two, hidden_weight) + hidden_bias
+    act_low = gelu_tanh(inner_sum).astype(BF16)
+    hidden_final = hidden_middle + matmul(act_low, down_weight) + down_bias
+    base_low = hidden_final.astype(BF16)
+    mean_lat = matmul(base_low, mean_weight)
+    log_var = matmul(base_low, logvar_weight)
+    noise_local = latent_noise[0]
+
+    def bottleneck(mean_part, logvar_part, centres):
+        return (
+            mean_part + jnp.exp(0.5 * logvar_part) * noise_local,
+            divergence_cells(mean_part, logvar_part, centres),
+        )
+
+    (latent, kl_cell), pull_latent = jax.vjp(bottleneck, mean_lat, log_var, component_means)
+    latent_low = latent.astype(BF16)
+    decoded = matmul(latent_low, decoder_weight)
+    everyone = cells * 32
+    kl_rows = jnp.pad(jnp.sum(kl_cell, axis=0).reshape(-1, 128), ((0, 8 - latents // 128), (0, 0)))
+    kl_mean = sum_all(kl_rows)[: latents // 128].reshape(latents) / everyone
+    divergence = divergence_weight * jnp.mean(jnp.maximum(kl_mean, free_floor))
+    binding = (kl_mean > free_floor).astype(F32)
+    grad_source = decoded_grad[0]
+
+    whole_fwd = jnp.concatenate([express, normed_one, attended, normed_two, base_low, latent_low], axis=1)
+    whole_fwd = jnp.concatenate(gather_slide(whole_fwd), axis=0)
+    express_all, normed_one_all, attended_all, normed_two_all, base_all = [
+        whole_fwd[:, i * width : (i + 1) * width] for i in range(5)
+    ]
+    latent_all = whole_fwd[:, 5 * width :]
+    act_parts = act_low.reshape(cells, 8, 4, inner // 32)
+
+    def pick_fwd(which):
+        act = lax.dynamic_index_in_dim(act_parts, which, 2, keepdims=False).reshape(cells, inner // 4)
+        return jnp.concatenate([act, columns(grad_source, which * (genes // 4), genes // 4)], axis=1)
+
+    quarter_fwd = jnp.concatenate(swap_slide(pick_fwd, slide), axis=0)
+    act_all, source_all = quarter_fwd[:, : inner // 4], quarter_fwd[:, inner // 4 :]
+
+    grad_latent = matmul(grad_source, decoder_weight.T)
+    grad_kl = jnp.broadcast_to(divergence_weight * binding, kl_cell.shape)
+    grad_mean, grad_logvar, centres_grad = pull_latent((grad_latent, grad_kl))
+    grad_mean_low = grad_mean.astype(BF16)
+    grad_logvar_low = grad_logvar.astype(BF16)
+    grad_final = matmul(grad_mean_low, mean_weight.T) + matmul(grad_logvar_low, logvar_weight.T)
+    grad_branch = grad_final.astype(BF16)
+    down_bias_grad = jnp.sum(grad_branch.astype(F32), axis=0)
+    branch_all = jnp.concatenate(gather_slide(grad_branch), axis=0)
+    lat_quarter = latents // 4
+
+    def pick_lat(which):
+        return jnp.concatenate(
+            [
+                columns(grad_mean_low, which * lat_quarter, lat_quarter),
+                columns(grad_logvar_low, which * lat_quarter, lat_quarter),
+            ],
+            axis=1,
+        )
+
+    lat_all = jnp.concatenate(swap_slide(pick_lat, slide), axis=0)
+    down_sum = reduce_blk(act_all, branch_all, blk)
+    lat_sum = reduce_blk(base_all, lat_all, blk)
+    decoder_sum = reduce_blk(latent_all, source_all, blk)
+
+    grad_act = matmul(grad_branch, down_weight.T)
+    gelu_pull = jax.vjp(gelu_tanh, inner_sum)[1]
+    grad_inner = gelu_pull(grad_act)[0].astype(BF16)
+    hidden_bias_grad = jnp.sum(grad_inner.astype(F32), axis=0)
+    norm_two_pull = jax.vjp(layer_norm, hidden_middle, second_gain, second_shift)[1]
+    grad_norm_two, second_gain_grad, second_shift_grad = norm_two_pull(matmul(grad_inner, hidden_weight.T))
+    grad_middle = grad_final + grad_norm_two
+    grad_out = grad_middle.astype(BF16)
+    inner_all = jnp.concatenate(
+        swap_slide(lambda which: columns(grad_inner, which * (inner // 4), inner // 4), slide), axis=0
+    )
+    hidden_sum = reduce_blk(normed_two_all, inner_all, blk)
+    out_all = jnp.concatenate(
+        swap_slide(lambda which: columns(grad_out, which * (width // 4), width // 4), slide), axis=0
+    )
+    output_sum = reduce_blk(attended_all, out_all, blk)
+
+    grad_attended = matmul(grad_out, output_weight.T).astype(BF16)
+    grad_heads = lax.all_to_all(to_blocks(grad_attended), "blk", 0, 0).reshape(8 * cells, per)
+    grads = attend_back(query, grad_heads, key, value, row_labels, col_labels)
+    grads = jnp.concatenate([grad.reshape(8, cells, per) for grad in grads], axis=1)
+    grads = lax.all_to_all(grads, "blk", 0, 0)
+    grad_query, grad_key, grad_value = [
+        from_blocks(grads[:, i * cells : (i + 1) * cells]) for i in range(3)
+    ]
+    grad_norm_input = (
+        matmul(grad_query, query_weight.T) + matmul(grad_key, key_weight.T) + matmul(grad_value, value_weight.T)
+    )
+    norm_one_pull = jax.vjp(layer_norm, hidden_start, first_gain, first_shift)[1]
+    grad_norm_one, first_gain_grad, first_shift_grad = norm_one_pull(grad_norm_input)
+    grad_encoded = (grad_middle + grad_norm_one).astype(BF16)
+    quarter = width // 4
+
+    def pick_qkv(which):
+        return jnp.concatenate(
+            [columns(grad, which * quarter, quarter) for grad in (grad_query, grad_key, grad_value)], axis=1
+        )
+
+    qkv_all = jnp.concatenate(swap_slide(pick_qkv, slide), axis=0)
+    encoded_all = jnp.concatenate(
+        swap_slide(lambda which: columns(grad_encoded, which * quarter, quarter), slide), axis=0
+    )
+    panel_sum = reduce_blk(express_all, encoded_all, blk)
+    qkv_sum = reduce_blk(normed_one_all, qkv_all, blk)
+
+    panel_all = gather_everywhere(panel_sum).reshape(4, genes, quarter)
+    spread = (row_ids[:, None] == gene_ids[None, :]).astype(BF16)
+    table_grad = jnp.concatenate([matmul(spread, panel_all[i]) for i in range(4)], axis=1)
+
+    small = jnp.concatenate(
+        [
+            item.reshape(8, -1, 128)
+            for item in (
+                first_gain_grad,
+                first_shift_grad,
+                second_gain_grad,
+                second_shift_grad,
+                hidden_bias_grad,
+                down_bias_grad,
+                centres_grad.reshape(16, 8, -1).transpose(1, 0, 2),
+            )
+        ],
+        axis=1,
+    )
+    count = small.shape[1]
+    small = sum_parts(jnp.pad(small, ((0, 0), (0, -count % 8), (0, 0))))
+    bias_rows = inner // 8 // 128
+    small_gain_one, small_shift_one, small_gain_two, small_shift_two = [
+        small[i] for i in range(4)
+    ]
+    small_hidden = small[4 : 4 + bias_rows].reshape(-1)
+    small_down = small[4 + bias_rows]
+    small_centres = small[5 + bias_rows : count].reshape(16, -1)
+
+    def wide(total):
+        return jnp.concatenate(in_order([p.astype(F32) for p in gather_slide(total)], slide), axis=1)
+
+    def tall(total):
+        return jnp.concatenate(in_order([p.astype(F32) for p in gather_slide(total)], slide), axis=0)
+
+    def split(total, sizes):
+        parts = in_order([p.astype(F32) for p in gather_slide(total)], slide)
+        outs, start = [], 0
+        for size in sizes:
+            outs.append(jnp.concatenate([p[:, start : start + size] for p in parts], axis=1))
+            start += size
+        return outs
+
+    query_grad, key_grad, value_grad = split(qkv_sum, [quarter] * 3)
+    mean_grad, logvar_grad = split(lat_sum, [lat_quarter] * 2)
+    return (
+        decoded[None],
+        divergence,
+        table_grad,
+        small_gain_one,
+        small_shift_one,
+        query_grad,
+        key_grad,
+        value_grad,
+        wide(output_sum),
+        small_gain_two,
+        small_shift_two,
+        wide(hidden_sum),
+        small_hidden,
+        tall(down_sum),
+        small_down,
+        mean_grad,
+        logvar_grad,
+        small_centres,
+        wide(decoder_sum),
+    )
+
+
 def solution(mesh):
     placed = (
         P("slide", "blk", None),
@@ -360,7 +1015,7 @@
         P(),
     )
     return jax.shard_map(
-        on_device,
+        on_device_fast if fits(mesh) else on_device_general,
         mesh=mesh,
         in_specs=placed,
         out_specs=(

time: 1940 us -> 564 us (0.29)
  the two profiles are of different devices: /device:TPU:1 before, /device:TPU:13 now
where the time goes in v1:
time: 564 us; the launch traced here: 555 us
  waiting for transfers between devices  122 us (22%)
  local copies, waits for them, and re-layouts  104 us (18%)
  starting transfers between devices  103 us (18%)
  Pallas kernels  90.7 us (16%)
  matrix products  82.2 us (15%)
  other arithmetic  47.1 us (8%)
  between operations  5.8 us (1%)
    ppermute x28, waiting for transfers between devices, over_blk(): lax.ppermute(array, 'blk', [(place, place ^ mask) for place in range(8)])  76.5 us
    dot_general x24, matrix products, matmul(): return jnp.dot(left, right, preferred_element_type=jnp.float32)  53 us
    ppermute x42, starting transfers between devices, over_slide(): lax.ppermute(array, 'slide', [(place, place ^ mask) for place in range(4)])  50.5 us
    unnamed x284, local copies, waits for them, and re-layouts  47.3 us
    pallas_call x1, Pallas kernels, panel_rows(): pl.pallas_call(panel_kernel, out_shape=jax.ShapeDtypeStruct((32, rows, wi...  32 us
    ppermute x28, starting transfers between devices, over_blk(): lax.ppermute(array, 'blk', [(place, place ^ mask) for place in range(8)])  31.9 us
    dot_general x14, matrix products, dot_tn(): lax.dot_general(left, right, (((0,), (0,)), ((), ())), preferred_element_...  24.2 us
    ppermute x42, waiting for transfers between devices, over_slide(): lax.ppermute(array, 'slide', [(place, place ^ mask) for place in range(4)])  23.2 us
  transfers between devices with their start and end apart: 74, of which 21 were waited for; matrix products, arithmetic and copies ran while one was open for 32% of the time, Pallas kernels for 7%

profile of v1, /device:TPU:13, one launch (start us, length us, event | category | flops | bytes accessed | tf_op | source)
XLA Modules:
  0.0 554.6 jit_solution(13422310685614898874)
XLA Ops:
  5.2 32.0 %panel_rows.1 = bf16[32,32,1024]{2,1,0:T(8,128)(2,1)S(1)} custom-call(bf16[8,32,1024]{2,1,0:T(8,128)(2,1)S(1)} %bitcast.307), custom_call_target="tpu_custom_call" | custom-call | tf_op jit(solution)/shard_map/panel_rows/pallas_call | solution.py:437
  49.4 18.6 %all-to-all-done = bf16[8,400,128]{2,1,0:T(8,128)(2,1)S(1)} async-done(((bf16[8,400,128]{2,1,0:T(8,128)(2,1)}), bf16[8,400,128]{2,1,0:T(8,128)(2,1)S(1)}, u32[]{:S(2)}, u32[]{:S(2)}) %all-to-all-start) | async-done | bytes 819232 | tf_op jit(solution)/shard_map/all_to_all | solution.py:800
  68.3 6.4 %attend.1 = bf16[1024,128]{1,0:T(8,128)(2,1)} custom-call(bf16[1024,128]{1,0:T(8,128)(2,1)S(1)} %bitcast.316, bf16[1024,128]{1,0:T(8,128)(2,1)S(1)} %bitcast.314, bf16[1024,128]{1,0:T(8,128)(2,1)S(1)} %bitcast.312, f32[1024,1]{1,0:T(8,128)S(1)} %copy.89.row_ref, f32[1,1024]{1,0:T(1,128)S(1)} %bitcast.319), custom_call_target="tpu_custom_call" | custom-call | flops 1073741824 | bytes 1048576 | tf_op jit(solution)/shard_map/attend/pallas_call | solution.py:608
  75.5 6.2 %all-to-all-start.1 = ((bf16[8,128,128]{2,1,0:T(8,128)(2,1)}), bf16[8,128,128]{2,1,0:T(8,128)(2,1)S(1)}, u32[]{:S(2)}, u32[]{:S(2)}) async-start(bf16[8,128,128]{2,1,0:T(8,128)(2,1)} %bitcast.15), calls=%async_computation.1 | async-start | bytes 524288 | tf_op jit(solution)/shard_map/all_to_all | solution.py:807
  92.2 7.0 %multiply_convert_fusion = (bf16[128,4096]{1,0:T(8,128)(2,1)}, f32[128,4096]{1,0:T(8,128)}) fusion(f32[4096]{0:T(1024)S(1)} %copy-done.128, bf16[1024,4096]{1,0:T(8,128)(2,1)} %param.42, f32[128,1024]{1,0:T(8,128)S(1)} %get-tuple-element.258, f32[1024]{0:T(1024)S(1)} %copy-done.107, f32[1024]{0:T(1024)S(1)} %copy-done.84, f32[128]{0:T(128)S(1)} %fusion.122, ...), kind=kOutput, calls=%fused_computation.34 | convolution fusion | flops 1079640064 | bytes 12084224 | tf_op jit(solution)/shard_map/dot_general | solution.py:74
  102.1 5.8 %constant_dynamic-update-slice_fusion.1 = (bf16[128,5632]{1,0:T(8,128)(2,1)}, bf16[128,1024]{1,0:T(8,128)(2,1)S(1)}) fusion(bf16[128,5632]{1,0:T(8,128)(2,1)} %constant_dynamic-update-slice_fusion.2, f32[1024]{0:T(1024)S(1)} %copy-done.108, f32[128,1024]{1,0:T(8,128)S(1)} %get-tuple-element.258, bf16[128,4096]{1,0:T(8,128)(2,1)} %get-tuple-element.259, ...), kind=kOutput, calls=%fused_computation.321 | convolution fusion | flops 1074135040 | bytes 10489856 | tf_op jit(solution)/shard_map/dot_general | solution.py:74
  112.6 11.5 %sum_all.1 = f32[8,128]{1,0:T(8,128)} custom-call(f32[8,128]{1,0:T(8,128)} %pad.8.in_ref), custom_call_target="tpu_custom_call" | custom-call | tf_op jit(solution)/shard_map/sum_all/pallas_call | solution.py:517
  132.4 8.4 %convert_reduce_fusion = (f32[4096]{0:T(1024)}, bf16[128,4096]{1,0:T(8,128)(2,1)S(1)}) fusion(f32[128,4096]{1,0:T(8,128)S(1)} %copy-done.131, bf16[128,1024]{1,0:T(8,128)(2,1)} %get-tuple-element.89, bf16[4096,1024]{1,0:T(8,128)(2,1)} %param.44), kind=kOutput, calls=%fused_computation.33 | convolution fusion | flops 1087369216 | bytes 11812864 | tf_op jit(solution)/shard_map/dot_general | solution.py:74
  179.4 7.9 %collective-permute-done.41 = bf16[128,1280]{0,1:T(8,128)(2,1)} collective-permute-done((bf16[128,1280]{0,1:T(8,128)(2,1)}, bf16[128,1280]{0,1:T(8,128)(2,1)}, u32[]{:S(2)}, u32[]{:S(2)}) %collective-permute-start.41) | collective-permute-done | bytes 327712 | tf_op jit(solution)/shard_map/ppermute | solution.py:689
  206.8 9.5 %attend_back.1 = (bf16[1024,128]{1,0:T(8,128)(2,1)S(1)}, bf16[1024,128]{1,0:T(8,128)(2,1)S(1)}, bf16[1024,128]{1,0:T(8,128)(2,1)S(1)}) custom-call(bf16[1024,128]{1,0:T(8,128)(2,1)S(1)} %bitcast.317, bf16[1024,128]{1,0:T(8,128)(2,1)S(1)} %bitcast.308, bf16[1024,128]{1,0:T(8,128)(2,1)S(1)} %bitcast.315, bf16[1024,128]{1,0:T(8,128)(2,1)S(1)} %bitcast.313, ...), custom_call_target="tpu_custom_call" | custom-call | flops 2684354560 | bytes 1835008 | tf_op jit(solution)/shard_map/attend_back/pallas_call | solution.py:666
  219.7 5.6 %all-to-all-start.3 = ((bf16[8,384,128]{1,2,0:T(8,128)(2,1)}), bf16[8,384,128]{1,2,0:T(8,128)(2,1)}, u32[]{:S(2)}, u32[]{:S(2)}) async-start(bf16[8,384,128]{1,2,0:T(8,128)(2,1)} %pad_maximum_fusion.8), calls=%async_computation.3 | async-start | bytes 1572864 | tf_op jit(solution)/shard_map/all_to_all | solution.py:896
  247.5 12.7 %collective-permute-done.48 = bf16[128,1024]{1,0:T(8,128)(2,1)} collective-permute-done((bf16[128,1024]{1,0:T(8,128)(2,1)}, bf16[128,1024]{1,0:T(8,128)(2,1)}, u32[]{:S(2)}, u32[]{:S(2)}) %collective-permute-start.48) | collective-permute-done | bytes 262176 | tf_op jit(solution)/shard_map/ppermute | solution.py:693
  260.2 7.5 %collective-permute-done.49 = bf16[128,1024]{1,0:T(8,128)(2,1)} collective-permute-done((bf16[128,1024]{1,0:T(8,128)(2,1)}, bf16[128,1024]{1,0:T(8,128)(2,1)}, u32[]{:S(2)}, u32[]{:S(2)}) %collective-permute-start.49) | collective-permute-done | bytes 262176 | tf_op jit(solution)/shard_map/ppermute | solution.py:693
  281.7 10.4 %sum_parts.1 = f32[24,128]{1,0:T(8,128)} custom-call(f32[8,24,128]{2,1,0:T(8,128)} %pad.9.in_ref), custom_call_target="tpu_custom_call" | custom-call | tf_op jit(solution)/shard_map/sum_parts/pallas_call | solution.py:558
  315.5 7.0 %constant_dynamic-slice_fusion.2 = (bf16[512,4,1,128]{3,2,1,0:T(2,128)(2,1)}, bf16[512,4,1,128]{3,2,1,0:T(2,128)(2,1)}, bf16[512,4,1,128]{3,2,1,0:T(2,128)(2,1)}, bf16[512,4,1,128]{3,2,1,0:T(2,128)(2,1)}) fusion(bf16[512,4,2,128]{3,2,1,0:T(2,128)(2,1)} %reshape.498, s32[]{:T(128)S(6)} %select_n.385, s32[]{:T(128)S(6)} %select_n.381, ...), kind=kLoop, calls=%fused_computation.268 | loop fusion | bytes 4194312 | tf_op jit(solution)/shard_map/jit(dynamic_index_in_dim)/dynamic_slice | solution.py:720
  322.6 5.7 %constant_dynamic-slice_fusion.28 = (bf16[512,4,1,128]{3,2,1,0:T(2,128)(2,1)}, bf16[512,4,1,128]{3,2,1,0:T(2,128)(2,1)}, bf16[512,4,1,128]{3,2,1,0:T(2,128)(2,1)}, bf16[512,4,1,128]{3,2,1,0:T(2,128)(2,1)}) fusion(bf16[512,4,2,128]{3,2,1,0:T(2,128)(2,1)S(1)} %reshape.480, s32[]{:T(128)S(6)} %select_n.385, s32[]{:T(128)S(6)} %select_n.381, ...), kind=kLoop, calls=%fused_computation.294 | loop fusion | bytes 4194312 | tf_op jit(solution)/shard_map/jit(dynamic_index_in_dim)/dynamic_slice | solution.py:720
  396.9 12.0 %collective-permute-done.23 = bf16[512,256]{1,0:T(8,128)(2,1)} collective-permute-done((bf16[512,256]{1,0:T(8,128)(2,1)}, bf16[512,256]{1,0:T(8,128)(2,1)}, u32[]{:S(2)}, u32[]{:S(2)}) %collective-permute-start.23) | collective-permute-done | bytes 262176 | tf_op jit(solution)/shard_map/ppermute | solution.py:693
  412.5 18.8 %collective-permute-done.6 = bf16[512,256]{1,0:T(8,128)(2,1)S(1)} collective-permute-done((bf16[512,256]{1,0:T(8,128)(2,1)}, bf16[512,256]{1,0:T(8,128)(2,1)S(1)}, u32[]{:S(2)}, u32[]{:S(2)}) %collective-permute-start.6) | collective-permute-done | bytes 262176 | tf_op jit(solution)/shard_map/ppermute | solution.py:693
  449.8 20.8 %gather_everywhere.1 = bf16[32,128,256]{2,1,0:T(8,128)(2,1)S(1)} custom-call(bf16[128,256]{1,0:T(8,128)(2,1)S(1)} %fusion.93.block_ref), custom_call_target="tpu_custom_call" | custom-call | tf_op jit(solution)/shard_map/gather_everywhere/pallas_call | solution.py:464
  482.0 9.5 %copy.118 = f32[2048,1024]{1,0:T(8,128)} copy(f32[2048,1024]{0,1:T(8,128)} %pad_maximum_fusion) | data formatting | bytes 16777216
  507.8 8.6 %collective-permute-done.16 = bf16[128,768]{1,0:T(8,128)(2,1)S(1)} collective-permute-done((bf16[128,768]{1,0:T(8,128)(2,1)S(1)}, bf16[128,768]{1,0:T(8,128)(2,1)S(1)}, u32[]{:S(2)}, u32[]{:S(2)}) %collective-permute-start.16) | collective-permute-done | bytes 196640 | tf_op jit(solution)/shard_map/ppermute | solution.py:693
  518.2 12.4 %collective-permute-start.19 = (bf16[128,768]{1,0:T(8,128)(2,1)S(1)}, bf16[128,768]{1,0:T(8,128)(2,1)S(1)}, u32[]{:S(2)}, u32[]{:S(2)}) collective-permute-start(bf16[128,768]{1,0:T(8,128)(2,1)S(1)} %fusion.64), channel_id=1, source_target_pairs={{0,8},{8,0},{16,24},{24,16},{1,9},{9,1},{17,25},{25,17},{2,10},{10... | collective-permute-start | bytes 589832 | tf_op jit(solution)/shard_map/ppermute | solution.py:689
  532.7 6.2 %collective-permute-done.36 = bf16[128,1024]{1,0:T(8,128)(2,1)S(1)} collective-permute-done((bf16[128,1024]{1,0:T(8,128)(2,1)S(1)}, bf16[128,1024]{1,0:T(8,128)(2,1)S(1)}, u32[]{:S(2)}, u32[]{:S(2)}) %collective-permute-start.36) | collective-permute-done | bytes 262176 | tf_op jit(solution)/shard_map/ppermute | solution.py:693
  540.8 4.8 collective-permute-done.37
  (601 shorter events, 293.3 us)
Async XLA Ops:
  131.7 46.8 %collective-permute-start.44 = (bf16[128,1024]{1,0:T(8,128)(2,1)}, bf16[128,1024]{1,0:T(8,128)(2,1)}, u32[]{:S(2)}, u32[]{:S(2)}) collective-permute-start(bf16[128,1024]{1,0:T(8,128)(2,1)} %get-tuple-element.89), channel_id=1, source_target_pairs={{0,16},{8,24},{16,0},{24,8},{1,17},{9,25},{17,1},{25,9},{2,18},{10... | collective-permute-start | bytes 786440 | tf_op jit(solution)/shard_map/ppermute | solution.py:689
  148.4 93.7 %collective-permute-start.1 = (bf16[128,5632]{1,0:T(8,128)(2,1)}, bf16[128,5632]{1,0:T(8,128)(2,1)}, u32[]{:S(2)}, u32[]{:S(2)}) collective-permute-start(bf16[128,5632]{1,0:T(8,128)(2,1)} %get-tuple-element.102), channel_id=1, source_target_pairs={{0,16},{8,24},{16,0},{24,8},{1,17},{9,25},{17,1},{25,9},{2,18},{10... | collective-permute-start | bytes 4325384 | tf_op jit(solution)/shard_map/ppermute | solution.py:689
  165.3 30.7 %collective-permute-start.42 = (bf16[128,1280]{0,1:T(8,128)(2,1)}, bf16[128,1280]{0,1:T(8,128)(2,1)}, u32[]{:S(2)}, u32[]{:S(2)}) collective-permute-start(bf16[128,1280]{0,1:T(8,128)(2,1)} %pad_maximum_fusion.17), channel_id=1, source_target_pairs={{0,24},{8,16},{16,8},{24,0},{1,25},{9,17},{17,9},{25,1},{2,26},{10... | collective-permute-start | bytes 983048 | tf_op jit(solution)/shard_map/ppermute | solution.py:689
  168.0 35.9 %all-to-all-start.2 = ((bf16[8,128,128]{2,1,0:T(8,128)(2,1)}), bf16[8,128,128]{2,1,0:T(8,128)(2,1)S(1)}, u32[]{:S(2)}, u32[]{:S(2)}) async-start(bf16[8,128,128]{2,1,0:T(8,128)(2,1)} %bitcast.345), calls=%async_computation.2 | async-start | bytes 524288 | tf_op jit(solution)/shard_map/all_to_all | solution.py:893
  178.5 123.4 %collective-permute-start = (bf16[128,5632]{1,0:T(8,128)(2,1)}, bf16[128,5632]{1,0:T(8,128)(2,1)}, u32[]{:S(2)}, u32[]{:S(2)}) collective-permute-start(bf16[128,5632]{1,0:T(8,128)(2,1)} %get-tuple-element.102), channel_id=1, source_target_pairs={{0,8},{8,0},{16,24},{24,16},{1,9},{9,1},{17,25},{25,17},{2,10},{10... | collective-permute-start | bytes 4325384 | tf_op jit(solution)/shard_map/ppermute | solution.py:689
  219.7 51.4 %all-to-all-start.3 = ((bf16[8,384,128]{1,2,0:T(8,128)(2,1)}), bf16[8,384,128]{1,2,0:T(8,128)(2,1)}, u32[]{:S(2)}, u32[]{:S(2)}) async-start(bf16[8,384,128]{1,2,0:T(8,128)(2,1)} %pad_maximum_fusion.8), calls=%async_computation.3 | async-start | bytes 1572864 | tf_op jit(solution)/shard_map/all_to_all | solution.py:896
  234.2 33.5 %collective-permute-start.49 = (bf16[128,1024]{1,0:T(8,128)(2,1)}, bf16[128,1024]{1,0:T(8,128)(2,1)}, u32[]{:S(2)}, u32[]{:S(2)}) collective-permute-start(bf16[128,1024]{1,0:T(8,128)(2,1)} %get-tuple-element.122), channel_id=1, source_target_pairs={{0,6},{1,7},{2,4},{3,5},{4,2},{5,3},{6,0},{7,1},{8,14},{9,15},{10,... | collective-permute-start | bytes 786440 | tf_op jit(solution)/shard_map/ppermute | solution.py:693
  242.1 116.2 %collective-permute-start.53 = (bf16[128,256]{1,0:T(8,128)(2,1)}, bf16[128,256]{1,0:T(8,128)(2,1)}, u32[]{:S(2)}, u32[]{:S(2)}) collective-permute-start(bf16[128,256]{1,0:T(8,128)(2,1)} %pad_maximum_fusion.32), channel_id=1, source_target_pairs={{0,8},{8,0},{16,24},{24,16},{1,9},{9,1},{17,25},{25,17},{2,10},{10... | collective-permute-start | bytes 196616 | tf_op jit(solution)/shard_map/ppermute | solution.py:689
  245.8 57.1 %collective-permute-start.2 = (bf16[128,5632]{1,0:T(8,128)(2,1)}, bf16[128,5632]{1,0:T(8,128)(2,1)S(1)}, u32[]{:S(2)}, u32[]{:S(2)}) collective-permute-start(bf16[128,5632]{1,0:T(8,128)(2,1)} %collective-permute-done.1), channel_id=1, source_target_pairs={{0,8},{8,0},{16,24},{24,16},{1,9},{9,1},{17,25},{25,17},{2,10},{10... | collective-permute-start | bytes 4325384 | tf_op jit(solution)/shard_map/ppermute | solution.py:689
  297.2 62.7 %collective-permute-start.54 = (bf16[128,256]{1,0:T(8,128)(2,1)}, bf16[128,256]{1,0:T(8,128)(2,1)}, u32[]{:S(2)}, u32[]{:S(2)}) collective-permute-start(bf16[128,256]{1,0:T(8,128)(2,1)} %pad_maximum_fusion.33), channel_id=1, source_target_pairs={{0,16},{8,24},{16,0},{24,8},{1,17},{9,25},{17,1},{25,9},{2,18},{10... | collective-permute-start | bytes 196616 | tf_op jit(solution)/shard_map/ppermute | solution.py:689
  298.5 35.8 %collective-permute-start.30 = (bf16[128,1024]{1,0:T(8,128)(2,1)}, bf16[128,1024]{1,0:T(8,128)(2,1)}, u32[]{:S(2)}, u32[]{:S(2)}) collective-permute-start(bf16[128,1024]{1,0:T(8,128)(2,1)} %get-tuple-element.141), channel_id=1, source_target_pairs={{0,8},{8,0},{16,24},{24,16},{1,9},{9,1},{17,25},{25,17},{2,10},{10... | collective-permute-start | bytes 786440 | tf_op jit(solution)/shard_map/ppermute | solution.py:689
  301.9 32.6 %collective-permute-start.31 = (bf16[128,1024]{1,0:T(8,128)(2,1)}, bf16[128,1024]{1,0:T(8,128)(2,1)}, u32[]{:S(2)}, u32[]{:S(2)}) collective-permute-start(bf16[128,1024]{1,0:T(8,128)(2,1)} %get-tuple-element.140), channel_id=1, source_target_pairs={{0,16},{8,24},{16,0},{24,8},{1,17},{9,25},{17,1},{25,9},{2,18},{10... | collective-permute-start | bytes 786440 | tf_op jit(solution)/shard_map/ppermute | solution.py:689
  302.9 32.6 %collective-permute-start.32 = (bf16[128,1024]{1,0:T(8,128)(2,1)}, bf16[128,1024]{1,0:T(8,128)(2,1)}, u32[]{:S(2)}, u32[]{:S(2)}) collective-permute-start(bf16[128,1024]{1,0:T(8,128)(2,1)} %get-tuple-element.142), channel_id=1, source_target_pairs={{0,24},{8,16},{16,8},{24,0},{1,25},{9,17},{17,9},{25,1},{2,26},{10... | collective-permute-start | bytes 786440 | tf_op jit(solution)/shard_map/ppermute | solution.py:689
  378.3 120.8 %collective-permute-start.33 = (bf16[512,1024]{1,0:T(8,128)(2,1)}, bf16[512,1024]{1,0:T(8,128)(2,1)}, u32[]{:S(2)}, u32[]{:S(2)}) collective-permute-start(bf16[512,1024]{1,0:T(8,128)(2,1)} %convolution_convert_fusion.1), channel_id=1, source_target_pairs={{0,1},{1,0},{2,3},{3,2},{4,5},{5,4},{6,7},{7,6},{8,9},{9,8},{10,11... | collective-permute-start | bytes 3145736 | tf_op jit(solution)/shard_map/ppermute | solution.py:693
  379.0 30.0 %collective-permute-start.23 = (bf16[512,256]{1,0:T(8,128)(2,1)}, bf16[512,256]{1,0:T(8,128)(2,1)}, u32[]{:S(2)}, u32[]{:S(2)}) collective-permute-start(bf16[512,256]{1,0:T(8,128)(2,1)} %convolution_convert_fusion.4), channel_id=1, source_target_pairs={{0,1},{1,0},{2,3},{3,2},{4,5},{5,4},{6,7},{7,6},{8,9},{9,8},{10,11... | collective-permute-start | bytes 786440 | tf_op jit(solution)/shard_map/ppermute | solution.py:693
  390.1 104.3 %collective-permute-start.13 = (bf16[512,768]{1,0:T(8,128)(2,1)}, bf16[512,768]{1,0:T(8,128)(2,1)}, u32[]{:S(2)}, u32[]{:S(2)}) collective-permute-start(bf16[512,768]{1,0:T(8,128)(2,1)} %convolution_convert_fusion.2), channel_id=1, source_target_pairs={{0,1},{1,0},{2,3},{3,2},{4,5},{5,4},{6,7},{7,6},{8,9},{9,8},{10,11... | collective-permute-start | bytes 2359304 | tf_op jit(solution)/shard_map/ppermute | solution.py:693
  390.9 40.4 %collective-permute-start.6 = (bf16[512,256]{1,0:T(8,128)(2,1)}, bf16[512,256]{1,0:T(8,128)(2,1)S(1)}, u32[]{:S(2)}, u32[]{:S(2)}) collective-permute-start(bf16[512,256]{1,0:T(8,128)(2,1)} %convolution_convert_fusion.5), channel_id=1, source_target_pairs={{0,1},{1,0},{2,3},{3,2},{4,5},{5,4},{6,7},{7,6},{8,9},{9,8},{10,11... | collective-permute-start | bytes 786440 | tf_op jit(solution)/shard_map/ppermute | solution.py:693
  394.7 38.0 %collective-permute-start.57 = (bf16[128,256]{1,0:T(8,128)(2,1)S(1)}, bf16[128,256]{1,0:T(8,128)(2,1)S(1)}, u32[]{:S(2)}, u32[]{:S(2)}) collective-permute-start(bf16[128,256]{1,0:T(8,128)(2,1)S(1)} %get-tuple-element.180), channel_id=1, source_target_pairs={{0,2},{1,3},{2,0},{3,1},{4,6},{5,7},{6,4},{7,5},{8,10},{9,11},{10,... | collective-permute-start | bytes 196616 | tf_op jit(solution)/shard_map/ppermute | solution.py:693
  443.6 34.3 %collective-permute-start.60 = (bf16[128,256]{1,0:T(8,128)(2,1)S(1)}, bf16[128,256]{1,0:T(8,128)(2,1)S(1)}, u32[]{:S(2)}, u32[]{:S(2)}) collective-permute-start(bf16[128,256]{1,0:T(8,128)(2,1)S(1)} %fusion.87), channel_id=1, source_target_pairs={{0,16},{8,24},{16,0},{24,8},{1,17},{9,25},{17,1},{25,9},{2,18},{10... | collective-permute-start | bytes 196616 | tf_op jit(solution)/shard_map/ppermute | solution.py:689
  445.8 45.8 %collective-permute-start.62 = (bf16[128,256]{1,0:T(8,128)(2,1)S(1)}, bf16[128,256]{1,0:T(8,128)(2,1)S(1)}, u32[]{:S(2)}, u32[]{:S(2)}) collective-permute-start(bf16[128,256]{1,0:T(8,128)(2,1)S(1)} %fusion.87), channel_id=1, source_target_pairs={{0,8},{8,0},{16,24},{24,16},{1,9},{9,1},{17,25},{25,17},{2,10},{10... | collective-permute-start | bytes 196616 | tf_op jit(solution)/shard_map/ppermute | solution.py:689
  448.8 43.3 %collective-permute-start.27 = (bf16[128,256]{1,0:T(8,128)(2,1)S(1)}, bf16[128,256]{1,0:T(8,128)(2,1)}, u32[]{:S(2)}, u32[]{:S(2)}) collective-permute-start(bf16[128,256]{1,0:T(8,128)(2,1)S(1)} %fusion.90), channel_id=1, source_target_pairs={{0,16},{8,24},{16,0},{24,8},{1,17},{9,25},{17,1},{25,9},{2,18},{10... | collective-permute-start | bytes 196616 | tf_op jit(solution)/shard_map/ppermute | solution.py:689
  501.4 31.2 %collective-permute-start.34 = (bf16[128,1024]{1,0:T(8,128)(2,1)S(1)}, bf16[128,1024]{1,0:T(8,128)(2,1)S(1)}, u32[]{:S(2)}, u32[]{:S(2)}) collective-permute-start(bf16[128,1024]{1,0:T(8,128)(2,1)S(1)} %get-tuple-element.134), channel_id=1, source_target_pairs={{0,2},{1,3},{2,0},{3,1},{4,6},{5,7},{6,4},{7,5},{8,10},{9,11},{10,... | collective-permute-start | bytes 786440 | tf_op jit(solution)/shard_map/ppermute | solution.py:693
  503.1 29.6 %collective-permute-start.35 = (bf16[128,1024]{1,0:T(8,128)(2,1)S(1)}, bf16[128,1024]{1,0:T(8,128)(2,1)S(1)}, u32[]{:S(2)}, u32[]{:S(2)}) collective-permute-start(bf16[128,1024]{1,0:T(8,128)(2,1)S(1)} %get-tuple-element.136), channel_id=1, source_target_pairs={{0,4},{1,5},{2,6},{3,7},{4,0},{5,1},{6,2},{7,3},{8,12},{9,13},{10,... | collective-permute-start | bytes 786440 | tf_op jit(solution)/shard_map/ppermute | solution.py:693
  504.9 34.0 %collective-permute-start.36 = (bf16[128,1024]{1,0:T(8,128)(2,1)S(1)}, bf16[128,1024]{1,0:T(8,128)(2,1)S(1)}, u32[]{:S(2)}, u32[]{:S(2)}) collective-permute-start(bf16[128,1024]{1,0:T(8,128)(2,1)S(1)} %get-tuple-element.135), channel_id=1, source_target_pairs={{0,6},{1,7},{2,4},{3,5},{4,2},{5,3},{6,0},{7,1},{8,14},{9,15},{10,... | collective-permute-start | bytes 786440 | tf_op jit(solution)/shard_map/ppermute | solution.py:693
  (184 other events, 1607.3 us)

commit v2 on v1

--- a/solution.py
+++ b/solution.py
@@ -359,77 +359,23 @@
     pl.semaphore_wait(barrier, len(peers))
 
 
-def gather_blocks(slide, blk, out_ref, send_sem, recv_sem):
-    copies = {}
-
-    def push(rel_slide, rel_blk, to_slide, to_blk):
-        slot = flipped(slide, rel_slide) * 8 + flipped(blk, rel_blk)
-        key = (rel_slide ^ to_slide) * 8 + (rel_blk ^ to_blk)
-        copies[key] = pltpu.make_async_remote_copy(
-            src_ref=out_ref.at[slot],
-            dst_ref=out_ref.at[slot],
-            send_sem=send_sem.at[key],
-            recv_sem=recv_sem.at[key],
-            device_id={"slide": flipped(slide, to_slide), "blk": flipped(blk, to_blk)},
-            device_id_type=MESH,
-        )
-        copies[key].start()
-
-    for far in (2, 4, 6):
-        push(0, 0, 0, far)
-    push(0, 0, 0, 1)
-    push(0, 0, 2, 0)
-    push(0, 0, 1, 0)
-    for rel in (2, 4, 6):
-        copies[rel].wait_recv()
-        push(0, rel, 0, 1)
-        push(0, rel, 2, 0)
-        push(0, rel, 1, 0)
-    for rel in (1, 3, 5, 7):
-        copies[rel].wait_recv()
-        push(0, rel, 2, 0)
-        push(0, rel, 1, 0)
-    for rel in (0, 2, 4, 6, 1, 3, 5, 7):
-        copies[16 + rel].wait_recv()
-        push(2, rel, 1, 0)
-    for rel in (0, 2, 4, 6, 1, 3, 5, 7):
-        copies[8 + rel].wait_recv()
-    for rel in (0, 2, 4, 6, 1, 3, 5, 7):
-        copies[24 + rel].wait_recv()
-    for key in sorted(copies):
-        copies[key].wait_send()
-
-
-GATHER_PEERS = [(0, 1), (0, 2), (0, 4), (0, 6), (2, 0), (1, 0)]
 BLK_PEERS = [(0, far) for far in range(1, 8)]
 SLIDE_PEERS = [(far, 0) for far in range(1, 4)]
 
 
-def panel_kernel(part_ref, out_ref, land, send_one, recv_one, send_sem, recv_sem):
+def panel_kernel(part_ref, out_ref, land, send_sem, recv_sem):
     slide, blk = lax.axis_index("slide"), lax.axis_index("blk")
     greet(slide, blk, BLK_PEERS + [(2, 0), (1, 0)])
-    copies = []
-    for far in range(1, 8):
-        target = flipped(blk, far)
-        copies.append(
-            pltpu.make_async_remote_copy(
-                src_ref=part_ref.at[target],
-                dst_ref=land.at[far],
-                send_sem=send_one.at[far],
-                recv_sem=recv_one.at[far],
-                device_id={"slide": slide, "blk": target},
-                device_id_type=MESH,
-            )
-        )
-        copies[-1].start()
+    links = Links(slide, blk, send_sem, recv_sem)
+    copies = [links.send(part_ref.at[flipped(blk, far)], land.at[far], 0, far) for far in range(1, 8)]
     total = part_ref[blk].astype(F32)
     for far in range(1, 8):
         copies[far - 1].wait_recv()
         total = total + land[far].astype(F32)
     out_ref[slide * 8 + blk] = total.astype(BF16)
-    gather_blocks(slide, blk, out_ref, send_sem, recv_sem)
-    for copy in copies:
-        copy.wait_send()
+    for _ in spread_everywhere(links, lambda far_slide, far_blk: out_ref.at[far_slide * 8 + far_blk]):
+        pass
+    links.finish()
 
 
 def panel_rows(part):
@@ -441,40 +387,14 @@
         out_specs=pl.BlockSpec(memory_space=pltpu.VMEM),
         scratch_shapes=[
             pltpu.VMEM((8, rows, width), BF16),
-            pltpu.SemaphoreType.DMA((8,)),
-            pltpu.SemaphoreType.DMA((8,)),
-            pltpu.SemaphoreType.DMA((32,)),
-            pltpu.SemaphoreType.DMA((32,)),
+            pltpu.SemaphoreType.DMA((38,)),
+            pltpu.SemaphoreType.DMA((38,)),
         ],
         compiler_params=pltpu.CompilerParams(
             collective_id=1, has_side_effects=True, vmem_limit_bytes=32 << 20
         ),
         name="panel_rows",
     )(part)
-
-
-def gather_kernel(block_ref, out_ref, send_sem, recv_sem):
-    slide, blk = lax.axis_index("slide"), lax.axis_index("blk")
-    greet(slide, blk, GATHER_PEERS)
-    out_ref[slide * 8 + blk] = block_ref[...]
-    gather_blocks(slide, blk, out_ref, send_sem, recv_sem)
-
-
-def gather_everywhere(block):
-    return pl.pallas_call(
-        gather_kernel,
-        out_shape=jax.ShapeDtypeStruct((32,) + block.shape, block.dtype),
-        in_specs=[pl.BlockSpec(memory_space=pltpu.VMEM)],
-        out_specs=pl.BlockSpec(memory_space=pltpu.VMEM),
-        scratch_shapes=[
-            pltpu.SemaphoreType.DMA((32,)),
-            pltpu.SemaphoreType.DMA((32,)),
-        ],
-        compiler_params=pltpu.CompilerParams(
-            collective_id=2, has_side_effects=True, vmem_limit_bytes=32 << 20
-        ),
-        name="gather_everywhere",
-    )(block)
 
 
 def exchange(slide, blk, peers, source_of, land, place, send_sem, recv_sem):
@@ -531,47 +451,6 @@
         compiler_params=pltpu.CompilerParams(collective_id=3, has_side_effects=True),
         name="sum_all",
     )(block)
-
-
-def sum_parts_kernel(in_ref, out_ref, land_one, land_two, own, send_one, recv_one, send_two, recv_two):
-    slide, blk = lax.axis_index("slide"), lax.axis_index("blk")
-    greet(slide, blk, SLIDE_PEERS + BLK_PEERS)
-    copies = exchange(
-        slide, blk, BLK_PEERS, lambda _, to_blk: in_ref.at[to_blk], land_one, blk, send_two, recv_two
-    )
-    land_one[blk] = in_ref[blk]
-    for copy in copies:
-        copy.wait()
-    total = land_one[0]
-    for place in range(1, 8):
-        total = total + land_one[place]
-    own[...] = total
-    copies = exchange(slide, blk, SLIDE_PEERS, lambda *_: own, land_two, slide, send_one, recv_one)
-    land_two[slide] = total
-    for copy in copies:
-        copy.wait()
-    out_ref[...] = (land_two[0] + land_two[1]) + (land_two[2] + land_two[3])
-
-
-def sum_parts(parts):
-    shape = parts.shape[1:]
-    return pl.pallas_call(
-        sum_parts_kernel,
-        out_shape=jax.ShapeDtypeStruct(shape, F32),
-        in_specs=[pl.BlockSpec(memory_space=pltpu.VMEM)],
-        out_specs=pl.BlockSpec(memory_space=pltpu.VMEM),
-        scratch_shapes=[
-            pltpu.VMEM((8,) + shape, F32),
-            pltpu.VMEM((4,) + shape, F32),
-            pltpu.VMEM(shape, F32),
-            pltpu.SemaphoreType.DMA((3,)),
-            pltpu.SemaphoreType.DMA((3,)),
-            pltpu.SemaphoreType.DMA((7,)),
-            pltpu.SemaphoreType.DMA((7,)),
-        ],
-        compiler_params=pltpu.CompilerParams(collective_id=4, has_side_effects=True),
-        name="sum_parts",
-    )(parts)
 
 
 def dot_nt(left, right):
@@ -625,64 +504,525 @@
     )(query, key, value, row_labels, col_labels)
 
 
-def attend_back_kernel(q_ref, g_ref, k_ref, v_ref, row_ref, col_ref, dq_ref, dk_ref, dv_ref, dk_sum, dv_sum):
-    step = pl.program_id(0)
-
-    @pl.when(step == 0)
-    def _():
-        dk_sum[...] = jnp.zeros_like(dk_sum)
-        dv_sum[...] = jnp.zeros_like(dv_sum)
-
+class Links:
+    def __init__(self, slide, blk, send_sem, recv_sem):
+        self.slide, self.blk = slide, blk
+        self.send_sem, self.recv_sem = send_sem, recv_sem
+        self.copies = []
+
+    def send(self, source, target, far_slide, far_blk):
+        number = len(self.copies)
+        copy = pltpu.make_async_remote_copy(
+            src_ref=source,
+            dst_ref=target,
+            send_sem=self.send_sem.at[number],
+            recv_sem=self.recv_sem.at[number],
+            device_id={
+                "slide": flipped(self.slide, far_slide),
+                "blk": flipped(self.blk, far_blk),
+            },
+            device_id_type=MESH,
+        )
+        copy.start()
+        self.copies.append(copy)
+        return copy
+
+    def finish(self):
+        for copy in self.copies:
+            copy.wait_send()
+
+
+def spread_everywhere(links, slot):
+    slide, blk = links.slide, links.blk
+    copies = {}
+
+    def push(rel_slide, rel_blk, to_slide, to_blk):
+        block = slot(flipped(slide, rel_slide), flipped(blk, rel_blk))
+        copies[(rel_slide ^ to_slide, rel_blk ^ to_blk)] = links.send(block, block, to_slide, to_blk)
+
+    for far in (2, 4, 6):
+        push(0, 0, 0, far)
+    push(0, 0, 0, 1)
+    push(0, 0, 2, 0)
+    push(0, 0, 1, 0)
+    yield
+    for rel in (2, 4, 6):
+        copies[0, rel].wait_recv()
+        push(0, rel, 0, 1)
+        push(0, rel, 2, 0)
+        push(0, rel, 1, 0)
+    yield
+    for rel in (1, 3, 5, 7):
+        copies[0, rel].wait_recv()
+        push(0, rel, 2, 0)
+        push(0, rel, 1, 0)
+    yield
+    for rel in (0, 2, 4, 6, 1, 3, 5, 7):
+        copies[2, rel].wait_recv()
+        push(2, rel, 1, 0)
+    yield
+    for far in (1, 3):
+        for rel in (0, 2, 4, 6, 1, 3, 5, 7):
+            copies[far, rel].wait_recv()
+    yield
+
+
+class Reduction:
+    def __init__(self, links, left, right, rows, width, dense, buffers):
+        self.links, self.left, self.right = links, left, right
+        self.rows, self.width, self.dense = rows, width, dense
+        self.away, self.came, self.kept, self.pieces = buffers
+        self.along_x, self.along_z = links.blk % 2, links.blk // 2
+
+    def tiles(self, which, store):
+        def tile(i, carry):
+            place = which * 2 + i if self.dense else i * 2 + which
+            product = dot_tn(self.left(pl.multiple_of(place * 128, 128)), self.right())
+            store(pl.ds(pl.multiple_of(i * 128, 128), 128), product)
+            return carry
+
+        lax.fori_loop(0, self.rows * 4 // 128, tile, 0)
+
+    def send_x(self):
+        def store(where, product):
+            self.away[where, :] = product.astype(BF16)
+
+        self.tiles(1 - self.along_x, store)
+        self.copy_x = self.links.send(self.away, self.came, 0, 1)
+
+    def send_z(self):
+        self.copy_x.wait_recv()
+
+        def store(where, product):
+            self.kept[where, :] = (product + self.came[where, :].astype(F32)).astype(BF16)
+
+        self.tiles(self.along_x, store)
+        self.copies_z = []
+        for far in (2, 1, 3):
+            target = pl.multiple_of(flipped(self.along_z, far) * self.rows, self.rows)
+            self.copies_z.append(
+                self.links.send(self.kept.at[pl.ds(target, self.rows)], self.pieces.at[far - 1], 0, 2 * far)
+            )
+
+    def total(self):
+        for copy in self.copies_z:
+            copy.wait_recv()
+        own = self.kept[pl.ds(pl.multiple_of(self.along_z * self.rows, self.rows), self.rows), :]
+        return (
+            (own.astype(F32) + self.pieces[0].astype(F32))
+            + (self.pieces[1].astype(F32) + self.pieces[2].astype(F32))
+        ).astype(BF16)
+
+
+def spread_slide(links, slot, total):
+    slide = links.slide
+    own, far = slot(slide), slot(flipped(slide, 2))
+    own[...] = total
+    across = links.send(own, own, 2, 0)
+    beside = links.send(own, own, 1, 0)
+    yield
+    across.wait_recv()
+    last = links.send(far, far, 1, 0)
+    yield
+    beside.wait_recv()
+    last.wait_recv()
+    yield
+
+
+def reductions_of(cells, width, inner, latents):
+    return [
+        ("decoder", latents // 8, width // 4, True),
+        ("down0", inner // 32, width // 2, False),
+        ("down1", inner // 32, width // 2, False),
+        ("mean", width // 8, latents // 4, False),
+        ("logvar", width // 8, latents // 4, False),
+        ("hidden0", width // 8, inner // 8, False),
+        ("hidden1", width // 8, inner // 8, False),
+        ("output", width // 8, width // 4, False),
+        ("panel", width // 8, width // 4, False),
+        ("query", width // 8, width // 4, False),
+        ("key", width // 8, width // 4, False),
+        ("value", width // 8, width // 4, False),
+    ]
+
+
+def backward_kernel(
+    q_ref, k_ref, v_ref, row_ref, col_ref, branch_ref, gmean_ref, glogvar_ref, ginner_ref, gout_ref,
+    middle_ref, start_ref, gain_ref, small_ref,
+    whole0, whole1, whole2, whole3, quarter0, quarter1, quarter2, quarter3, wq_hbm, wk_hbm, wv_hbm, wo_hbm,
+    panel_out, query_out, key_out, value_out, output_out, hidden_out, down_out, mean_out, logvar_out, decoder_out, small_out,
+    whole, quarter, wq, wk, wv, wo, branch_all, gmean_all, glogvar_all, ginner_all, gout_all, gqkv_all, genc_all,
+    att_send, att_land, dqkv, dqkv_land, dk_sum, dv_sum, grad_qkv, encoded, small, small_land, small_own, small_slides,
+    load_sem, send_sem, recv_sem, *unit_refs,
+):
+    slide, blk = lax.axis_index("slide"), lax.axis_index("blk")
+    cells, width = middle_ref.shape
+    inner, latents, per = ginner_ref.shape[1], gmean_ref.shape[1], width // 8
+    loads = {}
+    for number, (name, source, target) in enumerate(
+        [("wo", wo_hbm, wo)]
+        + [("q%d" % i, ref, quarter.at[pl.ds(i * cells, cells)]) for i, ref in enumerate((quarter0, quarter1, quarter2, quarter3))]
+        + [("w%d" % i, ref, whole.at[pl.ds(i * cells, cells)]) for i, ref in enumerate((whole0, whole1, whole2, whole3))]
+        + [("wq", wq_hbm, wq), ("wk", wk_hbm, wk), ("wv", wv_hbm, wv)]
+    ):
+        loads[name] = pltpu.make_async_copy(source, target, load_sem.at[number])
+        loads[name].start()
+    greet(slide, blk, SLIDE_PEERS + BLK_PEERS)
+    links = Links(slide, blk, send_sem, recv_sem)
+
+    def lanes(ref, which, size):
+        return ref.at[:, pl.ds(pl.multiple_of(which * size, 128), size)]
+
+    def swap(ref, size, target):
+        copies = []
+        for far in (2, 3, 1):
+            copies.append(links.send(lanes(ref, flipped(slide, far), size), target.at[far], far, 0))
+        target[0] = lanes(ref, slide, size)[...]
+        return copies
+
+    branch_far = links.send(branch_ref, branch_all.at[2], 2, 0)
+    branch_near = links.send(branch_ref, branch_all.at[1], 1, 0)
+    branch_all[0] = branch_ref[...]
+    mean_swap = swap(gmean_ref, latents // 4, gmean_all)
+    logvar_swap = swap(glogvar_ref, latents // 4, glogvar_all)
+    inner_swap = swap(ginner_ref, inner // 4, ginner_all)
+    out_swap = swap(gout_ref, width // 4, gout_all)
+
+    loads["wo"].wait()
+
+    def att_block(target, store):
+        rows = wo[pl.ds(pl.multiple_of(target * per, per), per), :]
+        store(dot_nt(gout_ref[...], rows).astype(BF16))
+
+    att_copies = []
+    for far in (6, 4, 2, 7, 5, 3, 1):
+        target = flipped(blk, far)
+
+        def keep(block, far=far):
+            att_send[far] = block
+
+        att_block(target, keep)
+        att_copies.append(links.send(att_send.at[far], att_land.at[blk], 0, far))
+
+    def keep_own(block):
+        att_land[blk] = block
+
+    att_block(blk, keep_own)
+
+    width_at = {"express": 0, "one": width, "attended": 2 * width, "two": 3 * width, "base": 4 * width, "latent": 5 * width}
+
+    def of_whole(name):
+        def left(column):
+            return whole[:, pl.ds(width_at[name] + column, 128)]
+
+        return left
+
+    def of_act(column):
+        return quarter[:, pl.ds(column, 128)]
+
+    def flat(ref, start=None, size=None):
+        def right():
+            block = ref[...] if start is None else ref[:, :, start : start + size]
+            return block.reshape(4 * cells, block.shape[-1])
+
+        return right
+
+    def source_all():
+        return quarter[:, inner // 4 :]
+
+    half_w, half_i = width // 2, inner // 8
+    operands = {
+        "decoder": (of_whole("latent"), source_all),
+        "down0": (of_act, flat(branch_all, 0, half_w)),
+        "down1": (of_act, flat(branch_all, half_w, half_w)),
+        "mean": (of_whole("base"), flat(gmean_all)),
+        "logvar": (of_whole("base"), flat(glogvar_all)),
+        "hidden0": (of_whole("two"), flat(ginner_all, 0, half_i)),
+        "hidden1": (of_whole("two"), flat(ginner_all, half_i, half_i)),
+        "output": (of_whole("attended"), flat(gout_all)),
+        "panel": (of_whole("express"), flat(genc_all)),
+        "query": (of_whole("one"), flat(gqkv_all.at[0])),
+        "key": (of_whole("one"), flat(gqkv_all.at[1])),
+        "value": (of_whole("one"), flat(gqkv_all.at[2])),
+    }
+    units = {}
+    for number, (name, rows, columns, dense) in enumerate(reductions_of(cells, width, inner, latents)):
+        left, right = operands[name]
+        units[name] = Reduction(
+            links, left, right, rows, columns, dense, unit_refs[4 * number : 4 * number + 4]
+        )
+
+    def columns_slot(ref, size, offset=0):
+        return lambda place: ref.at[:, pl.ds(pl.multiple_of(place * size + offset, 128), size if not offset else size)]
+
+    slots = {
+        "decoder": lambda place: lanes(decoder_out, place, width // 4),
+        "down0": lambda place: down_out.at[pl.ds(pl.multiple_of(place * (inner // 32), inner // 32), inner // 32), pl.ds(0, half_w)],
+        "down1": lambda place: down_out.at[pl.ds(pl.multiple_of(place * (inner // 32), inner // 32), inner // 32), pl.ds(half_w, half_w)],
+        "mean": lambda place: lanes(mean_out, place, latents // 4),
+        "logvar": lambda place: lanes(logvar_out, place, latents // 4),
+        "hidden0": lambda place: hidden_out.at[:, pl.ds(pl.multiple_of(place * (inner // 4), 128), half_i)],
+        "hidden1": lambda place: hidden_out.at[:, pl.ds(pl.multiple_of(place * (inner // 4) + half_i, 128), half_i)],
+        "output": lambda place: lanes(output_out, place, width // 4),
+        "query": lambda place: lanes(query_out, place, width // 4),
+        "key": lambda place: lanes(key_out, place, width // 4),
+        "value": lambda place: lanes(value_out, place, width // 4),
+    }
+    spreads = {}
+
+    def spread(name):
+        spreads[name] = spread_slide(links, slots[name], units[name].total())
+        next(spreads[name])
+
+    for i in range(4):
+        loads["q%d" % i].wait()
+    for i in range(4):
+        loads["w%d" % i].wait()
+    units["decoder"].send_x()
+    branch_far.wait_recv()
+    branch_last = links.send(branch_all.at[2], branch_all.at[3], 1, 0)
+    branch_near.wait_recv()
+    branch_last.wait_recv()
+    units["down0"].send_x()
+    units["down1"].send_x()
+    for copy in mean_swap + logvar_swap:
+        copy.wait_recv()
+    units["mean"].send_x()
+    units["logvar"].send_x()
+
+    for copy in att_copies:
+        copy.wait_recv()
+    dk_sum[...] = jnp.zeros_like(dk_sum)
+    dv_sum[...] = jnp.zeros_like(dv_sum)
     scale = HEAD_DIM**-0.5
-    same_slide = row_ref[...] == col_ref[...]
-    lanes = lax.broadcasted_iota(jnp.int32, q_ref.shape, 1)
-    query, grad, key, value = q_ref[...], g_ref[...], k_ref[...], v_ref[...]
-    grad_query = None
-    for head in range(q_ref.shape[1] // HEAD_DIM):
-        mine = lanes // HEAD_DIM == head
-        own_query = jnp.where(mine, query, 0)
-        own_grad = jnp.where(mine, grad, 0)
-        shares = head_scores(own_query, key, same_slide)
-        grad_shares = dot_nt(own_grad, value)
-        inner = jnp.sum(shares * grad_shares, axis=1, keepdims=True)
-        grad_scores = (shares * (grad_shares - inner)).astype(BF16)
-        part = jnp.dot(grad_scores, key, preferred_element_type=F32)
-        grad_query = part if grad_query is None else jnp.where(mine, part, grad_query)
-        dk_sum[...] += dot_tn(grad_scores, own_query)
-        dv_sum[...] += dot_tn(shares.astype(BF16), own_grad)
-    dq_ref[...] = (grad_query * scale).astype(BF16)
-
-    @pl.when(step == pl.num_programs(0) - 1)
-    def _():
-        dk_ref[...] = (dk_sum[...] * scale).astype(BF16)
-        dv_ref[...] = dv_sum[...].astype(BF16)
-
-
-def attend_back(query, grad, key, value, row_labels, col_labels, rows=256):
-    count, width = query.shape
-    whole = pl.BlockSpec((count, width), lambda i: (0, 0))
-    part = pl.BlockSpec((rows, width), lambda i: (i, 0))
-    shape = jax.ShapeDtypeStruct((count, width), BF16)
+    rows = 2 * cells
+
+    def rows_back(i, carry):
+        where = pl.ds(pl.multiple_of(i * rows, rows), rows)
+        same_slide = row_ref[where, :] == col_ref[...]
+        query = q_ref[where, :]
+        grad = att_land[pl.ds(2 * i, 2)].reshape(rows, per)
+        key, value = k_ref[...], v_ref[...]
+        lane = lax.broadcasted_iota(jnp.int32, query.shape, 1)
+        grad_query = None
+        for head in range(per // HEAD_DIM):
+            mine = lane // HEAD_DIM == head
+            own_query = jnp.where(mine, query, 0)
+            own_grad = jnp.where(mine, grad, 0)
+            shares = head_scores(own_query, key, same_slide)
+            grad_shares = dot_nt(own_grad, value)
+            inner_dot = jnp.sum(shares * grad_shares, axis=1, keepdims=True)
+            grad_scores = (shares * (grad_shares - inner_dot)).astype(BF16)
+            part = jnp.dot(grad_scores, key, preferred_element_type=F32)
+            grad_query = part if grad_query is None else jnp.where(mine, part, grad_query)
+            dk_sum[...] += dot_tn(grad_scores, own_query)
+            dv_sum[...] += dot_tn(shares.astype(BF16), own_grad)
+        dqkv[pl.ds(2 * i, 2), 0:cells, :] = (grad_query * scale).astype(BF16).reshape(2, cells, per)
+        return carry
+
+    lax.fori_loop(0, 8 * cells // rows, rows_back, 0)
+    dqkv[:, cells : 2 * cells, :] = (dk_sum[...] * scale).astype(BF16).reshape(8, cells, per)
+    dqkv[:, 2 * cells :, :] = dv_sum[...].astype(BF16).reshape(8, cells, per)
+    back_copies = []
+    for far in (6, 4, 2, 7, 5, 3, 1):
+        back_copies.append(links.send(dqkv.at[flipped(blk, far)], dqkv_land.at[blk], 0, far))
+    dqkv_land[blk] = dqkv[blk]
+
+    for copy in inner_swap + out_swap:
+        copy.wait_recv()
+    units["hidden0"].send_x()
+    units["hidden1"].send_x()
+    units["output"].send_x()
+    units["decoder"].send_z()
+    units["down0"].send_z()
+
+    for copy in back_copies:
+        copy.wait_recv()
+    for name in ("wq", "wk", "wv"):
+        loads[name].wait()
+    for part in range(3):
+        for block in range(8):
+            grad_qkv[part, :, block * per : (block + 1) * per] = dqkv_land[block, part * cells : (part + 1) * cells, :]
+    qkv_swaps = [swap(grad_qkv.at[part], width // 4, gqkv_all.at[part]) for part in range(3)]
+
+    def norm_input(i, carry):
+        where = pl.ds(pl.multiple_of(i * 256, 256), 256)
+        encoded_sum = (
+            dot_nt(grad_qkv[0], wq[where, :]) + dot_nt(grad_qkv[1], wk[where, :]) + dot_nt(grad_qkv[2], wv[where, :])
+        )
+        encoded[:, where] = encoded_sum
+        return carry
+
+    lax.fori_loop(0, width // 256, norm_input, 0)
+    hidden = start_ref[...]
+    centre = hidden - jnp.mean(hidden, axis=1, keepdims=True)
+    invert = lax.rsqrt(jnp.mean(centre * centre, axis=1, keepdims=True) + 1e-05)
+    unit = centre * invert
+    grad_normed = encoded[...]
+    gain_grad = jnp.sum(grad_normed * unit, axis=0, keepdims=True)
+    shift_grad = jnp.sum(grad_normed, axis=0, keepdims=True)
+    grad_unit = grad_normed * gain_ref[...]
+    grad_hidden = invert * (
+        grad_unit
+        - jnp.mean(grad_unit, axis=1, keepdims=True)
+        - unit * jnp.mean(grad_unit * unit, axis=1, keepdims=True)
+    )
+    grad_qkv[3] = (middle_ref[...] + grad_hidden).astype(BF16)
+    encoded_swap = swap(grad_qkv.at[3], width // 4, genc_all)
+
+    small[...] = small_ref[...]
+    for block in range(8):
+        small[block, 0:1, :] = gain_grad[:, block * 128 : (block + 1) * 128]
+        small[block, 1:2, :] = shift_grad[:, block * 128 : (block + 1) * 128]
+    small_copies = [links.send(small.at[flipped(blk, far)], small_land.at[blk], 0, far) for far in range(1, 8)]
+    small_land[blk] = small[blk]
+
+    units["down1"].send_z()
+    for copy in encoded_swap:
+        copy.wait_recv()
+    units["panel"].send_x()
+    for part in range(3):
+        for copy in qkv_swaps[part]:
+            copy.wait_recv()
+        units[("query", "key", "value")[part]].send_x()
+    for copy in small_copies:
+        copy.wait_recv()
+    small_sum = small_land[0]
+    for block in range(1, 8):
+        small_sum = small_sum + small_land[block]
+    small_own[...] = small_sum
+    small_copies = [links.send(small_own, small_slides.at[slide], far, 0) for far in (2, 3, 1)]
+    small_slides[slide] = small_sum
+    units["mean"].send_z()
+    units["logvar"].send_z()
+    units["panel"].send_z()
+    units["hidden0"].send_z()
+    spread("decoder")
+    spread("down0")
+    spread("down1")
+
+    panel_slot = lambda far_slide, far_blk: panel_out.at[
+        pl.ds(pl.multiple_of(far_blk * (width // 8), 128), width // 8),
+        pl.ds(pl.multiple_of(far_slide * (width // 4), 128), width // 4),
+    ]
+    own_slot = panel_slot(slide, blk)
+    own_slot[...] = units["panel"].total()
+    everywhere = spread_everywhere(links, panel_slot)
+    next(everywhere)
+    units["hidden1"].send_z()
+    units["output"].send_z()
+    next(everywhere)
+    units["query"].send_z()
+    units["key"].send_z()
+    units["value"].send_z()
+    next(everywhere)
+    spread("mean")
+    spread("logvar")
+    spread("hidden0")
+    spread("hidden1")
+    next(everywhere)
+    spread("output")
+    spread("query")
+    spread("key")
+    spread("value")
+    for name in spreads:
+        next(spreads[name])
+    for copy in small_copies:
+        copy.wait_recv()
+    small_out[...] = (small_slides[0] + small_slides[1]) + (small_slides[2] + small_slides[3])
+    next(everywhere)
+    for name in spreads:
+        next(spreads[name])
+    links.finish()
+
+
+def backward(inputs, pieces, weights, cells, width, inner, latents, small_rows):
+    per = width // 8
+    shape = jax.ShapeDtypeStruct
+    unit_scratch = []
+    for _, rows, columns, _ in reductions_of(cells, width, inner, latents):
+        unit_scratch += [pltpu.VMEM((4 * rows, columns), BF16)] * 3 + [pltpu.VMEM((3, rows, columns), BF16)]
+    copies = 208
+    vmem, left = pl.BlockSpec(memory_space=pltpu.VMEM), pl.BlockSpec(memory_space=pl.ANY)
+    outs = (
+        shape((width, width), BF16),
+        shape((per, width), BF16),
+        shape((per, width), BF16),
+        shape((per, width), BF16),
+        shape((per, width), BF16),
+        shape((per, inner), BF16),
+        shape((inner // 8, width), BF16),
+        shape((per, latents), BF16),
+        shape((per, latents), BF16),
+        shape((latents // 8, width), BF16),
+        shape((small_rows, 128), F32),
+    )
     return pl.pallas_call(
-        attend_back_kernel,
-        grid=(count // rows,),
-        out_shape=(shape, shape, shape),
+        backward_kernel,
+        out_shape=outs,
+        in_specs=[vmem] * len(inputs) + [left] * (len(pieces) + len(weights)),
+        out_specs=[vmem] * len(outs),
+        scratch_shapes=[
+            pltpu.VMEM((4 * cells, 5 * width + latents), BF16),
+            pltpu.VMEM((4 * cells, inner // 4 + width // 4), BF16),
+            pltpu.VMEM((width, width), BF16),
+            pltpu.VMEM((width, width), BF16),
+            pltpu.VMEM((width, width), BF16),
+            pltpu.VMEM((width, width), BF16),
+            pltpu.VMEM((4, cells, width), BF16),
+            pltpu.VMEM((4, cells, latents // 4), BF16),
+            pltpu.VMEM((4, cells, latents // 4), BF16),
+            pltpu.VMEM((4, cells, inner // 4), BF16),
+            pltpu.VMEM((4, cells, width // 4), BF16),
+            pltpu.VMEM((3, 4, cells, width // 4), BF16),
+            pltpu.VMEM((4, cells, width // 4), BF16),
+            pltpu.VMEM((8, cells, per), BF16),
+            pltpu.VMEM((8, cells, per), BF16),
+            pltpu.VMEM((8, 3 * cells, per), BF16),
+            pltpu.VMEM((8, 3 * cells, per), BF16),
+            pltpu.VMEM((8 * cells, per), F32),
+            pltpu.VMEM((8 * cells, per), F32),
+            pltpu.VMEM((4, cells, width), BF16),
+            pltpu.VMEM((cells, width), F32),
+            pltpu.VMEM((8, small_rows, 128), F32),
+            pltpu.VMEM((8, small_rows, 128), F32),
+            pltpu.VMEM((small_rows, 128), F32),
+            pltpu.VMEM((4, small_rows, 128), F32),
+            pltpu.SemaphoreType.DMA((12,)),
+            pltpu.SemaphoreType.DMA((copies,)),
+            pltpu.SemaphoreType.DMA((copies,)),
+        ]
+        + unit_scratch,
+        compiler_params=pltpu.CompilerParams(
+            collective_id=5, has_side_effects=True, vmem_limit_bytes=60 << 20
+        ),
+        name="backward",
+    )(*inputs, *pieces, *weights)
+
+
+def table_kernel(first_ref, ids_ref, panel_ref, out_ref):
+    rows = out_ref.shape[0]
+    first = first_ref[0] + pl.program_id(0) * rows
+    row_ids = first + lax.broadcasted_iota(jnp.int32, (rows, ids_ref.shape[1]), 0)
+    spread = (row_ids == ids_ref[...]).astype(F32).astype(BF16)
+    out_ref[...] = jnp.dot(spread, panel_ref[...], preferred_element_type=F32)
+
+
+def table_rows_grad(first_row, gene_ids, panel, table_rows, rows=256):
+    genes, width = panel.shape
+    return pl.pallas_call(
+        table_kernel,
+        grid=(table_rows // rows,),
+        out_shape=jax.ShapeDtypeStruct((table_rows, width), F32),
         in_specs=[
-            part,
-            part,
-            whole,
-            whole,
-            pl.BlockSpec((rows, 1), lambda i: (i, 0)),
-            pl.BlockSpec((1, count), lambda i: (0, 0)),
+            pl.BlockSpec(memory_space=pltpu.SMEM),
+            pl.BlockSpec((1, genes), lambda i: (0, 0)),
+            pl.BlockSpec((genes, width), lambda i: (0, 0)),
         ],
-        out_specs=(part, whole, whole),
-        scratch_shapes=[pltpu.VMEM((count, width), F32), pltpu.VMEM((count, width), F32)],
-        compiler_params=pltpu.CompilerParams(vmem_limit_bytes=48 << 20),
-        cost_estimate=pl.CostEstimate(
-            flops=20 * count * count * width, bytes_accessed=14 * count * width, transcendentals=0
-        ),
-        name="attend_back",
-    )(query, grad, key, value, row_labels, col_labels)
+        out_specs=pl.BlockSpec((rows, width), lambda i: (i, 0)),
+        compiler_params=pltpu.CompilerParams(vmem_limit_bytes=40 << 20),
+        name="table_rows_grad",
+    )(first_row.reshape(1), gene_ids.reshape(1, genes), panel)
 
 
 def over_slide(array, mask):
@@ -700,36 +1040,6 @@
 
 def swap_slide(pick, slide):
     return [pick(slide)] + [over_slide(pick(jnp.bitwise_xor(slide, far)), far) for far in (1, 2, 3)]
-
-
-def in_order(parts, index):
-    low = jnp.bitwise_and(index, 1) == 1
-    high = jnp.bitwise_and(index, 2) == 2
-    one = [jnp.where(low, parts[j ^ 1], parts[j]) for j in range(4)]
-    return [jnp.where(high, one[j ^ 2], one[j]) for j in range(4)]
-
-
-def reduce_blk(left, right, blk):
-    cells, total_rows = left.shape
-    rows = total_rows // 8
-    shaped = left.reshape(cells, 4, 2, rows)
-    along_x = blk % 2
-    along_z = blk // 2
-
-    def half(which):
-        columns = lax.dynamic_index_in_dim(shaped, which, 2, keepdims=False).reshape(cells, 4 * rows)
-        return dot_tn(columns, right)
-
-    away = over_blk(half(1 - along_x).astype(BF16), 1)
-    kept = (half(along_x) + away.astype(F32)).astype(BF16).reshape(4, rows, right.shape[1])
-
-    def piece(which):
-        return lax.dynamic_index_in_dim(kept, which, 0, keepdims=False)
-
-    total = piece(along_z).astype(F32)
-    for far in (1, 2, 3):
-        total = total + over_blk(piece(jnp.bitwise_xor(along_z, far)), 2 * far).astype(F32)
-    return total.astype(BF16)
 
 
 def on_device_fast(
@@ -832,20 +1142,17 @@
     binding = (kl_mean > free_floor).astype(F32)
     grad_source = decoded_grad[0]
 
-    whole_fwd = jnp.concatenate([express, normed_one, attended, normed_two, base_low, latent_low], axis=1)
-    whole_fwd = jnp.concatenate(gather_slide(whole_fwd), axis=0)
-    express_all, normed_one_all, attended_all, normed_two_all, base_all = [
-        whole_fwd[:, i * width : (i + 1) * width] for i in range(5)
-    ]
-    latent_all = whole_fwd[:, 5 * width :]
+    latent_turned = latent_low.reshape(cells, 4, 2, latents // 8).transpose(0, 2, 1, 3).reshape(cells, latents)
+    whole_fwd = gather_slide(
+        jnp.concatenate([express, normed_one, attended, normed_two, base_low, latent_turned], axis=1)
+    )
     act_parts = act_low.reshape(cells, 8, 4, inner // 32)
 
     def pick_fwd(which):
         act = lax.dynamic_index_in_dim(act_parts, which, 2, keepdims=False).reshape(cells, inner // 4)
         return jnp.concatenate([act, columns(grad_source, which * (genes // 4), genes // 4)], axis=1)
 
-    quarter_fwd = jnp.concatenate(swap_slide(pick_fwd, slide), axis=0)
-    act_all, source_all = quarter_fwd[:, : inner // 4], quarter_fwd[:, inner // 4 :]
+    quarter_fwd = swap_slide(pick_fwd, slide)
 
     grad_latent = matmul(grad_source, decoder_weight.T)
     grad_kl = jnp.broadcast_to(divergence_weight * binding, kl_cell.shape)
@@ -855,23 +1162,6 @@
     grad_final = matmul(grad_mean_low, mean_weight.T) + matmul(grad_logvar_low, logvar_weight.T)
     grad_branch = grad_final.astype(BF16)
     down_bias_grad = jnp.sum(grad_branch.astype(F32), axis=0)
-    branch_all = jnp.concatenate(gather_slide(grad_branch), axis=0)
-    lat_quarter = latents // 4
-
-    def pick_lat(which):
-        return jnp.concatenate(
-            [
-                columns(grad_mean_low, which * lat_quarter, lat_quarter),
-                columns(grad_logvar_low, which * lat_quarter, lat_quarter),
-            ],
-            axis=1,
-        )
-
-    lat_all = jnp.concatenate(swap_slide(pick_lat, slide), axis=0)
-    down_sum = reduce_blk(act_all, branch_all, blk)
-    lat_sum = reduce_blk(base_all, lat_all, blk)
-    decoder_sum = reduce_blk(latent_all, source_all, blk)
-
     grad_act = matmul(grad_branch, down_weight.T)
     gelu_pull = jax.vjp(gelu_tanh, inner_sum)[1]
     grad_inner = gelu_pull(grad_act)[0].astype(BF16)
@@ -880,53 +1170,12 @@
     grad_norm_two, second_gain_grad, second_shift_grad = norm_two_pull(matmul(grad_inner, hidden_weight.T))
     grad_middle = grad_final + grad_norm_two
     grad_out = grad_middle.astype(BF16)
-    inner_all = jnp.concatenate(
-        swap_slide(lambda which: columns(grad_inner, which * (inner // 4), inner // 4), slide), axis=0
-    )
-    hidden_sum = reduce_blk(normed_two_all, inner_all, blk)
-    out_all = jnp.concatenate(
-        swap_slide(lambda which: columns(grad_out, which * (width // 4), width // 4), slide), axis=0
-    )
-    output_sum = reduce_blk(attended_all, out_all, blk)
-
-    grad_attended = matmul(grad_out, output_weight.T).astype(BF16)
-    grad_heads = lax.all_to_all(to_blocks(grad_attended), "blk", 0, 0).reshape(8 * cells, per)
-    grads = attend_back(query, grad_heads, key, value, row_labels, col_labels)
-    grads = jnp.concatenate([grad.reshape(8, cells, per) for grad in grads], axis=1)
-    grads = lax.all_to_all(grads, "blk", 0, 0)
-    grad_query, grad_key, grad_value = [
-        from_blocks(grads[:, i * cells : (i + 1) * cells]) for i in range(3)
-    ]
-    grad_norm_input = (
-        matmul(grad_query, query_weight.T) + matmul(grad_key, key_weight.T) + matmul(grad_value, value_weight.T)
-    )
-    norm_one_pull = jax.vjp(layer_norm, hidden_start, first_gain, first_shift)[1]
-    grad_norm_one, first_gain_grad, first_shift_grad = norm_one_pull(grad_norm_input)
-    grad_encoded = (grad_middle + grad_norm_one).astype(BF16)
-    quarter = width // 4
-
-    def pick_qkv(which):
-        return jnp.concatenate(
-            [columns(grad, which * quarter, quarter) for grad in (grad_query, grad_key, grad_value)], axis=1
-        )
-
-    qkv_all = jnp.concatenate(swap_slide(pick_qkv, slide), axis=0)
-    encoded_all = jnp.concatenate(
-        swap_slide(lambda which: columns(grad_encoded, which * quarter, quarter), slide), axis=0
-    )
-    panel_sum = reduce_blk(express_all, encoded_all, blk)
-    qkv_sum = reduce_blk(normed_one_all, qkv_all, blk)
-
-    panel_all = gather_everywhere(panel_sum).reshape(4, genes, quarter)
-    spread = (row_ids[:, None] == gene_ids[None, :]).astype(BF16)
-    table_grad = jnp.concatenate([matmul(spread, panel_all[i]) for i in range(4)], axis=1)
 
     small = jnp.concatenate(
-        [
+        [jnp.zeros((8, 2, 128), F32)]
+        + [
             item.reshape(8, -1, 128)
             for item in (
-                first_gain_grad,
-                first_shift_grad,
                 second_gain_grad,
                 second_shift_grad,
                 hidden_bias_grad,
@@ -937,51 +1186,44 @@
         axis=1,
     )
     count = small.shape[1]
-    small = sum_parts(jnp.pad(small, ((0, 0), (0, -count % 8), (0, 0))))
+    small = jnp.pad(small, ((0, 0), (0, -count % 8), (0, 0)))
+    (
+        panel_sum, query_grad, key_grad, value_grad, output_grad, hidden_grad, down_grad, mean_grad, logvar_grad,
+        decoder_grad, small,
+    ) = backward(
+        (
+            query, key, value, row_labels, col_labels, grad_branch, grad_mean_low, grad_logvar_low, grad_inner, grad_out,
+            grad_middle, hidden_start, first_gain[None], small,
+        ),
+        tuple(whole_fwd) + tuple(quarter_fwd),
+        (query_weight, key_weight, value_weight, output_weight),
+        cells, width, inner, latents, small.shape[1],
+    )
+    table_grad = table_rows_grad(first_row, gene_ids, panel_sum, table_rows)
     bias_rows = inner // 8 // 128
-    small_gain_one, small_shift_one, small_gain_two, small_shift_two = [
-        small[i] for i in range(4)
-    ]
     small_hidden = small[4 : 4 + bias_rows].reshape(-1)
     small_down = small[4 + bias_rows]
     small_centres = small[5 + bias_rows : count].reshape(16, -1)
-
-    def wide(total):
-        return jnp.concatenate(in_order([p.astype(F32) for p in gather_slide(total)], slide), axis=1)
-
-    def tall(total):
-        return jnp.concatenate(in_order([p.astype(F32) for p in gather_slide(total)], slide), axis=0)
-
-    def split(total, sizes):
-        parts = in_order([p.astype(F32) for p in gather_slide(total)], slide)
-        outs, start = [], 0
-        for size in sizes:
-            outs.append(jnp.concatenate([p[:, start : start + size] for p in parts], axis=1))
-            start += size
-        return outs
-
-    query_grad, key_grad, value_grad = split(qkv_sum, [quarter] * 3)
-    mean_grad, logvar_grad = split(lat_sum, [lat_quarter] * 2)
     return (
         decoded[None],
         divergence,
         table_grad,
-        small_gain_one,
-        small_shift_one,
-        query_grad,
-        key_grad,
-        value_grad,
-        wide(output_sum),
-        small_gain_two,
-        small_shift_two,
-        wide(hidden_sum),
+        small[0],
+        small[1],
+        query_grad.astype(F32),
+        key_grad.astype(F32),
+        value_grad.astype(F32),
+        output_grad.astype(F32),
+        small[2],
+        small[3],
+        hidden_grad.astype(F32),
         small_hidden,
-        tall(down_sum),
+        down_grad.astype(F32),
         small_down,
-        mean_grad,
-        logvar_grad,
+        mean_grad.astype(F32),
+        logvar_grad.astype(F32),
         small_centres,
-        wide(decoder_sum),
+        decoder_grad.astype(F32),
     )
 
 

time: 564 us -> 357 us (0.63)
  the two profiles are of different devices: /device:TPU:13 before, /device:TPU:1 now
where the time goes in v2:
time: 357 us; the launch traced here: 351 us
  Pallas kernels  216 us (61%)
  matrix products  38.4 us (11%)
  local copies, waits for them, and re-layouts  25.3 us (7%)
  blocking collectives  24.5 us (7%)
  other arithmetic  18.4 us (5%)
  waiting for transfers between devices  11.9 us (3%)
  starting transfers between devices  11.6 us (3%)
  between operations  4.49 us (1%)
    pallas_call x1, Pallas kernels, backward(): pl.pallas_call(backward_kernel, out_shape=outs, in_specs=[vmem] * len(inp...  156 us
    dot_general x16, matrix products, matmul(): return jnp.dot(left, right, preferred_element_type=jnp.float32)  34.7 us
    pallas_call x1, Pallas kernels, panel_rows(): pl.pallas_call(panel_kernel, out_shape=jax.ShapeDtypeStruct((32, rows, wi...  34.1 us
    all_to_all x1, blocking collectives, on_device_fast(): qkv = lax.all_to_all(qkv, 'blk', 0, 0)  24.5 us
    pallas_call x1, Pallas kernels, sum_all(): pl.pallas_call(sum_all_kernel, out_shape=jax.ShapeDtypeStruct(block.shape...  11.9 us
    ppermute x6, starting transfers between devices, over_slide(): lax.ppermute(array, 'slide', [(place, place ^ mask) for place in range(4)])  7.8 us
    pallas_call x1, Pallas kernels, table_rows_grad(): pl.pallas_call(table_kernel, grid=(table_rows // rows,), out_shape=jax.Sh...  7.46 us
  transfers between devices with their start and end apart: 7, of which 3 were waited for; matrix products, arithmetic and copies ran while one was open for 9% of the time, Pallas kernels for 0%

profile of v2, /device:TPU:1, one launch (start us, length us, event | category | flops | bytes accessed | tf_op | source)
XLA Modules:
  0.0 350.8 jit_solution(90422151204635789)
XLA Ops:
  1.6 3.5 fusion.8
  5.1 34.1 %panel_rows.1 = bf16[32,32,1024]{2,1,0:T(8,128)(2,1)S(1)} custom-call(bf16[8,32,1024]{2,1,0:T(8,128)(2,1)S(1)} %bitcast.186), custom_call_target="tpu_custom_call" | custom-call | tf_op jit(solution)/shard_map/panel_rows/pallas_call | solution.py:383
  45.4 24.5 %all_to_all.10 = bf16[8,400,128]{2,1,0:T(8,128)(2,1)S(1)} all-to-all(bf16[8,400,128]{2,1,0:T(8,128)(2,1)S(1)} %pad_maximum_fusion), channel_id=1, replica_groups=mesh['slide'=4,'blk'=8] {'blk'}, dimensions={0} | all-to-all | bytes 1638400 | tf_op jit(solution)/shard_map/all_to_all | solution.py:1110
  72.5 6.5 %attend.1 = bf16[1024,128]{1,0:T(8,128)(2,1)} custom-call(bf16[1024,128]{1,0:T(8,128)(2,1)S(1)} %bitcast.184, bf16[1024,128]{1,0:T(8,128)(2,1)S(1)} %bitcast.182, bf16[1024,128]{1,0:T(8,128)(2,1)S(1)} %bitcast.180, f32[1024,1]{1,0:T(8,128)S(1)} %copy.73.row_ref, f32[1,1024]{1,0:T(1,128)S(1)} %bitcast.188), custom_call_target="tpu_custom_call" | custom-call | flops 1073741824 | bytes 1048576 | tf_op jit(solution)/shard_map/attend/pallas_call | solution.py:487
  79.0 3.8 %all-to-all-start.1 = ((bf16[8,128,128]{2,1,0:T(8,128)(2,1)}), bf16[8,128,128]{2,1,0:T(8,128)(2,1)S(1)}, u32[]{:S(2)}, u32[]{:S(2)}) async-start(bf16[8,128,128]{2,1,0:T(8,128)(2,1)} %bitcast.15), calls=%async_computation.1 | async-start | bytes 524288 | tf_op jit(solution)/shard_map/all_to_all | solution.py:1117
  84.3 5.6 %all-to-all-done.1 = bf16[8,128,128]{2,1,0:T(8,128)(2,1)S(1)} async-done(((bf16[8,128,128]{2,1,0:T(8,128)(2,1)}), bf16[8,128,128]{2,1,0:T(8,128)(2,1)S(1)}, u32[]{:S(2)}, u32[]{:S(2)}) %all-to-all-start.1) | async-done | bytes 262176 | tf_op jit(solution)/shard_map/all_to_all | solution.py:1117
  89.9 2.1 fusion.70
  93.9 7.1 %multiply_convert_fusion = (bf16[128,4096]{1,0:T(8,128)(2,1)S(1)}, f32[128,4096]{1,0:T(8,128)}) fusion(f32[4096]{0:T(1024)S(1)} %copy-done.49, bf16[1024,4096]{1,0:T(8,128)(2,1)} %param.42, f32[128,1024]{1,0:T(8,128)S(1)} %get-tuple-element.91, f32[1024]{0:T(1024)S(1)} %copy-done.43, f32[1024]{0:T(1024)S(1)} %copy-done.40, f32[128]{0:T(128)S(1)} %fusion.54, ...), kind=kOutput, calls=%fused_computation.12 | convolution fusion | flops 1079640064 | bytes 12084224 | tf_op jit(solution)/shard_map/dot_general | solution.py:74
  101.0 2.0 constant_dynamic-update-slice_fusion.1
  105.6 11.9 %sum_all.1 = f32[8,128]{1,0:T(8,128)} custom-call(f32[8,128]{1,0:T(8,128)} %pad.8.in_ref), custom_call_target="tpu_custom_call" | custom-call | tf_op jit(solution)/shard_map/sum_all/pallas_call | solution.py:437
  118.9 2.3 fusion.38
  123.9 1.5 collective-permute-start
  126.3 2.0 reshape.302
  130.6 1.7 fusion.74
  132.3 6.3 %dynamic-slice_reduce_fusion = (bf16[128,8,128]{2,1,0:T(8,128)(2,1)S(1)}, bf16[128,8,128]{2,1,0:T(8,128)(2,1)S(1)}, bf16[128,8,128]{2,1,0:T(8,128)(2,1)S(1)}, bf16[128,8,128]{2,1,0:T(8,128)(2,1)S(1)}) fusion(bf16[128,8,4,128]{3,2,1,0:T(4,128)(2,1)S(1)} %reshape.302, s32[]{:T(128)S(6)} %select_n.32, s32[]{:T(128)S(6)} %select_n.30, s32[]{:T(128)S(6)} %select_n.28, ...), kind=kLoop, calls=%fused_computation.50 | loop fusion | bytes 2097168 | tf_op jit(solution)/shard_map/jit(dynamic_index_in_dim)/dynamic_slice | solution.py:1152
  141.4 8.4 %convert_reduce_fusion = (f32[4096]{0:T(1024)}, bf16[128,4096]{1,0:T(8,128)(2,1)S(1)}) fusion(f32[128,4096]{1,0:T(8,128)S(1)} %copy-done.52, bf16[128,1024]{1,0:T(8,128)(2,1)S(1)} %get-tuple-element.51.branch_ref, bf16[4096,1024]{1,0:T(8,128)(2,1)} %param.44), kind=kOutput, calls=%fused_computation.11 | convolution fusion | flops 1087369216 | bytes 11812864 | tf_op jit(solution)/shard_map/dot_general | solution.py:74
  149.9 3.3 multiply_reduce_fusion
  153.5 1.6 collective-permute-done.1.whole2
  155.2 4.0 %collective-permute-start.2 = (bf16[128,5632]{1,0:T(8,128)(2,1)}, bf16[128,5632]{1,0:T(8,128)(2,1)}, u32[]{:S(2)}, u32[]{:S(2)}) collective-permute-start(bf16[128,5632]{1,0:T(8,128)(2,1)} %collective-permute-done.1.whole2), channel_id=1, source_target_pairs={{0,8},{8,0},{16,24},{24,16},{1,9},{9,1},{17,25},{25,17},{2,10},{10... | collective-permute-start | bytes 4325384 | tf_op jit(solution)/shard_map/ppermute | solution.py:1029
  166.0 4.6 %collective-permute-done.5.quarter3 = bf16[128,1280]{1,0:T(8,128)(2,1)S(1)} collective-permute-done((bf16[128,1280]{1,0:T(8,128)(2,1)S(1)}, bf16[128,1280]{1,0:T(8,128)(2,1)S(1)}, u32[]{:S(2)}, u32[]{:S(2)}) %collective-permute-start.5) | collective-permute-done | bytes 327712 | tf_op jit(solution)/shard_map/ppermute | solution.py:1029
  171.4 156.3 %backward.1 = (bf16[1024,1024]{1,0:T(8,128)(2,1)}, bf16[128,1024]{1,0:T(8,128)(2,1)}, bf16[128,1024]{1,0:T(8,128)(2,1)}, bf16[128,1024]{1,0:T(8,128)(2,1)}, bf16...) custom-call(bf16[1024,128]{1,0:T(8,128)(2,1)} %bitcast.185, ...), custom_call_target="tpu_custom_call" | custom-call | tf_op jit(solution)/shard_map/backward/pallas_call | solution.py:960
  331.1 2.8 convert_element_type.199
  333.8 1.6 convert_element_type.200
  341.7 7.5 %table_rows_grad.1 = f32[2048,1024]{1,0:T(8,128)} custom-call(s32[1]{0:T(128)} %bitcast.22.first_ref, s32[1,1024]{1,0:T(1,128)S(1)} %bitcast.190, bf16[1024,1024]{1,0:T(8,128)(2,1)S(1)} %copy-done.2), custom_call_target="tpu_custom_call" | custom-call | tf_op jit(solution)/shard_map/table_rows_grad/pallas_call | solution.py:1013
  (212 shorter events, 41.2 us)
Async XLA Ops:
  0.7 103.6 %copy-start = (bf16[1024,512]{1,0:T(8,128)(2,1)S(1)}, bf16[1024,512]{1,0:T(8,128)(2,1)}, u32[]{:S(2)}) copy-start(bf16[1024,512]{1,0:T(8,128)(2,1)} %param.47) | copy-start | bytes 3145732
  5.0 34.2 %copy-start.46 = (s32[1,2,128]{2,1,0:T(2,128)S(1)}, s32[1,2,128]{2,1,0:T(2,128)}, u32[]{:S(2)}) copy-start(s32[1,2,128]{2,1,0:T(2,128)} %param.29) | copy-start | bytes 3076
  5.0 34.2 %copy-start.50 = (s32[1,128]{1,0:T(1,128)S(1)}, s32[1,128]{1,0:T(1,128)}, u32[]{:S(2)}) copy-start(s32[1,128]{1,0:T(1,128)} %param.27) | copy-start | bytes 1540
  5.1 34.2 %copy-start.20 = (s32[1,128,1024]{2,1,0:T(8,128)S(1)}, s32[1,128,1024]{2,1,0:T(8,128)}, u32[]{:S(2)}) copy-start(s32[1,128,1024]{2,1,0:T(8,128)} %param.26) | copy-start | bytes 1572868
  41.2 48.6 %copy-start.9 = (f32[128,1024]{1,0:T(8,128)}, f32[128,1024]{1,0:T(8,128)S(1)}, u32[]{:S(2)}) copy-start(f32[128,1024]{1,0:T(8,128)S(1)} %get-tuple-element.89.start_ref) | copy-start | bytes 1572868
  72.4 11.0 %copy-start.19 = (f32[16,512]{1,0:T(8,128)S(1)}, f32[16,512]{1,0:T(8,128)}, u32[]{:S(2)}) copy-start(f32[16,512]{1,0:T(8,128)} %param.48) | copy-start | bytes 98308
  72.5 11.1 %copy-start.28 = (bf16[1,128,1024]{2,1,0:T(8,128)(2,1)S(1)}, bf16[1,128,1024]{2,1,0:T(8,128)(2,1)}, u32[]{:S(2)}) copy-start(bf16[1,128,1024]{2,1,0:T(8,128)(2,1)} %param.32) | copy-start | bytes 786436
  79.0 10.9 %all-to-all-start.1 = ((bf16[8,128,128]{2,1,0:T(8,128)(2,1)}), bf16[8,128,128]{2,1,0:T(8,128)(2,1)S(1)}, u32[]{:S(2)}, u32[]{:S(2)}) async-start(bf16[8,128,128]{2,1,0:T(8,128)(2,1)} %bitcast.15), calls=%async_computation.1 | async-start | bytes 524288 | tf_op jit(solution)/shard_map/all_to_all | solution.py:1117
  84.2 8.7 %copy-start.40 = (f32[1024]{0:T(1024)S(1)}, f32[1024]{0:T(1024)}, u32[]{:S(2)}) copy-start(f32[1024]{0:T(1024)} %param.40) | copy-start | bytes 12292
  84.2 8.7 %copy-start.43 = (f32[1024]{0:T(1024)S(1)}, f32[1024]{0:T(1024)}, u32[]{:S(2)}) copy-start(f32[1024]{0:T(1024)} %param.41) | copy-start | bytes 12292
  84.2 9.6 %copy-start.49 = (f32[4096]{0:T(1024)S(1)}, f32[4096]{0:T(1024)}, u32[]{:S(2)}) copy-start(f32[4096]{0:T(1024)} %param.43) | copy-start | bytes 49156
  103.1 14.5 %copy-start.45 = (f32[512]{0:T(512)S(1)}, f32[512]{0:T(512)}, u32[]{:S(2)}) copy-start(f32[512]{0:T(512)} %param.51) | copy-start | bytes 6148
  103.1 15.8 %copy-start.15 = (bf16[512,1024]{1,0:T(8,128)(2,1)S(1)}, bf16[512,1024]{1,0:T(8,128)(2,1)}, u32[]{:S(2)}) copy-start(bf16[512,1024]{1,0:T(8,128)(2,1)} %param.49) | copy-start | bytes 3145732
  123.1 32.1 %collective-permute-start.1 = (bf16[128,5632]{1,0:T(8,128)(2,1)}, bf16[128,5632]{1,0:T(8,128)(2,1)}, u32[]{:S(2)}, u32[]{:S(2)}) collective-permute-start(bf16[128,5632]{1,0:T(8,128)(2,1)} %constant_dynamic-update-slice_fusion.whole0), channel_id=1, source_target_pairs={{0,16},{8,24},{16,0},{24,8},{1,17},{9,25},{17,1},{25,9},{2,18},{10... | collective-permute-start | bytes 4325384 | tf_op jit(solution)/shard_map/ppermute | solution.py:1029
  123.9 46.7 %collective-permute-start = (bf16[128,5632]{1,0:T(8,128)(2,1)}, bf16[128,5632]{1,0:T(8,128)(2,1)}, u32[]{:S(2)}, u32[]{:S(2)}) collective-permute-start(bf16[128,5632]{1,0:T(8,128)(2,1)} %constant_dynamic-update-slice_fusion.whole0), channel_id=1, source_target_pairs={{0,8},{8,0},{16,24},{24,16},{1,9},{9,1},{17,25},{25,17},{2,10},{10... | collective-permute-start | bytes 4325384 | tf_op jit(solution)/shard_map/ppermute | solution.py:1029
  139.4 26.6 %collective-permute-start.3 = (bf16[128,1280]{1,0:T(8,128)(2,1)}, bf16[128,1280]{1,0:T(8,128)(2,1)}, u32[]{:S(2)}, u32[]{:S(2)}) collective-permute-start(bf16[128,1280]{1,0:T(8,128)(2,1)} %pad_maximum_fusion.2), channel_id=1, source_target_pairs={{0,8},{8,0},{16,24},{24,16},{1,9},{9,1},{17,25},{25,17},{2,10},{10... | collective-permute-start | bytes 983048 | tf_op jit(solution)/shard_map/ppermute | solution.py:1029
  140.2 25.8 %collective-permute-start.4 = (bf16[128,1280]{1,0:T(8,128)(2,1)}, bf16[128,1280]{1,0:T(8,128)(2,1)}, u32[]{:S(2)}, u32[]{:S(2)}) collective-permute-start(bf16[128,1280]{1,0:T(8,128)(2,1)} %pad_maximum_fusion.3), channel_id=1, source_target_pairs={{0,16},{8,24},{16,0},{24,8},{1,17},{9,25},{17,1},{25,9},{2,18},{10... | collective-permute-start | bytes 983048 | tf_op jit(solution)/shard_map/ppermute | solution.py:1029
  140.9 9.0 %slice-start.2 = ((s8[8388608]{0:T(1024)(128)(4,1)}), s8[4194304]{0:T(1024)(128)(4,1)S(1)}, s32[]{:S(2)}) async-start(s8[8388608]{0:T(1024)(128)(4,1)} %bitcast.193), calls=%async_computation.4 | async-start | bytes 8388608
  141.4 8.5 %copy-start.25 = (bf16[128,1024]{1,0:T(8,128)(2,1)}, bf16[128,1024]{1,0:T(8,128)(2,1)S(1)}, u32[]{:S(2)}) copy-start(bf16[128,1024]{1,0:T(8,128)(2,1)S(1)} %get-tuple-element.51.branch_ref) | copy-start | bytes 786436
  141.4 8.5 %slice-start.3 = ((s8[8388608]{0:T(1024)(128)(4,1)}), s8[4194304]{0:T(1024)(128)(4,1)S(1)}, s32[]{:S(2)}) async-start(s8[8388608]{0:T(1024)(128)(4,1)} %bitcast.193), calls=%async_computation.5 | async-start | bytes 8388608
  149.9 9.2 %copy-start.34 = (bf16[128,256]{1,0:T(8,128)(2,1)S(1)}, bf16[128,256]{1,0:T(8,128)(2,1)}, u32[]{:S(2)}) copy-start(bf16[128,256]{1,0:T(8,128)(2,1)} %get-tuple-element.69) | copy-start | bytes 196612
  153.3 8.3 %copy-start.16 = (bf16[512,1024]{1,0:T(8,128)(2,1)S(1)}, bf16[512,1024]{1,0:T(8,128)(2,1)}, u32[]{:S(2)}) copy-start(bf16[512,1024]{1,0:T(8,128)(2,1)} %param.49) | copy-start | bytes 3145732
  155.2 15.4 %collective-permute-start.2 = (bf16[128,5632]{1,0:T(8,128)(2,1)}, bf16[128,5632]{1,0:T(8,128)(2,1)}, u32[]{:S(2)}, u32[]{:S(2)}) collective-permute-start(bf16[128,5632]{1,0:T(8,128)(2,1)} %collective-permute-done.1.whole2), channel_id=1, source_target_pairs={{0,8},{8,0},{16,24},{24,16},{1,9},{9,1},{17,25},{25,17},{2,10},{10... | collective-permute-start | bytes 4325384 | tf_op jit(solution)/shard_map/ppermute | solution.py:1029
  159.2 11.4 %collective-permute-start.5 = (bf16[128,1280]{1,0:T(8,128)(2,1)S(1)}, bf16[128,1280]{1,0:T(8,128)(2,1)S(1)}, u32[]{:S(2)}, u32[]{:S(2)}) collective-permute-start(bf16[128,1280]{1,0:T(8,128)(2,1)S(1)} %pad_maximum_fusion.4), channel_id=1, source_target_pairs={{0,24},{8,16},{16,8},{24,0},{1,25},{9,17},{17,9},{25,1},{2,26},{10... | collective-permute-start | bytes 983048 | tf_op jit(solution)/shard_map/ppermute | solution.py:1029
  (40 other events, 166.3 us)

commit v3 on v2

--- a/solution.py
+++ b/solution.py
@@ -363,96 +363,6 @@
 SLIDE_PEERS = [(far, 0) for far in range(1, 4)]
 
 
-def panel_kernel(part_ref, out_ref, land, send_sem, recv_sem):
-    slide, blk = lax.axis_index("slide"), lax.axis_index("blk")
-    greet(slide, blk, BLK_PEERS + [(2, 0), (1, 0)])
-    links = Links(slide, blk, send_sem, recv_sem)
-    copies = [links.send(part_ref.at[flipped(blk, far)], land.at[far], 0, far) for far in range(1, 8)]
-    total = part_ref[blk].astype(F32)
-    for far in range(1, 8):
-        copies[far - 1].wait_recv()
-        total = total + land[far].astype(F32)
-    out_ref[slide * 8 + blk] = total.astype(BF16)
-    for _ in spread_everywhere(links, lambda far_slide, far_blk: out_ref.at[far_slide * 8 + far_blk]):
-        pass
-    links.finish()
-
-
-def panel_rows(part):
-    _, rows, width = part.shape
-    return pl.pallas_call(
-        panel_kernel,
-        out_shape=jax.ShapeDtypeStruct((32, rows, width), BF16),
-        in_specs=[pl.BlockSpec(memory_space=pltpu.VMEM)],
-        out_specs=pl.BlockSpec(memory_space=pltpu.VMEM),
-        scratch_shapes=[
-            pltpu.VMEM((8, rows, width), BF16),
-            pltpu.SemaphoreType.DMA((38,)),
-            pltpu.SemaphoreType.DMA((38,)),
-        ],
-        compiler_params=pltpu.CompilerParams(
-            collective_id=1, has_side_effects=True, vmem_limit_bytes=32 << 20
-        ),
-        name="panel_rows",
-    )(part)
-
-
-def exchange(slide, blk, peers, source_of, land, place, send_sem, recv_sem):
-    copies = []
-    for number, (far_slide, far_blk) in enumerate(peers):
-        to_slide, to_blk = flipped(slide, far_slide), flipped(blk, far_blk)
-        copies.append(
-            pltpu.make_async_remote_copy(
-                src_ref=source_of(to_slide, to_blk),
-                dst_ref=land.at[place],
-                send_sem=send_sem.at[number],
-                recv_sem=recv_sem.at[number],
-                device_id={"slide": to_slide, "blk": to_blk},
-                device_id_type=MESH,
-            )
-        )
-        copies[-1].start()
-    return copies
-
-
-def sum_all_kernel(in_ref, out_ref, land_one, land_two, own, send_one, recv_one, send_two, recv_two):
-    slide, blk = lax.axis_index("slide"), lax.axis_index("blk")
-    greet(slide, blk, SLIDE_PEERS + BLK_PEERS)
-    copies = exchange(slide, blk, SLIDE_PEERS, lambda *_: in_ref, land_one, slide, send_one, recv_one)
-    land_one[slide] = in_ref[...]
-    for copy in copies:
-        copy.wait()
-    own[...] = (land_one[0] + land_one[1]) + (land_one[2] + land_one[3])
-    copies = exchange(slide, blk, BLK_PEERS, lambda *_: own, land_two, blk, send_two, recv_two)
-    land_two[blk] = own[...]
-    for copy in copies:
-        copy.wait()
-    total = land_two[0]
-    for place in range(1, 8):
-        total = total + land_two[place]
-    out_ref[...] = total
-
-
-def sum_all(block):
-    return pl.pallas_call(
-        sum_all_kernel,
-        out_shape=jax.ShapeDtypeStruct(block.shape, F32),
-        in_specs=[pl.BlockSpec(memory_space=pltpu.VMEM)],
-        out_specs=pl.BlockSpec(memory_space=pltpu.VMEM),
-        scratch_shapes=[
-            pltpu.VMEM((4,) + block.shape, F32),
-            pltpu.VMEM((8,) + block.shape, F32),
-            pltpu.VMEM(block.shape, F32),
-            pltpu.SemaphoreType.DMA((3,)),
-            pltpu.SemaphoreType.DMA((3,)),
-            pltpu.SemaphoreType.DMA((7,)),
-            pltpu.SemaphoreType.DMA((7,)),
-        ],
-        compiler_params=pltpu.CompilerParams(collective_id=3, has_side_effects=True),
-        name="sum_all",
-    )(block)
-
-
 def dot_nt(left, right):
     return lax.dot_general(left, right, (((1,), (1,)), ((), ())), preferred_element_type=F32)
 
@@ -465,43 +375,6 @@
     scores = jnp.where(same_slide, dot_nt(query, key) * (HEAD_DIM**-0.5), -1e30)
     shifted = jnp.exp(scores - jnp.max(scores, axis=1, keepdims=True))
     return shifted / jnp.sum(shifted, axis=1, keepdims=True)
-
-
-def attend_kernel(q_ref, k_ref, v_ref, row_ref, col_ref, out_ref):
-    same_slide = row_ref[...] == col_ref[...]
-    lanes = lax.broadcasted_iota(jnp.int32, q_ref.shape, 1)
-    query, key, value = q_ref[...], k_ref[...], v_ref[...]
-    out = None
-    for head in range(q_ref.shape[1] // HEAD_DIM):
-        mine = lanes // HEAD_DIM == head
-        shares = head_scores(jnp.where(mine, query, 0), key, same_slide)
-        part = jnp.dot(shares.astype(BF16), value, preferred_element_type=F32)
-        out = part if out is None else jnp.where(mine, part, out)
-    out_ref[...] = out.astype(BF16)
-
-
-def attend(query, key, value, row_labels, col_labels, rows=256):
-    count, width = query.shape
-    whole = pl.BlockSpec((count, width), lambda i: (0, 0))
-    part = pl.BlockSpec((rows, width), lambda i: (i, 0))
-    return pl.pallas_call(
-        attend_kernel,
-        grid=(count // rows,),
-        out_shape=jax.ShapeDtypeStruct((count, width), BF16),
-        in_specs=[
-            part,
-            whole,
-            whole,
-            pl.BlockSpec((rows, 1), lambda i: (i, 0)),
-            pl.BlockSpec((1, count), lambda i: (0, 0)),
-        ],
-        out_specs=part,
-        compiler_params=pltpu.CompilerParams(vmem_limit_bytes=48 << 20),
-        cost_estimate=pl.CostEstimate(
-            flops=8 * count * count * width, bytes_accessed=8 * count * width, transcendentals=0
-        ),
-        name="attend",
-    )(query, key, value, row_labels, col_labels)
 
 
 class Links:
@@ -646,27 +519,324 @@
     ]
 
 
+def across(links, ref, columns, cells):
+    def rows(place):
+        return ref.at[pl.ds(place * cells, cells), columns]
+
+    far = links.send(rows(0), rows(2), 2, 0)
+    near = links.send(rows(0), rows(1), 1, 0)
+    yield
+    far.wait_recv()
+    last = links.send(rows(2), rows(3), 1, 0)
+    yield
+    near.wait_recv()
+    last.wait_recv()
+    yield
+
+
+def norm_parts(hidden):
+    centre = hidden - jnp.mean(hidden, axis=1, keepdims=True)
+    invert = lax.rsqrt(jnp.mean(centre * centre, axis=1, keepdims=True) + 1e-05)
+    return centre * invert, invert
+
+
+def norm_back(hidden, gain, grad):
+    unit, invert = norm_parts(hidden)
+    gain_grad = jnp.sum(grad * unit, axis=0, keepdims=True)
+    shift_grad = jnp.sum(grad, axis=0, keepdims=True)
+    grad_unit = grad * gain
+    grad_hidden = invert * (
+        grad_unit
+        - jnp.mean(grad_unit, axis=1, keepdims=True)
+        - unit * jnp.mean(grad_unit * unit, axis=1, keepdims=True)
+    )
+    return grad_hidden, gain_grad, shift_grad
+
+
+def exact_dot(left, right, dims):
+    return lax.dot_general(
+        left, right, (dims, ((), ())), precision=lax.Precision.HIGHEST, preferred_element_type=F32
+    )
+
+
+def mixture(mean_part, centres):
+    crossed = exact_dot(mean_part, centres, ((1,), (1,)))
+    ones = jnp.ones((8, centres.shape[1]), F32)
+    centre_square = exact_dot(ones, centres * centres, ((1,), (1,)))[0:1]
+    logits = (crossed - 0.5 * centre_square) / math.sqrt(centres.shape[1])
+    shifted = jnp.exp(logits - jnp.max(logits, axis=1, keepdims=True))
+    resp = shifted / jnp.sum(shifted, axis=1, keepdims=True)
+    return resp, exact_dot(resp, centres, ((1,), (0,)))
+
+
+def slide_masks(land, row_labels, col_labels, cells):
+    for block in range(8):
+        line = land[block, 3 * cells : 3 * cells + 1, :].astype(F32)
+        col_labels[:, block * cells : (block + 1) * cells] = line
+        row_labels[block * cells : (block + 1) * cells, :] = jnp.broadcast_to(line, (cells, cells)).T
+
+
+def forward_kernel(
+    part_ref, counts_ref, library_ref, positions_ref, freqs_ref, labels_ref, noise_ref, source_ref, gain_one, shift_one,
+    gain_two, shift_two, hidden_bias, down_bias, centres_ref,
+    wq_hbm, wk_hbm, wv_hbm, wo_hbm, wh_hbm, wd_hbm, wm_hbm, wl_hbm, wdec_hbm,
+    land_out, start_out, middle_out, inner_out, mean_out, logvar_out, glatent_out, base_out, latent_out, kl_out, decoded_out,
+    whole_out, quarter_out,
+    wq, wk, wv, wo, wh, wd, wm, wl, wdec, panel_land, panel, qkv_send, att_send, att_land, row_labels, col_labels,
+    act_parts, final, kl_own, kl_slides, kl_sum, kl_blks, load_sem, send_sem, recv_sem,
+):
+    slide, blk = lax.axis_index("slide"), lax.axis_index("blk")
+    cells, width = counts_ref.shape
+    inner, latents, per = inner_out.shape[1], mean_out.shape[1], width // 8
+    loads = []
+    for number, (source, target) in enumerate(
+        [(wq_hbm, wq), (wk_hbm, wk), (wv_hbm, wv), (wo_hbm, wo), (wh_hbm, wh), (wd_hbm, wd), (wm_hbm, wm), (wl_hbm, wl), (wdec_hbm, wdec)]
+    ):
+        loads.append(pltpu.make_async_copy(source, target, load_sem.at[number]))
+        loads[-1].start()
+    greet(slide, blk, SLIDE_PEERS + BLK_PEERS)
+    links = Links(slide, blk, send_sem, recv_sem)
+
+    part_copies = [links.send(part_ref.at[flipped(blk, far)], panel_land.at[far], 0, far) for far in (6, 4, 2, 7, 5, 3, 1)]
+    express = jnp.log(1.0 + counts_ref[...].astype(F32) * (10000.0 / library_ref[...].astype(F32))).astype(BF16)
+    whole_out[0:cells, 0:width] = express
+    quarter = width // 4
+    for block in range(4):
+        angle = positions_ref[:, block // 2 : block // 2 + 1].astype(F32) * freqs_ref[...]
+        start_out[:, block * quarter : (block + 1) * quarter] = jnp.cos(angle) if block % 2 else jnp.sin(angle)
+    total = part_ref[blk].astype(F32)
+    for place, far in enumerate((6, 4, 2, 7, 5, 3, 1)):
+        part_copies[place].wait_recv()
+        total = total + panel_land[far].astype(F32)
+    panel[slide * 8 + blk] = total.astype(BF16)
+    spread = spread_everywhere(links, lambda far_slide, far_blk: panel.at[far_slide * 8 + far_blk])
+    for _ in spread:
+        pass
+    send_express = across(links, whole_out, pl.ds(0, width), cells)
+    next(send_express)
+
+    def source_part(which):
+        return source_ref.at[:, pl.ds(pl.multiple_of(which * quarter, 128), quarter)]
+
+    def source_slot(place):
+        return quarter_out.at[pl.ds(place * cells, cells), pl.ds(inner // 4, quarter)]
+
+    source_copies = [links.send(source_part(flipped(slide, far)), source_slot(far), far, 0) for far in (2, 3, 1)]
+    source_slot(0)[...] = source_part(slide)[...]
+
+    hidden_start = start_out[...] + jnp.dot(express, panel[...].reshape(width, width), preferred_element_type=F32)
+    start_out[...] = hidden_start
+    normed = (norm_parts(hidden_start)[0] * gain_one[...] + shift_one[...]).astype(BF16)
+    whole_out[0:cells, width : 2 * width] = normed
+    qkv_send[:, 3 * cells :, :] = jnp.broadcast_to(labels_ref[...].astype(BF16)[None], (8, 16, per))
+    for number in range(3):
+        loads[number].wait()
+
+    along_x, along_z = blk % 2, blk // 2
+    qkv_copies = []
+    for far in (3, 2, 1, 0):
+        pair = flipped(along_z, far)
+        columns = pl.ds(pl.multiple_of(pair * 2 * per, 128), 2 * per)
+        for number, weight in enumerate((wq, wk, wv)):
+            product = jnp.dot(normed, weight[:, columns], preferred_element_type=F32).astype(BF16)
+            for side in range(2):
+                qkv_send[pair * 2 + side, number * cells : (number + 1) * cells, :] = product[:, side * per : (side + 1) * per]
+        for side in (1, 0):
+            if far or side:
+                target = flipped(pair * 2 + along_x, side)
+                qkv_copies.append(links.send(qkv_send.at[target], land_out.at[blk], 0, 2 * far + side))
+    land_out[blk] = qkv_send[blk]
+    next(send_express)
+    send_normed = across(links, whole_out, pl.ds(width, width), cells)
+    next(send_normed)
+    for copy in qkv_copies:
+        copy.wait_recv()
+
+    slide_masks(land_out, row_labels, col_labels, cells)
+    key = land_out[:, cells : 2 * cells, :].reshape(8 * cells, per)
+    value = land_out[:, 2 * cells : 3 * cells, :].reshape(8 * cells, per)
+    att_copies = []
+    for far in (3, 2, 1, 0):
+        pair = flipped(along_z, far)
+        query = land_out[pl.ds(pair * 2, 2), 0:cells, :].reshape(2 * cells, per)
+        same_slide = row_labels[pl.ds(pl.multiple_of(pair * 2 * cells, 128), 2 * cells), 0:1] == col_labels[...]
+        lane = lax.broadcasted_iota(jnp.int32, query.shape, 1)
+        out = None
+        for head in range(per // HEAD_DIM):
+            mine = lane // HEAD_DIM == head
+            shares = head_scores(jnp.where(mine, query, 0), key, same_slide)
+            part = jnp.dot(shares.astype(BF16), value, preferred_element_type=F32)
+            out = part if out is None else jnp.where(mine, part, out)
+        att_send[pl.ds(pair * 2, 2)] = out.astype(BF16).reshape(2, cells, per)
+        for side in (1, 0):
+            if far or side:
+                target = flipped(pair * 2 + along_x, side)
+                att_copies.append(links.send(att_send.at[target], att_land.at[blk], 0, 2 * far + side))
+    att_land[blk] = att_send[blk]
+    next(send_normed)
+    for copy in att_copies:
+        copy.wait_recv()
+    for block in range(8):
+        whole_out[0:cells, 2 * width + block * per : 2 * width + (block + 1) * per] = att_land[block]
+    send_attended = across(links, whole_out, pl.ds(2 * width, width), cells)
+    next(send_attended)
+
+    loads[3].wait()
+    hidden_middle = start_out[...] + jnp.dot(
+        whole_out[0:cells, 2 * width : 3 * width], wo[...], preferred_element_type=F32
+    )
+    middle_out[...] = hidden_middle
+    normed_two = (norm_parts(hidden_middle)[0] * gain_two[...] + shift_two[...]).astype(BF16)
+    whole_out[0:cells, 3 * width :] = normed_two
+    send_two = across(links, whole_out, pl.ds(3 * width, width), cells)
+    next(send_two)
+    loads[4].wait()
+    loads[5].wait()
+    final[...] = hidden_middle + down_bias[...]
+    chunk = inner // 8
+
+    def feed(j, carry):
+        where = pl.ds(pl.multiple_of(j * chunk, 128), chunk)
+        inner_sum = jnp.dot(whole_out[0:cells, 3 * width :], wh[:, where], preferred_element_type=F32) + hidden_bias[:, where]
+        inner_out[:, where] = inner_sum
+        act = gelu_tanh(inner_sum).astype(BF16)
+        for block in range(4):
+            act_parts[block, :, pl.ds(pl.multiple_of(j * (chunk // 4), 128), chunk // 4)] = act[:, block * (chunk // 4) : (block + 1) * (chunk // 4)]
+        final[...] += jnp.dot(act, wd[where, :], preferred_element_type=F32)
+        return carry
+
+    lax.fori_loop(0, 8, feed, 0)
+    act_copies = [
+        links.send(act_parts.at[flipped(slide, far)], quarter_out.at[pl.ds(far * cells, cells), pl.ds(0, inner // 4)], far, 0)
+        for far in (2, 3, 1)
+    ]
+    quarter_out[0:cells, 0 : inner // 4] = act_parts[slide]
+    base = final[...].astype(BF16)
+    base_out[...] = base
+    for number in (6, 7, 8):
+        loads[number].wait()
+    mean_lat = jnp.dot(base, wm[...], preferred_element_type=F32)
+    log_var = jnp.dot(base, wl[...], preferred_element_type=F32)
+    mean_out[...] = mean_lat
+    logvar_out[...] = log_var
+    centres = centres_ref[...]
+    resp, mixed = mixture(mean_lat, centres)
+    mixed_square = exact_dot(resp, centres * centres, ((1,), (0,)))
+    kl_cell = 0.5 * (
+        jnp.exp(log_var) - 1.0 - log_var + mean_lat * mean_lat - 2.0 * mean_lat * mixed + mixed_square
+    )
+    kl_line = jnp.sum(kl_cell, axis=0, keepdims=True)
+    kl_own[...] = jnp.zeros_like(kl_own)
+    for block in range(latents // 128):
+        kl_own[block : block + 1, :] = kl_line[:, block * 128 : (block + 1) * 128]
+    kl_copies = [links.send(kl_own, kl_slides.at[slide], far, 0) for far in (2, 3, 1)]
+    kl_slides[slide] = kl_own[...]
+    latent = (mean_lat + jnp.exp(0.5 * log_var) * noise_ref[...]).astype(BF16)
+    latent_out[...] = latent
+    decoded_out[...] = jnp.dot(latent, wdec[...], preferred_element_type=F32)
+    for copy in kl_copies:
+        copy.wait_recv()
+    kl_sum[...] = (kl_slides[0] + kl_slides[1]) + (kl_slides[2] + kl_slides[3])
+    kl_copies = [links.send(kl_sum, kl_blks.at[blk], 0, far) for far in (6, 4, 2, 7, 5, 3, 1)]
+    kl_blks[blk] = kl_sum[...]
+    glatent_out[...] = dot_nt(source_ref[...], wdec[...])
+    next(send_attended)
+    next(send_two)
+    for copy in kl_copies:
+        copy.wait_recv()
+    kl_total = kl_blks[0]
+    for block in range(1, 8):
+        kl_total = kl_total + kl_blks[block]
+    kl_out[...] = kl_total
+    for copy in source_copies + act_copies:
+        copy.wait_recv()
+    for sent in (send_express, send_normed, send_attended, send_two):
+        next(sent)
+    links.finish()
+
+
+def forward(inputs, weights, cells, width, inner, latents):
+    per = width // 8
+    shape = jax.ShapeDtypeStruct
+    vmem, left = pl.BlockSpec(memory_space=pltpu.VMEM), pl.BlockSpec(memory_space=pl.ANY)
+    outs = (
+        shape((8, 3 * cells + 16, per), BF16),
+        shape((cells, width), F32),
+        shape((cells, width), F32),
+        shape((cells, inner), F32),
+        shape((cells, latents), F32),
+        shape((cells, latents), F32),
+        shape((cells, latents), F32),
+        shape((cells, width), BF16),
+        shape((cells, latents), BF16),
+        shape((8, 128), F32),
+        shape((cells, width), F32),
+        shape((4 * cells, 4 * width), BF16),
+        shape((4 * cells, inner // 4 + width // 4), BF16),
+    )
+    copies = 96
+    return pl.pallas_call(
+        forward_kernel,
+        out_shape=outs,
+        in_specs=[vmem] * len(inputs) + [left] * len(weights),
+        out_specs=[vmem] * len(outs),
+        scratch_shapes=[pltpu.VMEM(weight.shape, BF16) for weight in weights]
+        + [
+            pltpu.VMEM((8, width // 32, width), BF16),
+            pltpu.VMEM((32, width // 32, width), BF16),
+            pltpu.VMEM((8, 3 * cells + 16, per), BF16),
+            pltpu.VMEM((8, cells, per), BF16),
+            pltpu.VMEM((8, cells, per), BF16),
+            pltpu.VMEM((8 * cells, cells), F32),
+            pltpu.VMEM((1, 8 * cells), F32),
+            pltpu.VMEM((4, cells, inner // 4), BF16),
+            pltpu.VMEM((cells, width), F32),
+            pltpu.VMEM((8, 128), F32),
+            pltpu.VMEM((4, 8, 128), F32),
+            pltpu.VMEM((8, 128), F32),
+            pltpu.VMEM((8, 8, 128), F32),
+            pltpu.SemaphoreType.DMA((len(weights),)),
+            pltpu.SemaphoreType.DMA((copies,)),
+            pltpu.SemaphoreType.DMA((copies,)),
+        ],
+        compiler_params=pltpu.CompilerParams(
+            collective_id=1, has_side_effects=True, vmem_limit_bytes=62 << 20
+        ),
+        name="forward",
+    )(*inputs, *weights)
+
+
 def backward_kernel(
-    q_ref, k_ref, v_ref, row_ref, col_ref, branch_ref, gmean_ref, glogvar_ref, ginner_ref, gout_ref,
-    middle_ref, start_ref, gain_ref, small_ref,
-    whole0, whole1, whole2, whole3, quarter0, quarter1, quarter2, quarter3, wq_hbm, wk_hbm, wv_hbm, wo_hbm,
+    land_ref, start_ref, middle_ref, inner_ref, mean_ref, logvar_ref, glatent_ref, base_ref, latent_ref, kl_ref, noise_ref,
+    centres_ref, weight_ref, floor_ref, gain_one, gain_two,
+    whole_hbm, quarter_hbm, wq_hbm, wk_hbm, wv_hbm, wo_hbm, wh_hbm, wd_hbm, wm_hbm, wl_hbm,
     panel_out, query_out, key_out, value_out, output_out, hidden_out, down_out, mean_out, logvar_out, decoder_out, small_out,
-    whole, quarter, wq, wk, wv, wo, branch_all, gmean_all, glogvar_all, ginner_all, gout_all, gqkv_all, genc_all,
+    whole, base_all, latent_all, quarter, wide_slots, wo, wm, wl, branch_all, gmean, glogvar, gmean_all, glogvar_all, ginner,
+    ginner_all, gout, gout_all, gmiddle, gqkv_all, genc_all, row_ref, col_ref,
     att_send, att_land, dqkv, dqkv_land, dk_sum, dv_sum, grad_qkv, encoded, small, small_land, small_own, small_slides,
     load_sem, send_sem, recv_sem, *unit_refs,
 ):
     slide, blk = lax.axis_index("slide"), lax.axis_index("blk")
     cells, width = middle_ref.shape
-    inner, latents, per = ginner_ref.shape[1], gmean_ref.shape[1], width // 8
+    inner, latents, per = inner_ref.shape[1], mean_ref.shape[1], width // 8
     loads = {}
-    for number, (name, source, target) in enumerate(
-        [("wo", wo_hbm, wo)]
-        + [("q%d" % i, ref, quarter.at[pl.ds(i * cells, cells)]) for i, ref in enumerate((quarter0, quarter1, quarter2, quarter3))]
-        + [("w%d" % i, ref, whole.at[pl.ds(i * cells, cells)]) for i, ref in enumerate((whole0, whole1, whole2, whole3))]
-        + [("wq", wq_hbm, wq), ("wk", wk_hbm, wk), ("wv", wv_hbm, wv)]
-    ):
-        loads[name] = pltpu.make_async_copy(source, target, load_sem.at[number])
+
+    def load(name, source, target):
+        loads[name] = pltpu.make_async_copy(source, target, load_sem.at[len(loads)])
         loads[name].start()
+
+    def load_feed(far, slot):
+        which = pl.ds(pl.multiple_of(flipped(slide, far) * (inner // 4), 128), inner // 4)
+        load("wd%d" % far, wd_hbm.at[which, :], wide_slots.at[2 * slot])
+        load("wh%d" % far, wh_hbm.at[:, which], wide_slots.at[2 * slot + 1])
+
+    load("wm", wm_hbm, wm)
+    load("wl", wl_hbm, wl)
+    load_feed(2, 0)
+    load_feed(3, 1)
+    load("wo", wo_hbm, wo)
+    load("quarter", quarter_hbm, quarter)
+    load("whole", whole_hbm, whole)
     greet(slide, blk, SLIDE_PEERS + BLK_PEERS)
     links = Links(slide, blk, send_sem, recv_sem)
 
@@ -680,19 +850,108 @@
         target[0] = lanes(ref, slide, size)[...]
         return copies
 
-    branch_far = links.send(branch_ref, branch_all.at[2], 2, 0)
-    branch_near = links.send(branch_ref, branch_all.at[1], 1, 0)
-    branch_all[0] = branch_ref[...]
-    mean_swap = swap(gmean_ref, latents // 4, gmean_all)
-    logvar_swap = swap(glogvar_ref, latents // 4, glogvar_all)
-    inner_swap = swap(ginner_ref, inner // 4, ginner_all)
-    out_swap = swap(gout_ref, width // 4, gout_all)
+    small[...] = jnp.zeros_like(small)
+
+    kl_mean = jnp.concatenate([kl_ref[block : block + 1, :] for block in range(latents // 128)], axis=1) / (32 * cells)
+    grad_kl = weight_ref[0, 0] * (kl_mean > floor_ref[...]).astype(F32)
+    mean_lat, log_var, centres = mean_ref[...], logvar_ref[...], centres_ref[...]
+    grad_latent = glatent_ref[...]
+    resp, mixed = mixture(mean_lat, centres)
+    weighted = mean_lat * grad_kl
+    half_square = exact_dot(jnp.broadcast_to(0.5 * grad_kl, (8, latents)), centres * centres, ((1,), (1,)))[0:1]
+    grad_resp = half_square - exact_dot(weighted, centres, ((1,), (1,)))
+    grad_logits = resp * (grad_resp - jnp.sum(resp * grad_resp, axis=1, keepdims=True)) / math.sqrt(latents)
+    grad_mean = grad_latent + grad_kl * (mean_lat - mixed) + exact_dot(grad_logits, centres, ((1,), (0,)))
+    grad_logvar = grad_latent * (0.5 * jnp.exp(0.5 * log_var) * noise_ref[...]) + 0.5 * grad_kl * (jnp.exp(log_var) - 1.0)
+    gmean[...] = grad_mean.astype(BF16)
+    glogvar[...] = grad_logvar.astype(BF16)
+    loads["wm"].wait()
+    loads["wl"].wait()
+    grad_final = dot_nt(gmean[...], wm[...]) + dot_nt(glogvar[...], wl[...])
+    gmiddle[...] = grad_final
+    branch_all[0] = grad_final.astype(BF16)
+    branch_far = links.send(branch_all.at[0], branch_all.at[2], 2, 0)
+    branch_near = links.send(branch_all.at[0], branch_all.at[1], 1, 0)
+    mean_swap = swap(gmean, latents // 4, gmean_all)
+    logvar_swap = swap(glogvar, latents // 4, glogvar_all)
+    base_all[0:cells, :] = base_ref[...]
+    send_base = across(links, base_all, pl.ds(0, width), cells)
+    next(send_base)
+    rows = latents // 8
+    for along_x in range(2):
+        for along_z in range(4):
+            place = (along_z * 2 + along_x) * rows
+            latent_all[0:cells, (along_x * 4 + along_z) * rows : (along_x * 4 + along_z + 1) * rows] = latent_ref[:, place : place + rows]
+    send_latent = across(links, latent_all, pl.ds(0, latents), cells)
+    next(send_latent)
+    ones = jnp.ones((cells, 128), F32)
+    logit_sum = exact_dot(grad_logits, ones, ((0,), (0,)))[:, 0:1]
+    resp_sum = exact_dot(resp, ones, ((0,), (0,)))[:, 0:1]
+    centres_grad = (
+        exact_dot(grad_logits, mean_lat, ((0,), (0,)))
+        - logit_sum * centres
+        - exact_dot(resp, weighted, ((0,), (0,)))
+        + resp_sum * grad_kl * centres
+    )
+    count = centres.shape[0]
+    for block in range(8):
+        small[block, 16 : 16 + count, 0 : latents // 8] = centres_grad[:, block * (latents // 8) : (block + 1) * (latents // 8)]
+    bias_line = jnp.sum(branch_all[0].astype(F32), axis=0, keepdims=True)
+    for block in range(8):
+        small[block, 8:9, :] = bias_line[:, block * 128 : (block + 1) * 128]
+
+    encoded[...] = jnp.zeros_like(encoded)
+    chunk = inner // 8
+    inner_swap = []
+    for turn, far in enumerate((2, 3, 1, 0)):
+        slot = turn % 2
+        loads["wd%d" % far].wait()
+        loads["wh%d" % far].wait()
+        which = flipped(slide, far)
+
+        def feed(j, carry, slot=slot, which=which):
+            near = pl.ds(pl.multiple_of(j * chunk, 128), chunk)
+            where = pl.ds(pl.multiple_of(which * (inner // 4) + j * chunk, 128), chunk)
+            values = inner_ref[:, where]
+            squared = values * values
+            bent = jnp.tanh(0.7978845608028654 * (values + 0.044715 * squared * values))
+            slope = 0.5 * (1.0 + bent) + 0.5 * values * (1.0 - bent * bent) * (
+                0.7978845608028654 * (1.0 + 3 * 0.044715 * squared)
+            )
+            grad = (dot_nt(branch_all[0], wide_slots[2 * slot, near, :]) * slope).astype(BF16)
+            ginner[:, where] = grad
+            line = jnp.sum(grad.astype(F32), axis=0, keepdims=True)
+            for block in range(chunk // 128):
+                small[which * 2 + j, 4 + block : 5 + block, :] = line[:, block * 128 : (block + 1) * 128]
+            encoded[...] += dot_nt(grad, wide_slots[2 * slot + 1, :, near])
+            return carry
+
+        lax.fori_loop(0, 2, feed, 0)
+        if far:
+            inner_swap.append(links.send(lanes(ginner, which, inner // 4), ginner_all.at[far], far, 0))
+        else:
+            ginner_all[0] = lanes(ginner, slide, inner // 4)[...]
+        if turn < 2:
+            load_feed((1, 0)[turn], slot)
+        if turn == 1:
+            branch_far.wait_recv()
+            branch_last = links.send(branch_all.at[2], branch_all.at[3], 1, 0)
+    for number, (name, source) in enumerate((("wq", wq_hbm), ("wk", wk_hbm), ("wv", wv_hbm))):
+        load(name, source, wide_slots.at[number])
+    wq, wk, wv = wide_slots.at[0], wide_slots.at[1], wide_slots.at[2]
+
+    grad_hidden, gain_grad, shift_grad = norm_back(middle_ref[...], gain_two[...], encoded[...])
+    for block in range(8):
+        small[block, 2:3, :] = gain_grad[:, block * 128 : (block + 1) * 128]
+        small[block, 3:4, :] = shift_grad[:, block * 128 : (block + 1) * 128]
+    gmiddle[...] += grad_hidden
+    gout[...] = gmiddle[...].astype(BF16)
 
     loads["wo"].wait()
 
     def att_block(target, store):
         rows = wo[pl.ds(pl.multiple_of(target * per, per), per), :]
-        store(dot_nt(gout_ref[...], rows).astype(BF16))
+        store(dot_nt(gout[...], rows).astype(BF16))
 
     att_copies = []
     for far in (6, 4, 2, 7, 5, 3, 1):
@@ -708,14 +967,21 @@
         att_land[blk] = block
 
     att_block(blk, keep_own)
-
-    width_at = {"express": 0, "one": width, "attended": 2 * width, "two": 3 * width, "base": 4 * width, "latent": 5 * width}
+    out_swap = swap(gout, width // 4, gout_all)
+
+    width_at = {"express": 0, "one": width, "attended": 2 * width, "two": 3 * width}
 
     def of_whole(name):
         def left(column):
             return whole[:, pl.ds(width_at[name] + column, 128)]
 
         return left
+
+    def of_base(column):
+        return base_all[:, pl.ds(column, 128)]
+
+    def of_latent(column):
+        return latent_all[:, pl.ds(column, 128)]
 
     def of_act(column):
         return quarter[:, pl.ds(column, 128)]
@@ -732,11 +998,11 @@
 
     half_w, half_i = width // 2, inner // 8
     operands = {
-        "decoder": (of_whole("latent"), source_all),
+        "decoder": (of_latent, source_all),
         "down0": (of_act, flat(branch_all, 0, half_w)),
         "down1": (of_act, flat(branch_all, half_w, half_w)),
-        "mean": (of_whole("base"), flat(gmean_all)),
-        "logvar": (of_whole("base"), flat(glogvar_all)),
+        "mean": (of_base, flat(gmean_all)),
+        "logvar": (of_base, flat(glogvar_all)),
         "hidden0": (of_whole("two"), flat(ginner_all, 0, half_i)),
         "hidden1": (of_whole("two"), flat(ginner_all, half_i, half_i)),
         "output": (of_whole("attended"), flat(gout_all)),
@@ -752,9 +1018,6 @@
             links, left, right, rows, columns, dense, unit_refs[4 * number : 4 * number + 4]
         )
 
-    def columns_slot(ref, size, offset=0):
-        return lambda place: ref.at[:, pl.ds(pl.multiple_of(place * size + offset, 128), size if not offset else size)]
-
     slots = {
         "decoder": lambda place: lanes(decoder_out, place, width // 4),
         "down0": lambda place: down_out.at[pl.ds(pl.multiple_of(place * (inner // 32), inner // 32), inner // 32), pl.ds(0, half_w)],
@@ -774,24 +1037,25 @@
         spreads[name] = spread_slide(links, slots[name], units[name].total())
         next(spreads[name])
 
-    for i in range(4):
-        loads["q%d" % i].wait()
-    for i in range(4):
-        loads["w%d" % i].wait()
-    units["decoder"].send_x()
-    branch_far.wait_recv()
-    branch_last = links.send(branch_all.at[2], branch_all.at[3], 1, 0)
+    loads["quarter"].wait()
+    loads["whole"].wait()
     branch_near.wait_recv()
     branch_last.wait_recv()
     units["down0"].send_x()
     units["down1"].send_x()
+    next(send_base)
+    next(send_latent)
     for copy in mean_swap + logvar_swap:
         copy.wait_recv()
+    next(send_latent)
+    units["decoder"].send_x()
+    next(send_base)
     units["mean"].send_x()
     units["logvar"].send_x()
 
     for copy in att_copies:
         copy.wait_recv()
+    slide_masks(land_ref, row_ref, col_ref, cells)
     dk_sum[...] = jnp.zeros_like(dk_sum)
     dv_sum[...] = jnp.zeros_like(dv_sum)
     scale = HEAD_DIM**-0.5
@@ -799,10 +1063,11 @@
 
     def rows_back(i, carry):
         where = pl.ds(pl.multiple_of(i * rows, rows), rows)
-        same_slide = row_ref[where, :] == col_ref[...]
-        query = q_ref[where, :]
+        same_slide = row_ref[where, 0:1] == col_ref[...]
+        query = land_ref[pl.ds(2 * i, 2), 0:cells, :].reshape(rows, per)
         grad = att_land[pl.ds(2 * i, 2)].reshape(rows, per)
-        key, value = k_ref[...], v_ref[...]
+        key = land_ref[:, cells : 2 * cells, :].reshape(8 * cells, per)
+        value = land_ref[:, 2 * cells : 3 * cells, :].reshape(8 * cells, per)
         lane = lax.broadcasted_iota(jnp.int32, query.shape, 1)
         grad_query = None
         for head in range(per // HEAD_DIM):
@@ -854,23 +1119,10 @@
         return carry
 
     lax.fori_loop(0, width // 256, norm_input, 0)
-    hidden = start_ref[...]
-    centre = hidden - jnp.mean(hidden, axis=1, keepdims=True)
-    invert = lax.rsqrt(jnp.mean(centre * centre, axis=1, keepdims=True) + 1e-05)
-    unit = centre * invert
-    grad_normed = encoded[...]
-    gain_grad = jnp.sum(grad_normed * unit, axis=0, keepdims=True)
-    shift_grad = jnp.sum(grad_normed, axis=0, keepdims=True)
-    grad_unit = grad_normed * gain_ref[...]
-    grad_hidden = invert * (
-        grad_unit
-        - jnp.mean(grad_unit, axis=1, keepdims=True)
-        - unit * jnp.mean(grad_unit * unit, axis=1, keepdims=True)
-    )
-    grad_qkv[3] = (middle_ref[...] + grad_hidden).astype(BF16)
+    grad_hidden, gain_grad, shift_grad = norm_back(start_ref[...], gain_one[...], encoded[...])
+    grad_qkv[3] = (gmiddle[...] + grad_hidden).astype(BF16)
     encoded_swap = swap(grad_qkv.at[3], width // 4, genc_all)
 
-    small[...] = small_ref[...]
     for block in range(8):
         small[block, 0:1, :] = gain_grad[:, block * 128 : (block + 1) * 128]
         small[block, 1:2, :] = shift_grad[:, block * 128 : (block + 1) * 128]
@@ -936,8 +1188,9 @@
     links.finish()
 
 
-def backward(inputs, pieces, weights, cells, width, inner, latents, small_rows):
+def backward(inputs, weights, cells, width, inner, latents):
     per = width // 8
+    small_rows = 32
     shape = jax.ShapeDtypeStruct
     unit_scratch = []
     for _, rows, columns, _ in reductions_of(cells, width, inner, latents):
@@ -957,47 +1210,59 @@
         shape((latents // 8, width), BF16),
         shape((small_rows, 128), F32),
     )
+    scratch = [
+        ((4 * cells, 4 * width), BF16),
+        ((4 * cells, width), BF16),
+        ((4 * cells, latents), BF16),
+        ((4 * cells, inner // 4 + width // 4), BF16),
+        ((4, width, width), BF16),
+        ((width, width), BF16),
+        ((width, latents), BF16),
+        ((width, latents), BF16),
+        ((4, cells, width), BF16),
+        ((cells, latents), BF16),
+        ((cells, latents), BF16),
+        ((4, cells, latents // 4), BF16),
+        ((4, cells, latents // 4), BF16),
+        ((cells, inner), BF16),
+        ((4, cells, inner // 4), BF16),
+        ((cells, width), BF16),
+        ((4, cells, width // 4), BF16),
+        ((cells, width), F32),
+        ((3, 4, cells, width // 4), BF16),
+        ((4, cells, width // 4), BF16),
+        ((8 * cells, cells), F32),
+        ((1, 8 * cells), F32),
+        ((8, cells, per), BF16),
+        ((8, cells, per), BF16),
+        ((8, 3 * cells, per), BF16),
+        ((8, 3 * cells, per), BF16),
+        ((8 * cells, per), F32),
+        ((8 * cells, per), F32),
+        ((4, cells, width), BF16),
+        ((cells, width), F32),
+        ((8, small_rows, 128), F32),
+        ((8, small_rows, 128), F32),
+        ((small_rows, 128), F32),
+        ((4, small_rows, 128), F32),
+    ]
     return pl.pallas_call(
         backward_kernel,
         out_shape=outs,
-        in_specs=[vmem] * len(inputs) + [left] * (len(pieces) + len(weights)),
+        in_specs=[vmem] * len(inputs) + [left] * len(weights),
         out_specs=[vmem] * len(outs),
-        scratch_shapes=[
-            pltpu.VMEM((4 * cells, 5 * width + latents), BF16),
-            pltpu.VMEM((4 * cells, inner // 4 + width // 4), BF16),
-            pltpu.VMEM((width, width), BF16),
-            pltpu.VMEM((width, width), BF16),
-            pltpu.VMEM((width, width), BF16),
-            pltpu.VMEM((width, width), BF16),
-            pltpu.VMEM((4, cells, width), BF16),
-            pltpu.VMEM((4, cells, latents // 4), BF16),
-            pltpu.VMEM((4, cells, latents // 4), BF16),
-            pltpu.VMEM((4, cells, inner // 4), BF16),
-            pltpu.VMEM((4, cells, width // 4), BF16),
-            pltpu.VMEM((3, 4, cells, width // 4), BF16),
-            pltpu.VMEM((4, cells, width // 4), BF16),
-            pltpu.VMEM((8, cells, per), BF16),
-            pltpu.VMEM((8, cells, per), BF16),
-            pltpu.VMEM((8, 3 * cells, per), BF16),
-            pltpu.VMEM((8, 3 * cells, per), BF16),
-            pltpu.VMEM((8 * cells, per), F32),
-            pltpu.VMEM((8 * cells, per), F32),
-            pltpu.VMEM((4, cells, width), BF16),
-            pltpu.VMEM((cells, width), F32),
-            pltpu.VMEM((8, small_rows, 128), F32),
-            pltpu.VMEM((8, small_rows, 128), F32),
-            pltpu.VMEM((small_rows, 128), F32),
-            pltpu.VMEM((4, small_rows, 128), F32),
-            pltpu.SemaphoreType.DMA((12,)),
+        scratch_shapes=[pltpu.VMEM(*item) for item in scratch]
+        + [
+            pltpu.SemaphoreType.DMA((16,)),
             pltpu.SemaphoreType.DMA((copies,)),
             pltpu.SemaphoreType.DMA((copies,)),
         ]
         + unit_scratch,
         compiler_params=pltpu.CompilerParams(
-            collective_id=5, has_side_effects=True, vmem_limit_bytes=60 << 20
+            collective_id=2, has_side_effects=True, vmem_limit_bytes=62 << 20
         ),
         name="backward",
-    )(*inputs, *pieces, *weights)
+    )(*inputs, *weights)
 
 
 def table_kernel(first_ref, ids_ref, panel_ref, out_ref):
@@ -1023,23 +1288,6 @@
         compiler_params=pltpu.CompilerParams(vmem_limit_bytes=40 << 20),
         name="table_rows_grad",
     )(first_row.reshape(1), gene_ids.reshape(1, genes), panel)
-
-
-def over_slide(array, mask):
-    return lax.ppermute(array, "slide", [(place, place ^ mask) for place in range(4)])
-
-
-def over_blk(array, mask):
-    return lax.ppermute(array, "blk", [(place, place ^ mask) for place in range(8)])
-
-
-def gather_slide(array):
-    far = over_slide(array, 2)
-    return [array, over_slide(array, 1), far, over_slide(far, 1)]
-
-
-def swap_slide(pick, slide):
-    return [pick(slide)] + [over_slide(pick(jnp.bitwise_xor(slide, far)), far) for far in (1, 2, 3)]
 
 
 def on_device_fast(
@@ -1076,134 +1324,52 @@
     latents = mean_weight.shape[1]
     inner = hidden_weight.shape[1]
     slide, blk = lax.axis_index("slide"), lax.axis_index("blk")
-    per = width // 8
-
-    def columns(array, start, size):
-        return lax.dynamic_slice_in_dim(array, start, size, 1)
-
     table_rows = gene_table.shape[0]
     first_row = blk * table_rows
     row_ids = first_row + jnp.arange(table_rows, dtype=jnp.int32)
     my_ids = lax.dynamic_slice_in_dim(gene_ids, slide * (genes // 4), genes // 4, 0)
     selector = (my_ids[:, None] == row_ids[None, :]).astype(BF16)
     part = matmul(selector, gene_table).astype(BF16).reshape(8, genes // 32, width)
-    panel_weight = panel_rows(part).reshape(genes, width)
-
-    express = normalized(counts[0], library[0]).astype(BF16)
-    hidden_start = matmul(express, panel_weight) + position_code(positions[0], width)
-    normed_one = layer_norm(hidden_start, first_gain, first_shift).astype(BF16)
-
-    def to_blocks(array):
-        return array.reshape(cells, 8, per).transpose(1, 0, 2)
-
-    def from_blocks(array):
-        return array.transpose(1, 0, 2).reshape(cells, 8 * per)
-
-    labels = jnp.broadcast_to(
-        jnp.pad(slide_of_cell[0].astype(BF16), (0, per - cells))[None, None, :], (8, 16, per)
-    )
-    qkv = jnp.concatenate(
-        [to_blocks(matmul(normed_one, w).astype(BF16)) for w in (query_weight, key_weight, value_weight)]
-        + [labels],
-        axis=1,
-    )
-    qkv = lax.all_to_all(qkv, "blk", 0, 0)
-    query, key, value = [
-        qkv[:, i * cells : (i + 1) * cells].reshape(8 * cells, per) for i in range(3)
-    ]
-    labels_all = qkv[:, 3 * cells, :cells].reshape(8 * cells).astype(F32)
-    row_labels, col_labels = labels_all[:, None], labels_all[None, :]
-    attended = attend(query, key, value, row_labels, col_labels)
-    attended = from_blocks(lax.all_to_all(attended.reshape(8, cells, per), "blk", 0, 0))
-
-    hidden_middle = hidden_start + matmul(attended, output_weight)
-    normed_two = layer_norm(hidden_middle, second_gain, second_shift).astype(BF16)
-    inner_sum = matmul(normed_two, hidden_weight) + hidden_bias
-    act_low = gelu_tanh(inner_sum).astype(BF16)
-    hidden_final = hidden_middle + matmul(act_low, down_weight) + down_bias
-    base_low = hidden_final.astype(BF16)
-    mean_lat = matmul(base_low, mean_weight)
-    log_var = matmul(base_low, logvar_weight)
-    noise_local = latent_noise[0]
-
-    def bottleneck(mean_part, logvar_part, centres):
-        return (
-            mean_part + jnp.exp(0.5 * logvar_part) * noise_local,
-            divergence_cells(mean_part, logvar_part, centres),
-        )
-
-    (latent, kl_cell), pull_latent = jax.vjp(bottleneck, mean_lat, log_var, component_means)
-    latent_low = latent.astype(BF16)
-    decoded = matmul(latent_low, decoder_weight)
-    everyone = cells * 32
-    kl_rows = jnp.pad(jnp.sum(kl_cell, axis=0).reshape(-1, 128), ((0, 8 - latents // 128), (0, 0)))
-    kl_mean = sum_all(kl_rows)[: latents // 128].reshape(latents) / everyone
+    quarter = width // 4
+    freqs = jnp.exp(-math.log(10000.0) * jnp.arange(quarter, dtype=F32) / quarter)
+    labels = jnp.broadcast_to(slide_of_cell[0].astype(F32)[None], (16, cells))
+    (
+        land, hidden_start, hidden_middle, inner_sum, mean_lat, log_var, grad_latent, base, latent, kl_total, decoded,
+        whole, quarters,
+    ) = forward(
+        (
+            part, counts[0], library[0][:, None], positions[0].T, freqs[None], labels, latent_noise[0], decoded_grad[0],
+            first_gain[None], first_shift[None], second_gain[None], second_shift[None], hidden_bias[None],
+            down_bias[None], component_means,
+        ),
+        (
+            query_weight, key_weight, value_weight, output_weight, hidden_weight, down_weight, mean_weight,
+            logvar_weight, decoder_weight,
+        ),
+        cells, width, inner, latents,
+    )
+    kl_mean = kl_total[: latents // 128].reshape(latents) / (32 * cells)
     divergence = divergence_weight * jnp.mean(jnp.maximum(kl_mean, free_floor))
-    binding = (kl_mean > free_floor).astype(F32)
-    grad_source = decoded_grad[0]
-
-    latent_turned = latent_low.reshape(cells, 4, 2, latents // 8).transpose(0, 2, 1, 3).reshape(cells, latents)
-    whole_fwd = gather_slide(
-        jnp.concatenate([express, normed_one, attended, normed_two, base_low, latent_turned], axis=1)
-    )
-    act_parts = act_low.reshape(cells, 8, 4, inner // 32)
-
-    def pick_fwd(which):
-        act = lax.dynamic_index_in_dim(act_parts, which, 2, keepdims=False).reshape(cells, inner // 4)
-        return jnp.concatenate([act, columns(grad_source, which * (genes // 4), genes // 4)], axis=1)
-
-    quarter_fwd = swap_slide(pick_fwd, slide)
-
-    grad_latent = matmul(grad_source, decoder_weight.T)
-    grad_kl = jnp.broadcast_to(divergence_weight * binding, kl_cell.shape)
-    grad_mean, grad_logvar, centres_grad = pull_latent((grad_latent, grad_kl))
-    grad_mean_low = grad_mean.astype(BF16)
-    grad_logvar_low = grad_logvar.astype(BF16)
-    grad_final = matmul(grad_mean_low, mean_weight.T) + matmul(grad_logvar_low, logvar_weight.T)
-    grad_branch = grad_final.astype(BF16)
-    down_bias_grad = jnp.sum(grad_branch.astype(F32), axis=0)
-    grad_act = matmul(grad_branch, down_weight.T)
-    gelu_pull = jax.vjp(gelu_tanh, inner_sum)[1]
-    grad_inner = gelu_pull(grad_act)[0].astype(BF16)
-    hidden_bias_grad = jnp.sum(grad_inner.astype(F32), axis=0)
-    norm_two_pull = jax.vjp(layer_norm, hidden_middle, second_gain, second_shift)[1]
-    grad_norm_two, second_gain_grad, second_shift_grad = norm_two_pull(matmul(grad_inner, hidden_weight.T))
-    grad_middle = grad_final + grad_norm_two
-    grad_out = grad_middle.astype(BF16)
-
-    small = jnp.concatenate(
-        [jnp.zeros((8, 2, 128), F32)]
-        + [
-            item.reshape(8, -1, 128)
-            for item in (
-                second_gain_grad,
-                second_shift_grad,
-                hidden_bias_grad,
-                down_bias_grad,
-                centres_grad.reshape(16, 8, -1).transpose(1, 0, 2),
-            )
-        ],
-        axis=1,
-    )
-    count = small.shape[1]
-    small = jnp.pad(small, ((0, 0), (0, -count % 8), (0, 0)))
     (
         panel_sum, query_grad, key_grad, value_grad, output_grad, hidden_grad, down_grad, mean_grad, logvar_grad,
         decoder_grad, small,
     ) = backward(
         (
-            query, key, value, row_labels, col_labels, grad_branch, grad_mean_low, grad_logvar_low, grad_inner, grad_out,
-            grad_middle, hidden_start, first_gain[None], small,
+            land, hidden_start, hidden_middle, inner_sum, mean_lat, log_var, grad_latent, base, latent, kl_total,
+            latent_noise[0], component_means, divergence_weight[None], free_floor[None], first_gain[None],
+            second_gain[None],
         ),
-        tuple(whole_fwd) + tuple(quarter_fwd),
-        (query_weight, key_weight, value_weight, output_weight),
-        cells, width, inner, latents, small.shape[1],
+        (
+            whole, quarters, query_weight, key_weight, value_weight, output_weight, hidden_weight, down_weight,
+            mean_weight, logvar_weight,
+        ),
+        cells, width, inner, latents,
     )
     table_grad = table_rows_grad(first_row, gene_ids, panel_sum, table_rows)
     bias_rows = inner // 8 // 128
     small_hidden = small[4 : 4 + bias_rows].reshape(-1)
-    small_down = small[4 + bias_rows]
-    small_centres = small[5 + bias_rows : count].reshape(16, -1)
+    small_down = small[8]
+    small_centres = small[16 : 16 + component_means.shape[0], : latents // 8]
     return (
         decoded[None],
         divergence,

time: 357 us -> 301 us (0.84); the launches traced: 351 us -> 300 us
  Pallas kernels: 216 us -> 276 us
  matrix products: 38.4 us -> 4.31 us
  blocking collectives: 24.5 us -> 0 us
  local copies, waits for them, and re-layouts: 25.3 us -> 7.01 us
  waiting for transfers between devices: 11.9 us -> 0 us
  starting transfers between devices: 11.6 us -> 0 us
  other arithmetic: 18.4 us -> 9.83 us
    pallas_call x3 -> x1, Pallas kernels: 52.5 us -> 98 us  [forward(): pl.pallas_call(forward_kernel, out_shape=outs, in_specs=[vmem] * len(inpu...]
    dot_general x16 -> x1, matrix products: 34.7 us -> 4.31 us  [matmul(): return jnp.dot(left, right, preferred_element_type=jnp.float32)]
    all_to_all x1 -> x0, blocking collectives: 24.5 us -> none  [on_device_fast(): qkv = lax.all_to_all(qkv, 'blk', 0, 0)]
    pallas_call x1, Pallas kernels: 156 us -> 171 us  [backward(): pl.pallas_call(backward_kernel, out_shape=outs, in_specs=[vmem] * len(inp...]
    ppermute x6 -> x0, starting transfers between devices: 7.8 us -> none  [over_slide(): lax.ppermute(array, 'slide', [(place, place ^ mask) for place in range(4)])]
    dynamic_slice x2 -> x0, local copies, waits for them, and re-layouts: 6.98 us -> none  [the longest x1 6.29 us: pick_fwd(): lax.dynamic_index_in_dim(act_parts, which, 2, keepdims=False)]
    ppermute x6 -> x0, waiting for transfers between devices: 6.26 us -> none  [over_slide(): lax.ppermute(array, 'slide', [(place, place ^ mask) for place in range(4)])]
    all_to_all x1 -> x0, waiting for transfers between devices: 5.62 us -> none  [on_device_fast(): lax.all_to_all(attended.reshape(8, cells, per), 'blk', 0, 0)]
  transfers between devices with their start and end apart: 7 -> 0, of which waited for: 3 -> 0; matrix products, arithmetic and copies ran while one was open for 9% -> 0% of each run, Pallas kernels for 0% -> 0%
where the time goes in v3:
time: 301 us; the launch traced here: 300 us
  Pallas kernels  276 us (92%)
  other arithmetic  9.83 us (3%)
  local copies, waits for them, and re-layouts  7.01 us (2%)
  matrix products  4.31 us (1%)
  between operations  3.22 us (1%)
    pallas_call x1, Pallas kernels, backward(): pl.pallas_call(backward_kernel, out_shape=outs, in_specs=[vmem] * len(inp...  171 us
    pallas_call x1, Pallas kernels, forward(): pl.pallas_call(forward_kernel, out_shape=outs, in_specs=[vmem] * len(inpu...  98 us
    pallas_call x1, Pallas kernels, table_rows_grad(): pl.pallas_call(table_kernel, grid=(table_rows // rows,), out_shape=jax.Sh...  7.44 us

profile of v3, /device:TPU:1, one launch (start us, length us, event | category | flops | bytes accessed | tf_op | source)
XLA Modules:
  0.0 300.4 jit_solution(9995371742737629954)
XLA Ops:
  0.7 0.8 dynamic_slice.3
  1.4 4.3 %fusion.2 = bf16[256,1024]{1,0:T(8,128)(2,1)} fusion(bf16[2048,1024]{1,0:T(8,128)(2,1)} %param.33, s32[2048]{0:T(1024)S(1)} %iota_add_fusion, s32[256]{0:T(256)S(1)} %dynamic_slice.3), kind=kOutput, calls=%fused_computation.2 | convolution fusion | flops 1074528256 | bytes 4727808 | tf_op jit(solution)/shard_map/dot_general | solution.py:74
  5.8 0.7 copy.45
  6.5 0.7 copy.46.library_ref
  7.2 0.6 broadcast_in_dim.41.labels_ref
  7.8 0.6 multiply_exponential_fusion.freqs_ref
  8.4 98.0 %forward.1 = (bf16[8,400,128]{2,1,0:T(8,128)(2,1)}, f32[128,1024]{1,0:T(8,128)}, f32[128,1024]{1,0:T(8,128)}, f32[128,4096]{1,0:T(8,128)}, f32[128,512]{1,0:T(8,...) custom-call(bf16[8,32,1024]{2,1,0:T(8,128)(2,1)} %bitcast.44, ...), custom_call_target="tpu_custom_call" | custom-call | tf_op jit(solution)/shard_map/forward/pallas_call | solution.py:778
  107.1 170.6 %backward.1 = (bf16[1024,1024]{1,0:T(8,128)(2,1)}, bf16[128,1024]{1,0:T(8,128)(2,1)}, bf16[128,1024]{1,0:T(8,128)(2,1)}, bf16[128,1024]{1,0:T(8,128)(2,1)}, bf16...) custom-call(bf16[8,400,128]{2,1,0:T(8,128)(2,1)} %get-tuple-element., ...), custom_call_target="tpu_custom_call" | custom-call | tf_op jit(solution)/shard_map/backward/pallas_call | solution.py:1249
  277.7 1.6 copy-done
  279.3 7.4 %table_rows_grad.1 = f32[2048,1024]{1,0:T(8,128)} custom-call(s32[1]{0:T(128)} %bitcast.17.first_ref, s32[1,1024]{1,0:T(1,128)S(1)} %bitcast.40, bf16[1024,1024]{1,0:T(8,128)(2,1)S(1)} %copy-done), custom_call_target="tpu_custom_call" | custom-call | tf_op jit(solution)/shard_map/table_rows_grad/pallas_call | solution.py:1278
  286.8 1.5 convert_element_type.41
  288.3 1.6 convert_element_type.42
  289.9 0.8 convert_element_type.37
  290.8 0.8 convert_element_type.38
  291.6 0.8 convert_element_type.39
  292.5 0.8 convert_element_type.40
  293.3 0.7 convert_element_type.43
  294.1 0.7 convert_element_type.44
  294.8 0.7 convert_element_type.45
  295.5 0.6 slice.31
  296.1 0.5 slice_bitcast_fusion.1
  296.6 0.6 slice_bitcast_fusion
  297.2 0.6 fusion.7
  298.5 0.8 copy.49
  (37 shorter events, 0.1 us)
Async XLA Ops:
  1.4 4.3 %copy-start.15 = (s32[1,2,128]{2,1,0:T(2,128)S(1)}, s32[1,2,128]{2,1,0:T(2,128)}, u32[]{:S(2)}) copy-start(s32[1,2,128]{2,1,0:T(2,128)} %param.29) | copy-start | bytes 3076
  1.4 5.1 %copy-start.16 = (s32[1,128]{1,0:T(1,128)S(1)}, s32[1,128]{1,0:T(1,128)}, u32[]{:S(2)}) copy-start(s32[1,128]{1,0:T(1,128)} %param.27) | copy-start | bytes 1540
  1.4 5.8 %copy-start.17 = (s32[1,128]{1,0:T(1,128)S(1)}, s32[1,128]{1,0:T(1,128)}, u32[]{:S(2)}) copy-start(s32[1,128]{1,0:T(1,128)} %param.30) | copy-start | bytes 1540
  107.1 170.7 %copy-start.1 = (s32[1024]{0:T(1024)S(1)}, s32[1024]{0:T(1024)}, u32[]{:S(2)}) copy-start(s32[1024]{0:T(1024)} %param.28) | copy-start | bytes 12292
  277.7 1.6 copy-start
  279.3 7.4 %copy-start.3 = (bf16[128,4096]{1,0:T(8,128)(2,1)S(1)}, bf16[128,4096]{1,0:T(8,128)(2,1)}, u32[]{:S(2)}) copy-start(bf16[128,4096]{1,0:T(8,128)(2,1)} %get-tuple-element.62) | copy-start | bytes 3145732
  286.8 1.5 copy-start.2
  288.3 1.6 copy-start.8
  288.3 2.5 copy-start.7
  288.3 3.3 %copy-start.6 = (bf16[128,1024]{1,0:T(8,128)(2,1)S(1)}, bf16[128,1024]{1,0:T(8,128)(2,1)}, u32[]{:S(2)}) copy-start(bf16[128,1024]{1,0:T(8,128)(2,1)} %get-tuple-element.60) | copy-start | bytes 786436
  288.3 4.2 %copy-start.5 = (bf16[128,1024]{1,0:T(8,128)(2,1)S(1)}, bf16[128,1024]{1,0:T(8,128)(2,1)}, u32[]{:S(2)}) copy-start(bf16[128,1024]{1,0:T(8,128)(2,1)} %get-tuple-element.61) | copy-start | bytes 786436
  289.9 3.4 %copy-start.11 = (bf16[128,512]{1,0:T(8,128)(2,1)S(1)}, bf16[128,512]{1,0:T(8,128)(2,1)}, u32[]{:S(2)}) copy-start(bf16[128,512]{1,0:T(8,128)(2,1)} %get-tuple-element.64) | copy-start | bytes 393220
  289.9 4.2 %copy-start.10 = (bf16[128,512]{1,0:T(8,128)(2,1)S(1)}, bf16[128,512]{1,0:T(8,128)(2,1)}, u32[]{:S(2)}) copy-start(bf16[128,512]{1,0:T(8,128)(2,1)} %get-tuple-element.65) | copy-start | bytes 393220
  289.9 4.9 %copy-start.9 = (bf16[64,1024]{1,0:T(8,128)(2,1)S(1)}, bf16[64,1024]{1,0:T(8,128)(2,1)}, u32[]{:S(2)}) copy-start(bf16[64,1024]{1,0:T(8,128)(2,1)} %get-tuple-element.66) | copy-start | bytes 393220
  289.9 5.6 %copy-start.12 = (f32[32,128]{1,0:T(8,128)S(1)}, f32[32,128]{1,0:T(8,128)}, u32[]{:S(2)}) copy-start(f32[32,128]{1,0:T(8,128)} %get-tuple-element.57) | copy-start | bytes 49156
  289.9 7.3 %copy-start.13 = (f32[8,128]{1,0:T(8,128)S(1)}, f32[8,128]{1,0:T(8,128)}, u32[]{:S(2)}) copy-start(f32[8,128]{1,0:T(8,128)} %get-tuple-element.44.kl_ref) | copy-start | bytes 12292
  289.9 7.3 %copy-start.14 = (f32[512]{0:T(512)S(1)}, f32[512]{0:T(512)}, u32[]{:S(2)}) copy-start(f32[512]{0:T(512)} %param.51) | copy-start | bytes 6148
  289.9 8.6 %copy-start.4 = (f32[128,1024]{1,0:T(8,128)S(1)}, f32[128,1024]{1,0:T(8,128)}, u32[]{:S(2)}) copy-start(f32[128,1024]{1,0:T(8,128)} %get-tuple-element.43) | copy-start | bytes 1572868
